TPU v7x, 32 devices: a whole 2x2x4 slice. The times are simulated.
32 devices in a mesh: dp: 4 (over y, x), ctx: 8 (over z, core).
Axes of the slice: x: 2, y: 2, z: 4, core: 2. Of those that a mesh axis runs over, the one named last changes fastest.
Arguments:
- tokens: bfloat16 [4, 1024, 2048], P('dp', 'ctx'), may hold values from -6 to 6
- cotangent: bfloat16 [4, 1024, 2048], P('dp', 'ctx'), may hold values from -6 to 6
- group_ids: int32 [4], P('dp'), may hold values from 0 to 3, as said below
- group_scale: float32 [4], replicated, may hold values from 0.5 to 2
- attn_gain: bfloat16 [2048], P(('dp', 'ctx')), may hold values from 0.099609375 to 1.8984375
- w_qkv: bfloat16 [2048, 6144], P(('dp', 'ctx')), may hold values from -0.125 to 0.125
- conv_weight: bfloat16 [4, 6144], P(None, ('dp', 'ctx')), may hold values from -3 to 3
- w_beta: bfloat16 [2048, 16], P(('dp', 'ctx')), may hold values from -0.25 to 0.25
- w_gate_o: bfloat16 [2048, 2048], P(('dp', 'ctx')), may hold values from -0.125 to 0.125
- norm_gain_o: bfloat16 [128], P(('dp', 'ctx')), may hold values from 0.099609375 to 1.8984375
- w_out: bfloat16 [2048, 2048], P(('dp', 'ctx')), may hold values from -0.125 to 0.125
- ffn_gain: bfloat16 [2048], P(('dp', 'ctx')), may hold values from 0.099609375 to 1.8984375
- w_gate_up: bfloat16 [2048, 11264], P(('dp', 'ctx')), may hold values from -0.125 to 0.125
- w_down: bfloat16 [5632, 2048], P(('dp', 'ctx')), may hold values from -0.078125 to 0.078125
Outputs:
- block_out: bfloat16 [4, 1024, 2048], P('dp', 'ctx')
- d_tokens: float32 [4, 1024, 2048], P('dp', 'ctx')
- g_attn_gain: float32 [2048], P(('dp', 'ctx'))
- g_w_qkv: float32 [2048, 6144], P(('dp', 'ctx'))
- g_conv_weight: float32 [4, 6144], P(None, ('dp', 'ctx'))
- g_w_beta: float32 [2048, 16], P(('dp', 'ctx'))
- g_w_gate_o: float32 [2048, 2048], P(('dp', 'ctx'))
- g_norm_gain_o: float32 [128], P(('dp', 'ctx'))
- g_w_out: float32 [2048, 2048], P(('dp', 'ctx'))
- g_ffn_gain: float32 [2048], P(('dp', 'ctx'))
- g_w_gate_up: float32 [2048, 11264], P(('dp', 'ctx'))
- g_w_down: float32 [5632, 2048], P(('dp', 'ctx'))
Inputs may be any that keep to these rules, and one draw needn't show every extreme that they name: `group_ids`: every group is named by exactly 1 sequence.
All inputs are finite; a program needn't handle non-finite values.
Results may differ from a plain program's by a relative error of at most 0.019.
The roundings to bfloat16 on the way count: a program that leaves them out, or rounds other values in their place, can miss the bound.
Values may be sent and summed in bfloat16 or wider, within the bound.
No kernel may reach another device: no remote copies, remote signals or barrier semaphores. Data moves between devices by JAX's collectives and lax.ppermute only.
A program may use at most 576 MiB of HBM per device.

v0:
```python
import functools

import jax
import jax.numpy as jnp
from jax import lax
from jax.experimental import pallas as pl
from jax.experimental.layout import Layout, with_layout_constraint
from jax.experimental.pallas import tpu as pltpu
from jax.sharding import PartitionSpec as P

CONV = 4
HD = 128
CHUNK = 128
STEP = 256
EPS = 1e-05
KEY_EPS = 1e-06
BF = jnp.bfloat16
F32 = jnp.float32
NN = ((1,), (0,))
NT = ((1,), (1,))
TN = ((0,), (0,))


def mm(left, right, dims):
    return lax.dot_general(
        left.astype(BF), right.astype(BF), (dims, ((), ())), preferred_element_type=F32
    )


def halves(values):
    high = values.astype(BF)
    return high, (values - high.astype(F32)).astype(BF)


def mm_fine(left, right, dims):
    left_hi, left_lo = halves(left)
    right_hi, right_lo = halves(right)

    def product(a, b):
        return lax.dot_general(a, b, (dims, ((), ())), preferred_element_type=F32)

    return product(left_hi, right_hi) + (product(left_hi, right_lo) + product(left_lo, right_hi))


def sigmoid(values):
    return 1.0 / (1.0 + jnp.exp(-values))


def chunk_ids():
    row_ids = lax.broadcasted_iota(jnp.int32, (CHUNK, CHUNK), 0)
    col_ids = lax.broadcasted_iota(jnp.int32, (CHUNK, CHUNK), 1)
    return row_ids, col_ids


def lower_inverses(strict_parts):
    row_ids, col_ids = chunk_ids()
    results = None
    size = 1
    while size < CHUNK:
        pair_mask = (row_ids // (2 * size) == col_ids // (2 * size)) & (
            (row_ids // size) != (col_ids // size)
        )
        corners = [jnp.where(pair_mask, part, 0.0) for part in strict_parts]
        if results is None:
            ident = jnp.where(row_ids == col_ids, 1.0, 0.0)
            results = [ident - corner for corner in corners]
        else:
            moved = [mm_fine(corner, result, NN) for corner, result in zip(corners, results)]
            results = [result - mm_fine(result, part, NN) for result, part in zip(results, moved)]
        size *= 2
    return results


def conv_taps(extended, taps, extent):
    total = taps[0:1] * extended[5 : 5 + extent]
    for offset in range(1, CONV):
        total = total + taps[offset : offset + 1] * extended[5 + offset : 5 + offset + extent]
    return total


def unit_keys(raw):
    scale = lax.rsqrt(jnp.sum(raw * raw, axis=-1, keepdims=True) + KEY_EPS)
    return raw * scale, scale


def mix_forward_kernel(
    pre_ref, gate_ref, beta_ref, taps_ref, gain_ref, y_ref, core_ref, state_ref, inverse_ref,
    state_now, rim, *, heads
):
    width = heads * HD
    step = pre_ref.shape[0]
    chunks = step // CHUNK

    @pl.when(pl.program_id(0) == 0)
    def _():
        state_now[...] = jnp.zeros_like(state_now)
        rim[...] = jnp.zeros_like(rim)

    pre = pre_ref[...].astype(F32)
    extended = jnp.concatenate([rim[...], pre], axis=0)
    rim[...] = pre[step - 8 :]
    conv = conv_taps(extended, taps_ref[...], step)
    mixture = conv * sigmoid(conv)
    beta = sigmoid(beta_ref[...])
    row_ids, col_ids = chunk_ids()
    tiles = [(chunk, head) for chunk in range(chunks) for head in range(heads)]
    q_t, k_t, v_t, b_t, score_t, strict_t = [], [], [], [], [], []
    for chunk, head in tiles:
        rows = slice(chunk * CHUNK, (chunk + 1) * CHUNK)
        q_rows = mixture[rows, head * HD : (head + 1) * HD]
        k_rows, _ = unit_keys(mixture[rows, width + head * HD : width + (head + 1) * HD])
        v_rows = mixture[rows, 2 * width + head * HD : 2 * width + (head + 1) * HD]
        b_rows = beta[rows, head : head + 1]
        q_t.append(q_rows)
        k_t.append(k_rows)
        v_t.append(v_rows)
        b_t.append(b_rows)
        score_t.append(jnp.where(row_ids >= col_ids, mm(q_rows, k_rows, NT), 0.0))
        strict_t.append(jnp.where(row_ids > col_ids, b_rows * mm_fine(k_rows, k_rows, NT), 0.0))
    inverse_t = lower_inverses(strict_t)
    w_t = [mm(t, b * k, NN) for t, b, k in zip(inverse_t, b_t, k_t)]
    u_t = [mm(t, b * v, NN) for t, b, v in zip(inverse_t, b_t, v_t)]
    for index, (chunk, head) in enumerate(tiles):
        rows = slice(chunk * CHUNK, (chunk + 1) * CHUNK)
        cols = slice(head * HD, (head + 1) * HD)
        state = state_now[head]
        state_ref[chunk, head] = state
        inverse_ref[chunk, head] = inverse_t[index]
        update = u_t[index] - mm(w_t[index], state, NN)
        core = mm(q_t[index], state, NN) + mm(score_t[index], update, NN)
        state_now[head] = state + mm(k_t[index], update, TN)
        core_ref[rows, cols] = core
        scale = lax.rsqrt(jnp.mean(core * core, axis=-1, keepdims=True) + EPS)
        gate = gate_ref[rows, cols]
        y_ref[rows, cols] = (
            core * scale * gain_ref[...] * (gate * sigmoid(gate))
        ).astype(y_ref.dtype)


def mix_backward_kernel(
    pre_ref, before_ref, gate_ref, beta_ref, dy_ref, core_ref, state_ref, inverse_ref, taps_ref,
    gain_ref, dproj_ref, dbeta_ref, gtaps_ref, ggain_ref, adjoint, rim, *, heads, blocks
):
    width = heads * HD
    step = pre_ref.shape[0]
    chunks = step // CHUNK
    block = blocks - 1 - pl.program_id(0)

    @pl.when(pl.program_id(0) == 0)
    def _():
        adjoint[...] = jnp.zeros_like(adjoint)
        rim[...] = jnp.zeros_like(rim)
        gtaps_ref[...] = jnp.zeros_like(gtaps_ref)
        ggain_ref[...] = jnp.zeros_like(ggain_ref)

    before = before_ref[...].astype(F32)
    before = jnp.where(block > 0, before[before.shape[0] - 8 :], 0.0)
    extended = jnp.concatenate([before, pre_ref[...].astype(F32)], axis=0)
    taps = taps_ref[...]
    conv = conv_taps(extended, taps, step)
    conv_sig = sigmoid(conv)
    mixture = conv * conv_sig
    beta = sigmoid(beta_ref[...])
    gain = gain_ref[...]
    row_ids, col_ids = chunk_ids()
    causal, strict = row_ids >= col_ids, row_ids > col_ids
    tiles = [(chunk, head) for chunk in range(chunks) for head in range(heads)]
    held = {}
    ggain = jnp.zeros((1, HD), F32)
    for chunk, head in tiles:
        rows = slice(chunk * CHUNK, (chunk + 1) * CHUNK)
        cols = slice(head * HD, (head + 1) * HD)
        q_rows = mixture[rows, head * HD : (head + 1) * HD]
        k_rows, k_scale = unit_keys(mixture[rows, width + head * HD : width + (head + 1) * HD])
        v_rows = mixture[rows, 2 * width + head * HD : 2 * width + (head + 1) * HD]
        b_rows = beta[rows, head : head + 1]
        core = core_ref[rows, cols]
        scale = lax.rsqrt(jnp.mean(core * core, axis=-1, keepdims=True) + EPS)
        gate = gate_ref[rows, cols]
        gate_sig = sigmoid(gate)
        dy = dy_ref[rows, cols].astype(F32)
        normed = core * scale
        ggain += jnp.sum(dy * (gate * gate_sig) * normed, axis=0, keepdims=True)
        dproj_ref[rows, 3 * width + head * HD : 3 * width + (head + 1) * HD] = (
            dy * normed * gain * (gate_sig * (1.0 + gate * (1.0 - gate_sig)))
        ).astype(dproj_ref.dtype)
        dnorm = dy * (gate * gate_sig) * gain
        dcore = scale * (dnorm - normed * jnp.mean(dnorm * normed, axis=-1, keepdims=True))
        state = state_ref[chunk, head]
        inverse = inverse_ref[chunk, head]
        scores = jnp.where(causal, mm(q_rows, k_rows, NT), 0.0)
        weighted = mm(inverse, b_rows * k_rows, NN)
        resid = v_rows - mm(k_rows, state, NN)
        update = mm(inverse, b_rows * resid, NN)
        dupdate = mm(scores, dcore, TN)
        dstate = mm(q_rows, dcore, TN)
        held[chunk, head] = [
            q_rows, k_rows, k_scale, b_rows, dcore, state, inverse, weighted, resid, update, dupdate,
            dstate
        ]
    later = {}
    for chunk in reversed(range(chunks)):
        for head in range(heads):
            entry = held[chunk, head]
            after = adjoint[head]
            later[chunk, head] = after
            entry[10] = entry[10] + mm(entry[1], after, NN)
            adjoint[head] = after + entry[11] - mm(entry[7], entry[10], TN)
    pieces = {}
    for chunk, head in tiles:
        (
            q_rows, k_rows, k_scale, b_rows, dcore, state, inverse, _, resid, update, dupdate, _
        ) = held[chunk, head]
        after = later[chunk, head]
        rows = slice(chunk * CHUNK, (chunk + 1) * CHUNK)
        dr = mm(inverse, dupdate, TN)
        dv = b_rows * dr
        dstrict = jnp.where(strict, -mm(dr, update, NT), 0.0)
        gram = mm(k_rows, k_rows, NT)
        dbeta = jnp.sum(dr * resid, axis=-1, keepdims=True) + jnp.sum(
            dstrict * gram, axis=-1, keepdims=True
        )
        dgram = b_rows * dstrict
        dscores = jnp.where(causal, mm(dcore, update, NT), 0.0)
        dq = mm(dcore, state, NT) + mm(dscores, k_rows, NN)
        dk = (
            mm(dscores, q_rows, TN)
            + mm(update, after, NT)
            - mm(dv, state, NT)
            + mm(dgram, k_rows, NN)
            + mm(dgram, k_rows, TN)
        )
        dkraw = k_scale * (dk - k_rows * jnp.sum(dk * k_rows, axis=-1, keepdims=True))
        pieces[0, head, chunk] = dq
        pieces[1, head, chunk] = dkraw
        pieces[2, head, chunk] = dv
        dbeta_ref[rows, head : head + 1] = dbeta * b_rows * (1.0 - b_rows)
    dmixture = jnp.concatenate(
        [
            jnp.concatenate([pieces[part, head, chunk] for chunk in range(chunks)], axis=0)
            for part in range(3)
            for head in range(heads)
        ],
        axis=1,
    )
    dconv = dmixture * (conv_sig * (1.0 + conv * (1.0 - conv_sig)))
    followed = jnp.concatenate([dconv, rim[...]], axis=0)
    rim[...] = dconv[:8]
    dpre = taps[CONV - 1 : CONV] * followed[0:step]
    for offset in range(CONV - 1):
        shift = CONV - 1 - offset
        dpre = dpre + taps[offset : offset + 1] * followed[shift : shift + step]
    dproj_ref[:, : 3 * width] = dpre.astype(dproj_ref.dtype)
    for offset in range(CONV):
        gtaps_ref[offset : offset + 1] += jnp.sum(
            dconv * extended[5 + offset : 5 + offset + step], axis=0, keepdims=True
        )
    ggain_ref[0:1] += ggain


def mix_forward(pre, gate, beta, taps, gain):
    extent, width3 = pre.shape
    width = width3 // 3
    heads = width // HD
    step = min(STEP, extent)
    blocks, chunks = extent // step, step // CHUNK
    return pl.pallas_call(
        functools.partial(mix_forward_kernel, heads=heads),
        grid=(blocks,),
        in_specs=[
            pl.BlockSpec((step, width3), lambda i: (i, 0)),
            pl.BlockSpec((step, width), lambda i: (i, 0)),
            pl.BlockSpec((step, heads), lambda i: (i, 0)),
            pl.BlockSpec((8, width3), lambda i: (0, 0)),
            pl.BlockSpec((1, HD), lambda i: (0, 0)),
        ],
        out_specs=[
            pl.BlockSpec((step, width), lambda i: (i, 0)),
            pl.BlockSpec((step, width), lambda i: (i, 0)),
            pl.BlockSpec((chunks, heads, HD, HD), lambda i: (i, 0, 0, 0)),
            pl.BlockSpec((chunks, heads, CHUNK, CHUNK), lambda i: (i, 0, 0, 0)),
        ],
        out_shape=[
            jax.ShapeDtypeStruct((extent, width), BF),
            jax.ShapeDtypeStruct((extent, width), F32),
            jax.ShapeDtypeStruct((extent // CHUNK, heads, HD, HD), F32),
            jax.ShapeDtypeStruct((extent // CHUNK, heads, CHUNK, CHUNK), F32),
        ],
        scratch_shapes=[pltpu.VMEM((heads, HD, HD), F32), pltpu.VMEM((8, width3), F32)],
        compiler_params=pltpu.CompilerParams(
            dimension_semantics=("arbitrary",), vmem_limit_bytes=48 * 1024 * 1024
        ),
        cost_estimate=pl.CostEstimate(
            flops=90 * extent * width * CHUNK, bytes_accessed=40 * extent * width, transcendentals=0
        ),
        name="mix_forward",
    )(pre, gate, beta, taps, gain)


def mix_backward(pre, gate, beta, dy, core, states, inverses, taps, gain):
    extent, width3 = pre.shape
    width = width3 // 3
    heads = width // HD
    step = min(STEP, extent)
    blocks, chunks = extent // step, step // CHUNK
    rows_before = 16

    def at(i):
        return (blocks - 1 - i, 0)

    def at_tiles(i):
        return (blocks - 1 - i, 0, 0, 0)

    def just_before(i):
        return (jnp.maximum((blocks - 1 - i) * (step // rows_before) - 1, 0), 0)

    return pl.pallas_call(
        functools.partial(mix_backward_kernel, heads=heads, blocks=blocks),
        grid=(blocks,),
        in_specs=[
            pl.BlockSpec((step, width3), at),
            pl.BlockSpec((rows_before, width3), just_before),
            pl.BlockSpec((step, width), at),
            pl.BlockSpec((step, heads), at),
            pl.BlockSpec((step, width), at),
            pl.BlockSpec((step, width), at),
            pl.BlockSpec((chunks, heads, HD, HD), at_tiles),
            pl.BlockSpec((chunks, heads, CHUNK, CHUNK), at_tiles),
            pl.BlockSpec((8, width3), lambda i: (0, 0)),
            pl.BlockSpec((1, HD), lambda i: (0, 0)),
        ],
        out_specs=[
            pl.BlockSpec((step, width3 + width), at),
            pl.BlockSpec((step, heads), at),
            pl.BlockSpec((8, width3), lambda i: (0, 0)),
            pl.BlockSpec((8, HD), lambda i: (0, 0)),
        ],
        out_shape=[
            jax.ShapeDtypeStruct((extent, width3 + width), BF),
            jax.ShapeDtypeStruct((extent, heads), F32),
            jax.ShapeDtypeStruct((8, width3), F32),
            jax.ShapeDtypeStruct((8, HD), F32),
        ],
        scratch_shapes=[pltpu.VMEM((heads, HD, HD), F32), pltpu.VMEM((8, width3), F32)],
        compiler_params=pltpu.CompilerParams(
            dimension_semantics=("arbitrary",), vmem_limit_bytes=48 * 1024 * 1024
        ),
        cost_estimate=pl.CostEstimate(
            flops=90 * extent * width * CHUNK, bytes_accessed=40 * extent * width, transcendentals=0
        ),
        name="mix_backward",
    )(pre, pre, gate, beta, dy, core, states, inverses, taps, gain)


def heads_of(ctx, ctxs, heads, row_part):
    blocks = HD // row_part
    groups = ctxs // blocks
    return [((ctx % blocks) * heads + slot) * groups + ctx // blocks for slot in range(heads)]


def pack_mix_kernel(qkv_ref, gate_ref, beta_ref, small_ref, out_ref):
    ctxs = out_ref.shape[0]
    rows, total = gate_ref.shape
    width = total // ctxs
    heads = beta_ref.shape[1] // ctxs
    small = small_ref[...]
    for ctx in range(ctxs):
        betas = []
        for slot, head in enumerate(heads_of(ctx, ctxs, heads, rows)):
            to, cols = slot * HD, slice(head * HD, (head + 1) * HD)
            for part in range(3):
                out_ref[ctx, :, part * width + to : part * width + to + HD] = qkv_ref[
                    :, part * total + head * HD : part * total + (head + 1) * HD
                ]
            out_ref[ctx, :, 3 * width + to : 3 * width + to + HD] = gate_ref[:, cols]
            betas.append(beta_ref[:, head : head + 1])
        out_ref[ctx, :, 4 * width :] = jnp.concatenate(betas + [small], axis=1)


def pack_mix(w_qkv, w_gate_o, w_beta, small, ctxs):
    rows, total = w_gate_o.shape
    cols = 4 * (total // ctxs) + 128
    return pl.pallas_call(
        pack_mix_kernel,
        out_shape=jax.ShapeDtypeStruct((ctxs, rows, cols), w_qkv.dtype),
        name="pack_mix",
    )(w_qkv, w_gate_o, w_beta, small)


def unpack_mix_kernel(
    in_ref, small_in_ref, qkv_ref, gate_ref, beta_ref, gqkv_ref, ggate_ref, gbeta_ref, small_ref,
    rows_ref
):
    ctxs = in_ref.shape[0]
    rows, total = gate_ref.shape
    width = total // ctxs
    heads = gbeta_ref.shape[1] // ctxs
    row_sum = jnp.zeros(rows_ref.shape, F32)
    small_sum = jnp.zeros(small_ref.shape, F32)
    betas = [None] * (heads * ctxs)
    for ctx in range(ctxs):
        small = small_in_ref[ctx].astype(F32)
        small_sum += small
        for slot, head in enumerate(heads_of(ctx, ctxs, heads, rows)):
            betas[head] = small[:, slot : slot + 1]
            for part in range(4):
                start = part * width + slot * HD
                grad = in_ref[ctx, :, start : start + HD].astype(F32)
                if part == 3:
                    cols = slice(head * HD, (head + 1) * HD)
                    ggate_ref[:, cols] = grad
                    weight = gate_ref[:, cols].astype(F32)
                else:
                    cols = slice(part * total + head * HD, part * total + (head + 1) * HD)
                    gqkv_ref[:, cols] = grad
                    weight = qkv_ref[:, cols].astype(F32)
                row_sum += jnp.sum(grad * weight, axis=1, keepdims=True)
    grad = jnp.concatenate(betas, axis=1)
    gbeta_ref[...] = grad
    small_ref[...] = small_sum
    rows_ref[...] = row_sum + jnp.sum(grad * beta_ref[...].astype(F32), axis=1, keepdims=True)


def unpack_mix(received, small, w_qkv, w_gate_o, w_beta):
    rows = w_qkv.shape[0]
    return pl.pallas_call(
        unpack_mix_kernel,
        out_shape=[
            jax.ShapeDtypeStruct(w_qkv.shape, F32),
            jax.ShapeDtypeStruct(w_gate_o.shape, F32),
            jax.ShapeDtypeStruct(w_beta.shape, F32),
            jax.ShapeDtypeStruct((rows, 128), F32),
            jax.ShapeDtypeStruct((rows, 1), F32),
        ],
        compiler_params=pltpu.CompilerParams(vmem_limit_bytes=48 * 1024 * 1024),
        name="unpack_mix",
    )(received, small, w_qkv, w_gate_o, w_beta)


def pack_ff_kernel(in_ref, out_ref, *, dps):
    ctxs = out_ref.shape[0]
    part = out_ref.shape[2] // (2 * dps)
    hidden = in_ref.shape[1] // 2
    for ctx in range(ctxs):
        starts = [
            side * hidden + (place * ctxs + ctx) * part for side in range(2) for place in range(dps)
        ]
        out_ref[ctx] = jnp.concatenate([in_ref[:, s : s + part] for s in starts], axis=1)


def pack_ff(w_gate_up, ctxs, dps):
    rows, total = w_gate_up.shape
    return pl.pallas_call(
        functools.partial(pack_ff_kernel, dps=dps),
        out_shape=jax.ShapeDtypeStruct((ctxs, rows, total // ctxs), w_gate_up.dtype),
        compiler_params=pltpu.CompilerParams(vmem_limit_bytes=48 * 1024 * 1024),
        name="pack_ff",
    )(w_gate_up)


def unpack_ff_kernel(in_ref, w_ref, out_ref, rows_ref, *, dps):
    ctxs = in_ref.shape[0]
    part = in_ref.shape[2] // (2 * dps)
    hidden = out_ref.shape[1] // 2
    row_sum = jnp.zeros(rows_ref.shape, F32)
    for side in range(2):
        pieces = []
        for place in range(dps):
            start = (side * dps + place) * part
            pieces.extend(in_ref[ctx, :, start : start + part] for ctx in range(ctxs))
        grad = jnp.concatenate(pieces, axis=1).astype(F32)
        cols = slice(side * hidden, (side + 1) * hidden)
        out_ref[:, cols] = grad
        row_sum += jnp.sum(grad * w_ref[:, cols].astype(F32), axis=1, keepdims=True)
    rows_ref[...] = row_sum


def unpack_ff(received, w_gate_up, dps):
    return pl.pallas_call(
        functools.partial(unpack_ff_kernel, dps=dps),
        out_shape=[
            jax.ShapeDtypeStruct(w_gate_up.shape, F32),
            jax.ShapeDtypeStruct((w_gate_up.shape[0], 1), F32),
        ],
        compiler_params=pltpu.CompilerParams(vmem_limit_bytes=48 * 1024 * 1024),
        name="unpack_ff",
    )(received, w_gate_up)


def dot(left, right, dims=NN):
    return lax.dot_general(left, right, (dims, ((), ())), preferred_element_type=F32)


def after(value, *others):
    return lax.optimization_barrier((value,) + others)[0]


def swapped(value, axis, distance):
    count = lax.axis_size(axis)
    return lax.ppermute(value, axis, [(i, i ^ distance) for i in range(count)])


def row_major(value):
    return with_layout_constraint(value, Layout(major_to_minor=tuple(range(value.ndim))))


def placed(parts, order):
    whole = row_major(jnp.zeros((len(parts),) + parts[0].shape, parts[0].dtype))
    for part, place in zip(parts, order):
        whole = lax.dynamic_update_index_in_dim(whole, part, place, 0)
    return row_major(lax.optimization_barrier(whole))


def shards_of(shard, axis):
    count = lax.axis_size(axis)
    return [shard] + [swapped(shard, axis, distance) for distance in range(1, count)]


def placed_shards(parts, axis):
    place = lax.axis_index(axis)
    return placed(parts, [place ^ distance for distance in range(len(parts))])


def shard_parts(part_of, axis):
    count, place = lax.axis_size(axis), lax.axis_index(axis)
    sent = [part_of(place ^ distance) for distance in range(1, count)]
    return sent + [part_of(place)]


def swapped_parts(parts, axis):
    return [swapped(part, axis, index + 1) for index, part in enumerate(parts[:-1])] + parts[-1:]


def total_of(parts):
    total = parts[-1].astype(F32)
    for part in parts[:-1]:
        total = total + part.astype(F32)
    return total


def head_routes(row_part, turn):
    dps, ctxs = lax.axis_size("dp"), lax.axis_size("ctx")
    blocks = HD // row_part
    heads = dps // blocks
    routes = []
    for dp in range(dps):
        for ctx in range(ctxs):
            place = (dp % heads) * blocks + ctx % blocks
            user = (ctx // blocks) * blocks + dp // heads
            routes.append((dp * ctxs + ctx, (place ^ turn) * ctxs + user))
    return routes


def head_owner_parts(rows):
    turns = range(lax.axis_size("dp"))
    return [lax.ppermute(rows, ("dp", "ctx"), head_routes(rows.shape[0], turn)) for turn in turns]


def row_owner_parts(blocks):
    place = lax.axis_index("dp")
    parts = []
    for turn in range(lax.axis_size("dp")):
        routes = [(user, owner) for owner, user in head_routes(blocks.shape[1], turn)]
        block = lax.dynamic_index_in_dim(blocks, place ^ turn, 0, False)
        parts.append(lax.ppermute(block, ("dp", "ctx"), routes))
    return parts


def spread(value, axis):
    return lax.all_to_all(value, axis, 0, 0, tiled=True)


def rms_scale(values):
    return lax.rsqrt(jnp.mean(values * values, axis=-1, keepdims=True) + EPS)


def norm_pull(values, scale, gain, grad):
    weighted = grad * gain
    return scale * weighted - values * (
        scale * scale * scale * jnp.mean(weighted * values, axis=-1, keepdims=True)
    )


def per_device(
    tokens,
    cotangent,
    group_ids,
    group_scale,
    attn_gain,
    w_qkv,
    conv_weight,
    w_beta,
    w_gate_o,
    norm_gain_o,
    w_out,
    ffn_gain,
    w_gate_up,
    w_down,
):
    seg_len, width = tokens.shape[1:]
    dps, ctxs = lax.axis_size("dp"), lax.axis_size("ctx")
    devices = dps * ctxs
    ctx_place = lax.axis_index("ctx")
    head_count = w_beta.shape[1]
    heads = head_count // ctxs
    mix_width = heads * HD
    row_part = w_qkv.shape[0]
    dp_rows = ctxs * row_part
    ff_part = w_down.shape[0]
    ff_local = dps * ff_part
    taps_part = conv_weight.shape[1]
    taps_cols = CONV * taps_part // row_part
    gain_part = norm_gain_o.shape[0]
    head_dims = (HD // row_part, heads, ctxs * row_part // HD)

    small = jnp.concatenate(
        [
            attn_gain[:, None],
            ffn_gain[:, None],
            jnp.pad(norm_gain_o, (0, row_part - gain_part))[:, None],
            conv_weight.reshape(row_part, taps_cols),
        ],
        axis=1,
    )
    small = jnp.pad(small, ((0, 0), (0, 128 - heads - small.shape[1])))
    mix_rows = pack_mix(w_qkv, w_gate_o, w_beta, small, ctxs)
    mix_half = spread(mix_rows, "ctx").reshape(dp_rows, mix_rows.shape[2])
    down_parts = shards_of(w_down, "dp")
    mix_half, *down_parts = lax.optimization_barrier((mix_half, *down_parts))
    mix_parts = shards_of(mix_half, "dp")
    x_full = lax.all_gather(after(tokens[0], mix_half), "ctx", axis=0, tiled=True)
    gate_up_rows = pack_ff(w_gate_up, ctxs, dps)
    gate_up_half = spread(after(gate_up_rows, mix_half), "ctx").reshape(dp_rows, 2 * ff_local)
    x_full, gate_up_half, *mix_parts[1:3] = lax.optimization_barrier(
        (x_full, gate_up_half, *mix_parts[1:3])
    )
    out_parts = head_owner_parts(after(w_out, mix_half))
    w_mix = placed_shards(mix_parts, "dp").reshape(width, mix_rows.shape[2])

    matches = group_ids[:, None] == lax.broadcasted_iota(
        jnp.int32, (group_ids.shape[0], group_scale.shape[0]), 1
    )
    seq_scale = jnp.sum(jnp.where(matches, group_scale[None, :], 0.0), axis=1)
    d_out = cotangent[0].astype(F32) * seq_scale[0]
    d_out_full = lax.all_gather(after(d_out.astype(BF), x_full), "ctx", axis=0, tiled=True)

    w_small = lax.optimization_barrier(w_mix[:, 4 * mix_width :].T)
    place = heads
    attn_full = w_small[place].astype(F32)
    ffn_full = w_small[place + 1].astype(F32)
    norm_o_full = w_small[place + 2].reshape(devices, row_part)[:, :gain_part]
    norm_o_full = norm_o_full.reshape(1, HD).astype(F32)
    conv_full = (
        w_small[place + 3 : place + 3 + taps_cols]
        .reshape(taps_cols, devices, row_part)
        .transpose(1, 2, 0)
        .reshape(devices, CONV, taps_part)
        .transpose(1, 0, 2)
        .reshape(CONV, 3, *head_dims, HD)
        .transpose(4, 2, 0, 1, 3, 5)
        .reshape(ctxs, CONV, 3 * mix_width)
    )
    taps = lax.dynamic_index_in_dim(conv_full, ctx_place, 0, False)
    taps = jnp.pad(taps.astype(F32), ((0, 8 - CONV), (0, 0)))

    x_rows = x_full.astype(F32)
    h1_low = (x_rows * rms_scale(x_rows) * attn_full).astype(BF)
    proj = dot(h1_low, w_mix)
    pre_low = proj[:, : 3 * mix_width].astype(BF)
    gate_raw = proj[:, 3 * mix_width : 4 * mix_width]
    beta_logit = proj[:, 4 * mix_width : 4 * mix_width + heads]
    pre_low, *out_parts = lax.optimization_barrier((pre_low, *out_parts))
    w_out_own = placed_shards(out_parts, "dp").reshape(mix_width, width)
    y_local, core, states, inverses = mix_forward(pre_low, gate_raw, beta_logit, taps, norm_o_full)
    gate_up_parts = shards_of(gate_up_half, "dp")
    attn_part = dot(y_local, w_out_own).astype(BF)
    attn_part, d_out_full = lax.optimization_barrier((attn_part, d_out_full))
    attn_sum = lax.psum_scatter(attn_part, "ctx", scatter_dimension=0, tiled=True)

    x_own = tokens[0].astype(F32)
    attn_sum, *gate_up_parts[1:3] = lax.optimization_barrier((attn_sum, *gate_up_parts[1:3]))
    resid = x_own + attn_sum.astype(F32)
    resid_scale = rms_scale(resid)
    h2_own = (resid * resid_scale * ffn_full).astype(BF)
    h2_low = lax.all_gather(h2_own, "ctx", axis=0, tiled=True)

    w_dn = placed_shards(down_parts, "dp").reshape(ff_local, width)
    w_gu = placed_shards(gate_up_parts, "dp").reshape(width, 2 * ff_local)
    gate_up = dot(h2_low, w_gu)
    gate, up = gate_up[:, :ff_local], gate_up[:, ff_local:]
    gate_sig = jax.nn.sigmoid(gate)
    hidden_low = (gate * gate_sig * up).astype(BF)
    d_hidden = dot(d_out_full, w_dn, NT).astype(BF).astype(F32)
    d_gate_up = jnp.concatenate(
        [
            (d_hidden * up * (gate_sig * (1.0 + gate * (1.0 - gate_sig)))).astype(BF),
            (d_hidden * (gate * gate_sig)).astype(BF),
        ],
        axis=1,
    )
    d_h2_part = dot(d_gate_up, w_gu, NT).astype(BF)
    d_h2 = lax.psum_scatter(d_h2_part, "ctx", scatter_dimension=0, tiled=True)
    hidden_later, d_gate_up_later = lax.optimization_barrier((hidden_low, d_gate_up, d_h2_part))[:2]
    out_part = dot(hidden_later, w_dn).astype(BF)

    def down_part(place):
        hidden_cols = lax.dynamic_slice_in_dim(hidden_later, place * ff_part, ff_part, 1)
        return dot(hidden_cols, d_out_full, TN).astype(BF)

    def gate_up_part(place):
        h2_cols = lax.dynamic_slice_in_dim(h2_low, place * dp_rows, dp_rows, 1)
        return dot(h2_cols, d_gate_up_later, TN).astype(BF)

    g_gate_up_parts = shard_parts(gate_up_part, "dp")
    g_down_parts = shard_parts(down_part, "dp")
    g_gate_up_parts = swapped_parts(g_gate_up_parts, "dp")
    d_h2, out_part, *parts = lax.optimization_barrier(
        (d_h2, out_part, *g_gate_up_parts[:2], *g_down_parts)
    )
    g_gate_up_parts[:2] = parts[:2]
    g_down_parts = swapped_parts(parts[2:], "dp")

    d_resid = d_out + norm_pull(resid, resid_scale, ffn_full, d_h2.astype(F32))
    d_attn = lax.all_gather(d_resid.astype(BF), "ctx", axis=0, tiled=True)
    d_attn, *g_gate_up_parts = lax.optimization_barrier((d_attn, *g_gate_up_parts))
    out_sum = lax.psum_scatter(after(out_part, d_attn), "ctx", scatter_dimension=0, tiled=True)
    d_y = dot(d_attn, w_out_own, NT).astype(BF)
    g_gate_up = total_of(g_gate_up_parts).astype(BF)
    g_gate_up = spread(g_gate_up.reshape(ctxs, row_part, 2 * ff_local), "ctx")

    d_proj, d_beta, g_taps, g_gain_o = mix_backward(
        pre_low, gate_raw, beta_logit, d_y, core, states, inverses, taps, norm_o_full
    )

    def mix_part(place):
        h1_cols = lax.dynamic_slice_in_dim(h1_low, place * dp_rows, dp_rows, 1)
        return dot(h1_cols, d_proj, TN).astype(BF)

    g_mix_parts = shard_parts(mix_part, "dp")
    d_proj_later, *parts = lax.optimization_barrier(
        (d_proj, *g_mix_parts[:-1], *g_down_parts)
    )
    g_mix_parts = swapped_parts(parts[: dps - 1] + g_mix_parts[-1:], "dp")
    g_down_parts = parts[dps - 1 :]
    d_beta_low = jnp.pad(d_beta.astype(BF), ((0, 0), (0, 128 - heads)))
    d_h1_part = dot(jnp.concatenate([d_proj_later, d_beta_low], axis=1), w_mix, NT).astype(BF)
    d_h1_part, out_sum, g_gate_up, *g_mix_parts[:2] = lax.optimization_barrier(
        (d_h1_part, out_sum, g_gate_up, *g_mix_parts[:2])
    )
    block_out = (resid + out_sum.astype(F32)).astype(BF)[None]
    d_h1 = lax.psum_scatter(d_h1_part, "ctx", scatter_dimension=0, tiled=True).astype(F32)
    d_tokens = (d_resid + norm_pull(x_own, rms_scale(x_own), attn_full, d_h1))[None]

    taps_grad = jnp.zeros((ctxs, CONV, 3 * mix_width), F32)
    taps_grad = lax.dynamic_update_index_in_dim(taps_grad, g_taps[:CONV], ctx_place, 0)
    taps_grad = (
        taps_grad.reshape(head_dims[2], head_dims[0], CONV, 3, heads, HD)
        .transpose(2, 3, 1, 4, 0, 5)
        .reshape(CONV, devices, taps_part)
        .transpose(1, 0, 2)
        .reshape(width, taps_cols)
    )
    gain_grad = jnp.pad(g_gain_o[0].reshape(devices, gain_part), ((0, 0), (0, row_part - gain_part)))
    small_grad = jnp.concatenate(
        [jnp.zeros((width, heads), F32), gain_grad.reshape(width, 1), taps_grad], axis=1
    )
    small_grad = jnp.pad(small_grad, ((0, 0), (0, 128 - small_grad.shape[1])))
    small_grad = (small_grad + dot(h1_low, d_beta_low, TN)).astype(BF)
    small_grad = small_grad.reshape(dps, dp_rows, 128)

    def small_part(place):
        return lax.dynamic_index_in_dim(small_grad, place, 0, False)

    g_small = total_of(swapped_parts(shard_parts(small_part, "dp"), "dp")).astype(BF)
    g_small = spread(g_small.reshape(ctxs, row_part, 128), "ctx")
    g_out = dot(y_local, after(d_attn, *g_mix_parts[:2]), TN).astype(BF)
    g_w_out = total_of(row_owner_parts(g_out.reshape(dps, row_part, width)))
    g_w_down = total_of(g_down_parts)

    g_w_gate_up, ffn_sum = unpack_ff(g_gate_up, w_gate_up, dps)
    g_ffn_gain = ffn_sum[:, 0] / ffn_gain.astype(F32)
    g_mix = total_of(g_mix_parts).astype(BF)
    g_mix = spread(g_mix.reshape(ctxs, row_part, g_mix.shape[1]), "ctx")
    g_w_qkv, g_w_gate_o, g_w_beta, small_sum, attn_row_sum = unpack_mix(
        g_mix, g_small, w_qkv, w_gate_o, w_beta
    )
    g_attn_gain = attn_row_sum[:, 0] / attn_gain.astype(F32)
    g_norm_gain_o = small_sum[:gain_part, heads]
    g_conv = small_sum[:, heads + 1 : heads + 1 + taps_cols].reshape(CONV, taps_part)
    return (
        block_out,
        d_tokens,
        g_attn_gain,
        g_w_qkv,
        g_conv,
        g_w_beta,
        g_w_gate_o,
        g_norm_gain_o,
        g_w_out,
        g_ffn_gain,
        g_w_gate_up,
        g_w_down,
    )


def solution(mesh):
    rows = P(("dp", "ctx"), None)
    flat = P(("dp", "ctx"))
    taps = P(None, ("dp", "ctx"))
    acts = P("dp", "ctx", None)
    return jax.shard_map(
        per_device,
        mesh=mesh,
        in_specs=(
            acts, acts, P("dp"), P(), flat, rows, taps, rows, rows, flat, rows, flat, rows, rows
        ),
        out_specs=(acts, acts, flat, rows, taps, rows, rows, flat, rows, flat, rows, rows),
        check_vma=False,
    )
```

profile of v0, /device:TPU:0, one launch (start us, length us, event | category | flops | bytes accessed | tf_op | source)
XLA Modules:
  0.0 591.6 jit_solution(647619802748524229)
XLA Ops:
  15.0 6.3 %all-to-all-start = ((bf16[8,64,1152]{2,1,0:T(8,128)(2,1)}), bf16[8,64,1152]{2,1,0:T(8,128)(2,1)S(1)}, u32[]{:S(2)}, u32[]{:S(2)}) async-start(bf16[8,64,1152]{2,1,0:T(8,128)(2,1)} %pack_mix.1), calls=%async_computation | async-start | bytes 2359296 | tf_op jit(solution)/shard_map/all_to_all | solution.py:570
  24.9 15.5 %collective-permute-done = bf16[176,2048]{1,0:T(8,128)(2,1)S(1)} collective-permute-done((bf16[176,2048]{1,0:T(8,128)(2,1)S(1)}, bf16[176,2048]{1,0:T(8,128)(2,1)S(1)}, u32[]{:S(2)}, u32[]{:S(2)}) %collective-permute-start) | collective-permute-done | bytes 720928 | tf_op jit(solution)/shard_map/ppermute | solution.py:500
  40.3 16.2 %collective-permute-done.1 = bf16[176,2048]{1,0:T(8,128)(2,1)S(1)} collective-permute-done((bf16[176,2048]{1,0:T(8,128)(2,1)S(1)}, bf16[176,2048]{1,0:T(8,128)(2,1)S(1)}, u32[]{:S(2)}, u32[]{:S(2)}) %collective-permute-start.1) | collective-permute-done | bytes 720928 | tf_op jit(solution)/shard_map/ppermute | solution.py:500
  59.3 4.7 all-to-all-start.1
  70.4 3.6 collective-permute-start.6
  75.4 17.8 %collective-permute-done.3 = bf16[512,1152]{1,0:T(8,128)(2,1)} collective-permute-done((bf16[512,1152]{1,0:T(8,128)(2,1)}, bf16[512,1152]{1,0:T(8,128)(2,1)}, u32[]{:S(2)}, u32[]{:S(2)}) %collective-permute-start.3) | collective-permute-done | bytes 1179680 | tf_op jit(solution)/shard_map/ppermute | solution.py:500
  94.7 28.2 %collective-permute-done.4 = bf16[512,1152]{1,0:T(8,128)(2,1)} collective-permute-done((bf16[512,1152]{1,0:T(8,128)(2,1)}, bf16[512,1152]{1,0:T(8,128)(2,1)}, u32[]{:S(2)}, u32[]{:S(2)}) %collective-permute-start.4) | collective-permute-done | bytes 1179680 | tf_op jit(solution)/shard_map/ppermute | solution.py:500
  124.9 5.9 %all-to-all-done.1 = bf16[8,64,1408]{2,1,0:T(8,128)(2,1)S(1)} async-done(((bf16[8,64,1408]{2,1,0:T(8,128)(2,1)}), bf16[8,64,1408]{2,1,0:T(8,128)(2,1)S(1)}, u32[]{:S(2)}, u32[]{:S(2)}) %all-to-all-start.1) | async-done | bytes 1441824 | tf_op jit(solution)/shard_map/all_to_all | solution.py:570
  130.8 3.5 all-gather.5.cloned.1.call-done
  143.4 3.2 fusion
  150.0 5.6 fusion.58
  164.1 17.3 %mix_forward.1 = (bf16[1024,256]{1,0:T(8,128)(2,1)S(1)}, f32[1024,256]{1,0:T(8,128)S(1)}, f32[8,2,128,128]{3,2,1,0:T(8,128)S(1)}, f32[8,2,128,128]{3,2,1,0:T(8,128)S(1)}) custom-call(bf16[1024,768]{1,0:T(8,128)(2,1)} %slice.88.pre_ref.before_ref, f32[1024,256]{1,0:T(8,128)S(1)} %slice.64.gate_ref, f32[1024,2]{1,0:T(8,128)S(1)} %copy-done.5, ...), custom_call_target="tpu_custom_call" | custom-call | flops 3019898880 | bytes 10485760 | tf_op jit(solution)/shard_map/mix_forward/pallas_call | solution.py:267
  184.3 3.3 convolution_convert_fusion.3
  190.2 31.6 %collective-permute-done.10 = bf16[512,1408]{1,0:T(8,128)(2,1)} collective-permute-done((bf16[512,1408]{1,0:T(8,128)(2,1)}, bf16[512,1408]{1,0:T(8,128)(2,1)}, u32[]{:S(2)}, u32[]{:S(2)}) %collective-permute-start.10) | collective-permute-done | bytes 1441824 | tf_op jit(solution)/shard_map/ppermute | solution.py:500
  222.3 14.0 %reduce-scatter.5.cloned.1.call-done = bf16[128,2048]{1,0:T(8,128)(2,1)} async-done(((bf16[1024,2048]{1,0:T(8,128)(2,1)}), bf16[128,2048]{1,0:T(8,128)(2,1)}) %reduce-scatter.5.cloned.1.call-update) | async-done | bytes 524304 | tf_op jit(solution)/shard_map/reduce_scatter | solution.py:678
  258.7 20.4 %collective-permute-done.12 = bf16[512,1408]{1,0:T(8,128)(2,1)S(1)} collective-permute-done((bf16[512,1408]{1,0:T(8,128)(2,1)S(1)}, bf16[512,1408]{1,0:T(8,128)(2,1)S(1)}, u32[]{:S(2)}, u32[]{:S(2)}) %collective-permute-start.12) | collective-permute-done | bytes 1441824 | tf_op jit(solution)/shard_map/ppermute | solution.py:500
  280.3 5.4 all-gather.9.cloned.1.call-done
  285.6 10.7 %fusion.59 = f32[1024,1408]{0,1:T(8,128)S(1)} fusion(bf16[1024,2048]{1,0:T(8,128)(2,1)} %all-gather.9.cloned.1.call-done, bf16[2048,1408]{1,0:T(8,128)(2,1)} %bitcast.33), kind=kOutput, calls=%fused_computation.149 | convolution fusion | flops 5905580032 | bytes 15728640 | tf_op jit(solution)/shard_map/dot_general | solution.py:491
  296.4 7.1 %fusion.4 = (bf16[1024,704]{0,1:T(8,128)(2,1)S(1)}, bf16[1024,704]{0,1:T(8,128)(2,1)S(1)}, bf16[1024,704]{0,1:T(8,128)(2,1)}) fusion(f32[1024,1408]{0,1:T(8,128)S(1)} %fusion.59, bf16[1024,2048]{1,0:T(8,128)(2,1)S(1)} %copy-done.14, bf16[704,2048]{1,0:T(8,128)(2,1)} %bitcast.27), kind=kOutput, calls=%fused_computation.17 | convolution fusion | flops 2965045248 | bytes 17170432 | tf_op jit(solution)/shard_map/dot_general | solution.py:491
  305.0 10.9 %convolution_convert_fusion.2 = bf16[1024,2048]{1,0:T(8,128)(2,1)} fusion(bf16[2048,1408]{1,0:T(8,128)(2,1)} %bitcast.33, bf16[1024,704]{0,1:T(8,128)(2,1)S(1)} %get-tuple-element.223, bf16[1024,704]{0,1:T(8,128)(2,1)S(1)} %get-tuple-element.222), kind=kOutput, calls=%fused_computation.7 | convolution fusion | flops 5913444352 | bytes 12845056 | tf_op jit(solution)/shard_map/dot_general | solution.py:491
  335.5 6.9 %convolution_convert_fusion.1 = bf16[1024,2048]{1,0:T(8,128)(2,1)} fusion(bf16[1024,704]{0,1:T(8,128)(2,1)S(1)} %copy-done.40, bf16[704,2048]{1,0:T(8,128)(2,1)} %bitcast.27), kind=kOutput, calls=%fused_computation.6 | convolution fusion | flops 2954887168 | bytes 8519680 | tf_op jit(solution)/shard_map/dot_general | solution.py:491
  342.4 13.9 %collective-permute-done.13 = bf16[512,1408]{1,0:T(8,128)(2,1)} collective-permute-done((bf16[512,1408]{1,0:T(8,128)(2,1)}, bf16[512,1408]{1,0:T(8,128)(2,1)}, u32[]{:S(2)}, u32[]{:S(2)}) %collective-permute-start.13) | collective-permute-done | bytes 1441824 | tf_op jit(solution)/shard_map/ppermute | solution.py:500
  356.3 4.2 collective-permute-done.14
  360.5 4.3 reduce-scatter.7.cloned.1.call-done
  369.3 5.1 convolution_convert_fusion.5
  376.8 5.1 convolution_convert_fusion.4
  381.9 24.8 %collective-permute-done.15 = bf16[512,1408]{1,0:T(8,128)(2,1)S(1)} collective-permute-done((bf16[512,1408]{1,0:T(8,128)(2,1)}, bf16[512,1408]{1,0:T(8,128)(2,1)S(1)}, u32[]{:S(2)}, u32[]{:S(2)}) %collective-permute-start.15) | collective-permute-done | bytes 1441824 | tf_op jit(solution)/shard_map/ppermute | solution.py:500
  406.7 8.0 %all-gather.11.cloned.1.call-done = bf16[1024,2048]{1,0:T(8,128)(2,1)} async-done(((bf16[128,2048]{1,0:T(8,128)(2,1)}), bf16[1024,2048]{1,0:T(8,128)(2,1)}) %all-gather.11.cloned.1.call-update) | async-done | bytes 4194320 | tf_op jit(solution)/shard_map/all_gather | solution.py:724
  418.3 4.0 add_convert_fusion
  422.3 3.6 all-to-all-start.2
  426.2 4.0 convolution_convert_fusion.18.dy_ref
  430.3 18.6 %mix_backward.1 = (bf16[1024,1024]{1,0:T(8,128)(2,1)}, f32[1024,2]{1,0:T(8,128)S(1)}, f32[8,768]{1,0:T(8,128)S(1)}, f32[8,128]{1,0:T(8,128)S(1)}) custom-call(bf16[1024,768]{1,0:T(8,128)(2,1)} %slice.88.pre_ref.before_ref, bf16[1024,768]{1,0:T(8,128)(2,1)} %slice.88.pre_ref.before_ref, f32[1024,256]{1,0:T(8,128)S(1)} %copy-done.4, f32[1024,2]{1,0:T(8,128)S(1)} %copy-done.6, ...), custom_call_target="tpu_custom_call" | custom-call | flops 3019898880 | bytes 10485760 | tf_op jit(solution)/shard_map/mix_backward/pallas_call | solution.py:317
  448.9 4.0 convolution_convert_fusion.17
  461.3 7.5 %convolution_convert_fusion = bf16[1024,2048]{1,0:T(8,128)(2,1)} fusion(bf16[2048,1152]{1,0:T(8,128)(2,1)S(1)} %bitcast.143, bf16[1024,128]{1,0:T(8,128)(2,1)S(1)} %pad.30, bf16[1024,1024]{1,0:T(8,128)(2,1)S(1)} %copy-done.18), kind=kOutput, calls=%fused_computation.5 | convolution fusion | flops 4838653952 | bytes 11272192 | tf_op jit(solution)/shard_map/dot_general | solution.py:491
  468.8 14.5 %collective-permute-done.19 = bf16[512,1024]{1,0:T(8,128)(2,1)} collective-permute-done((bf16[512,1024]{1,0:T(8,128)(2,1)}, bf16[512,1024]{1,0:T(8,128)(2,1)}, u32[]{:S(2)}, u32[]{:S(2)}) %collective-permute-start.19) | collective-permute-done | bytes 1048608 | tf_op jit(solution)/shard_map/ppermute | solution.py:500
  486.1 6.5 %reduce-scatter.9.cloned.1.call-done = bf16[128,2048]{1,0:T(8,128)(2,1)} async-done(((bf16[1024,2048]{1,0:T(8,128)(2,1)}), bf16[128,2048]{1,0:T(8,128)(2,1)}) %reduce-scatter.9.cloned.1.call-update) | async-done | bytes 524304 | tf_op jit(solution)/shard_map/reduce_scatter | solution.py:726
  510.6 3.7 fusion.7
  517.9 3.5 convolution_convert_fusion.14
  521.9 3.5 collective-permute-done.23
  526.1 4.4 all-to-all-start.4
  530.6 4.1 add_convert_fusion.1
  534.6 5.2 all-to-all-done.4.small_in_ref
  539.8 4.2 all-to-all-start.3
  544.1 3.5 convolution_convert_fusion.8
  551.1 3.6 collective-permute-start.26
  567.9 4.1 all-to-all-done.3.in_ref
  573.1 3.2 unpack_mix.1
  580.4 3.9 fusion.15
  (284 shorter events, 162.3 us)
Async XLA Ops:
  7.2 50.4 %copy-start = (bf16[64,11264]{1,0:T(8,128)(2,1)S(1)}, bf16[64,11264]{1,0:T(8,128)(2,1)}, u32[]{:S(2)}) copy-start(bf16[64,11264]{1,0:T(8,128)(2,1)} %w_ref.1) | copy-start | bytes 4325380
  15.0 42.6 %all-to-all-start = ((bf16[8,64,1152]{2,1,0:T(8,128)(2,1)}), bf16[8,64,1152]{2,1,0:T(8,128)(2,1)S(1)}, u32[]{:S(2)}, u32[]{:S(2)}) async-start(bf16[8,64,1152]{2,1,0:T(8,128)(2,1)} %pack_mix.1), calls=%async_computation | async-start | bytes 2359296 | tf_op jit(solution)/shard_map/all_to_all | solution.py:570
  21.3 113.0 %all-gather.5.cloned.1.call-start = ((), (), s32[]{:S(2)}) async-start(), calls=%async_computation.9 | async-start | bytes 4718592 | tf_op jit(solution)/shard_map/all_gather | solution.py:631
  21.3 19.0 %collective-permute-start = (bf16[176,2048]{1,0:T(8,128)(2,1)S(1)}, bf16[176,2048]{1,0:T(8,128)(2,1)S(1)}, u32[]{:S(2)}, u32[]{:S(2)}) collective-permute-start(bf16[176,2048]{1,0:T(8,128)(2,1)S(1)} %copy-done.41), channel_id=1, source_target_pairs={{0,8},{8,0},{16,24},{24,16},{1,9},{9,1},{17,25},{25,17},{2,10},{10... | collective-permute-start | bytes 2162696 | tf_op jit(solution)/shard_map/ppermute | solution.py:500
  22.9 33.7 %collective-permute-start.1 = (bf16[176,2048]{1,0:T(8,128)(2,1)S(1)}, bf16[176,2048]{1,0:T(8,128)(2,1)S(1)}, u32[]{:S(2)}, u32[]{:S(2)}) collective-permute-start(bf16[176,2048]{1,0:T(8,128)(2,1)S(1)} %copy-done.41), channel_id=1, source_target_pairs={{0,16},{8,24},{16,0},{24,8},{1,17},{9,25},{17,1},{25,9},{2,18},{10... | collective-permute-start | bytes 2162696 | tf_op jit(solution)/shard_map/ppermute | solution.py:500
  24.4 33.1 %collective-permute-start.2 = (bf16[176,2048]{1,0:T(8,128)(2,1)S(1)}, bf16[176,2048]{1,0:T(8,128)(2,1)}, u32[]{:S(2)}, u32[]{:S(2)}) collective-permute-start(bf16[176,2048]{1,0:T(8,128)(2,1)S(1)} %copy-done.41), channel_id=1, source_target_pairs={{0,24},{8,16},{16,8},{24,0},{1,25},{9,17},{17,9},{25,1},{2,26},{10... | collective-permute-start | bytes 2162696 | tf_op jit(solution)/shard_map/ppermute | solution.py:500
  59.3 71.5 %all-to-all-start.1 = ((bf16[8,64,1408]{2,1,0:T(8,128)(2,1)}), bf16[8,64,1408]{2,1,0:T(8,128)(2,1)S(1)}, u32[]{:S(2)}, u32[]{:S(2)}) async-start(bf16[8,64,1408]{2,1,0:T(8,128)(2,1)} %pack_ff.1), calls=%async_computation.1 | async-start | bytes 2883584 | tf_op jit(solution)/shard_map/all_to_all | solution.py:570
  64.0 123.6 %all-gather.7.cloned.1.call-start = ((), (), s32[]{:S(2)}) async-start(), calls=%async_computation.10 | async-start | bytes 4718592 | tf_op jit(solution)/shard_map/all_gather | solution.py:645
  64.1 29.2 %collective-permute-start.3 = (bf16[512,1152]{1,0:T(8,128)(2,1)}, bf16[512,1152]{1,0:T(8,128)(2,1)}, u32[]{:S(2)}, u32[]{:S(2)}) collective-permute-start(bf16[512,1152]{1,0:T(8,128)(2,1)} %bitcast.149), channel_id=1, source_target_pairs={{0,8},{8,0},{16,24},{24,16},{1,9},{9,1},{17,25},{25,17},{2,10},{10... | collective-permute-start | bytes 3538952 | tf_op jit(solution)/shard_map/ppermute | solution.py:500
  64.5 58.4 %collective-permute-start.4 = (bf16[512,1152]{1,0:T(8,128)(2,1)}, bf16[512,1152]{1,0:T(8,128)(2,1)}, u32[]{:S(2)}, u32[]{:S(2)}) collective-permute-start(bf16[512,1152]{1,0:T(8,128)(2,1)} %bitcast.150), channel_id=1, source_target_pairs={{0,16},{8,24},{16,0},{24,8},{1,17},{9,25},{17,1},{25,9},{2,18},{10... | collective-permute-start | bytes 3538952 | tf_op jit(solution)/shard_map/ppermute | solution.py:500
  69.0 69.7 %collective-permute-start.5 = (bf16[512,1152]{1,0:T(8,128)(2,1)}, bf16[512,1152]{1,0:T(8,128)(2,1)}, u32[]{:S(2)}, u32[]{:S(2)}) collective-permute-start(bf16[512,1152]{1,0:T(8,128)(2,1)} %bitcast.151), channel_id=1, source_target_pairs={{0,24},{8,16},{16,8},{24,0},{1,25},{9,17},{17,9},{25,1},{2,26},{10... | collective-permute-start | bytes 3538952 | tf_op jit(solution)/shard_map/ppermute | solution.py:500
  70.4 88.4 %collective-permute-start.6 = (bf16[64,2048]{1,0:T(8,128)(2,1)}, bf16[64,2048]{1,0:T(8,128)(2,1)}, u32[]{:S(2)}, u32[]{:S(2)}) collective-permute-start(bf16[64,2048]{1,0:T(8,128)(2,1)} %param.24), channel_id=1, source_target_pairs={{0,0},{1,8},{2,2},{3,10},{4,4},{5,12},{6,6},{7,14},{8,16},{9,24},{... | collective-permute-start | bytes 786440 | tf_op jit(solution)/shard_map/ppermute | solution.py:556
  74.0 84.8 %collective-permute-start.7 = (bf16[64,2048]{1,0:T(8,128)(2,1)}, bf16[64,2048]{1,0:T(8,128)(2,1)}, u32[]{:S(2)}, u32[]{:S(2)}) collective-permute-start(bf16[64,2048]{1,0:T(8,128)(2,1)} %param.24), channel_id=1, source_target_pairs={{0,8},{1,0},{2,10},{3,2},{4,12},{5,4},{6,14},{7,6},{8,24},{9,16},{... | collective-permute-start | bytes 786440 | tf_op jit(solution)/shard_map/ppermute | solution.py:556
  93.2 65.6 %collective-permute-start.8 = (bf16[64,2048]{1,0:T(8,128)(2,1)}, bf16[64,2048]{1,0:T(8,128)(2,1)}, u32[]{:S(2)}, u32[]{:S(2)}) collective-permute-start(bf16[64,2048]{1,0:T(8,128)(2,1)} %param.24), channel_id=1, source_target_pairs={{0,16},{1,24},{2,18},{3,26},{4,20},{5,28},{6,22},{7,30},{8,0},{9,8... | collective-permute-start | bytes 786440 | tf_op jit(solution)/shard_map/ppermute | solution.py:556
  123.0 35.9 %collective-permute-start.9 = (bf16[64,2048]{1,0:T(8,128)(2,1)}, bf16[64,2048]{1,0:T(8,128)(2,1)}, u32[]{:S(2)}, u32[]{:S(2)}) collective-permute-start(bf16[64,2048]{1,0:T(8,128)(2,1)} %param.24), channel_id=1, source_target_pairs={{0,24},{1,16},{2,26},{3,18},{4,28},{5,20},{6,30},{7,22},{8,8},{9,0... | collective-permute-start | bytes 786440 | tf_op jit(solution)/shard_map/ppermute | solution.py:556
  134.3 101.9 %reduce-scatter.5.cloned.1.call-start = ((), (), s32[]{:S(2)}) async-start(), calls=%async_computation.11 | async-start | bytes 4718592 | tf_op jit(solution)/shard_map/reduce_scatter | solution.py:678
  164.0 20.3 %copy-start.33 = (bf16[4,64,2048]{2,1,0:T(8,128)(2,1)}, bf16[4,64,2048]{2,1,0:T(8,128)(2,1)S(1)}, u32[]{:S(2)}) copy-start(bf16[4,64,2048]{2,1,0:T(8,128)(2,1)S(1)} %bitcast_dynamic-update-slice_fusion.12) | copy-start | bytes 3145732
  187.6 48.7 %copy-start.20 = (bf16[1,128,2048]{2,1,0:T(8,128)(2,1)S(1)}, bf16[1,128,2048]{2,1,0:T(8,128)(2,1)}, u32[]{:S(2)}) copy-start(bf16[1,128,2048]{2,1,0:T(8,128)(2,1)} %param.14) | copy-start | bytes 1572868
  187.6 54.5 %copy-start.42 = (bf16[176,2048]{1,0:T(8,128)(2,1)S(1)}, bf16[176,2048]{1,0:T(8,128)(2,1)}, u32[]{:S(2)}) copy-start(bf16[176,2048]{1,0:T(8,128)(2,1)} %param.27) | copy-start | bytes 2162692
  187.7 98.0 %all-gather.9.cloned.1.call-start = ((), (), s32[]{:S(2)}) async-start(), calls=%async_computation.12 | async-start | bytes 4718592 | tf_op jit(solution)/shard_map/all_gather | solution.py:685
  187.7 34.0 %collective-permute-start.10 = (bf16[512,1408]{1,0:T(8,128)(2,1)}, bf16[512,1408]{1,0:T(8,128)(2,1)}, u32[]{:S(2)}, u32[]{:S(2)}) collective-permute-start(bf16[512,1408]{1,0:T(8,128)(2,1)} %bitcast.145), channel_id=1, source_target_pairs={{0,8},{8,0},{16,24},{24,16},{1,9},{9,1},{17,25},{25,17},{2,10},{10... | collective-permute-start | bytes 4325384 | tf_op jit(solution)/shard_map/ppermute | solution.py:500
  188.5 33.8 %collective-permute-start.11 = (bf16[512,1408]{1,0:T(8,128)(2,1)}, bf16[512,1408]{1,0:T(8,128)(2,1)}, u32[]{:S(2)}, u32[]{:S(2)}) collective-permute-start(bf16[512,1408]{1,0:T(8,128)(2,1)} %bitcast.146), channel_id=1, source_target_pairs={{0,16},{8,24},{16,0},{24,8},{1,17},{9,25},{17,1},{25,9},{2,18},{10... | collective-permute-start | bytes 4325384 | tf_op jit(solution)/shard_map/ppermute | solution.py:500
  238.1 128.1 %copy-start.47 = (f32[128]{0:T(128)}, f32[128]{0:T(128)S(1)}, u32[]{:S(2)}) copy-start(f32[128]{0:T(128)S(1)} %add_rsqrt_fusion.2) | copy-start | bytes 1540
  240.2 124.6 %reduce-scatter.7.cloned.1.call-start = ((), (), s32[]{:S(2)}) async-start(), calls=%async_computation.13 | async-start | bytes 4718592 | tf_op jit(solution)/shard_map/reduce_scatter | solution.py:702
  247.0 32.0 %collective-permute-start.12 = (bf16[512,1408]{1,0:T(8,128)(2,1)S(1)}, bf16[512,1408]{1,0:T(8,128)(2,1)S(1)}, u32[]{:S(2)}, u32[]{:S(2)}) collective-permute-start(bf16[512,1408]{1,0:T(8,128)(2,1)S(1)} %bitcast.147), channel_id=1, source_target_pairs={{0,24},{8,16},{16,8},{24,0},{1,25},{9,17},{17,9},{25,1},{2,26},{10... | collective-permute-start | bytes 4325384 | tf_op jit(solution)/shard_map/ppermute | solution.py:500
  315.9 98.8 %all-gather.11.cloned.1.call-start = ((), (), s32[]{:S(2)}) async-start(), calls=%async_computation.14 | async-start | bytes 4718592 | tf_op jit(solution)/shard_map/all_gather | solution.py:724
  322.3 34.0 %collective-permute-start.13 = (bf16[512,1408]{1,0:T(8,128)(2,1)}, bf16[512,1408]{1,0:T(8,128)(2,1)}, u32[]{:S(2)}, u32[]{:S(2)}) collective-permute-start(bf16[512,1408]{1,0:T(8,128)(2,1)} %convolution_convert_fusion.7), channel_id=1, source_target_pairs={{0,8},{8,0},{16,24},{24,16},{1,9},{9,1},{17,25},{25,17},{2,10},{10... | collective-permute-start | bytes 4325384 | tf_op jit(solution)/shard_map/ppermute | solution.py:500
  326.8 33.8 %collective-permute-start.14 = (bf16[512,1408]{1,0:T(8,128)(2,1)}, bf16[512,1408]{1,0:T(8,128)(2,1)}, u32[]{:S(2)}, u32[]{:S(2)}) collective-permute-start(bf16[512,1408]{1,0:T(8,128)(2,1)} %convolution_convert_fusion.6), channel_id=1, source_target_pairs={{0,16},{8,24},{16,0},{24,8},{1,17},{9,25},{17,1},{25,9},{2,18},{10... | collective-permute-start | bytes 4325384 | tf_op jit(solution)/shard_map/ppermute | solution.py:500
  335.5 29.3 %copy-start.23 = (bf16[128,2048]{1,0:T(8,128)(2,1)S(1)}, bf16[128,2048]{1,0:T(8,128)(2,1)}, u32[]{:S(2)}) copy-start(bf16[128,2048]{1,0:T(8,128)(2,1)} %reduce-scatter.5.cloned.1.call-done) | copy-start | bytes 1572868
  369.3 123.3 %reduce-scatter.9.cloned.1.call-start = ((), (), s32[]{:S(2)}) async-start(), calls=%async_computation.15 | async-start | bytes 4718592 | tf_op jit(solution)/shard_map/reduce_scatter | solution.py:726
  374.4 32.3 %collective-permute-start.15 = (bf16[512,1408]{1,0:T(8,128)(2,1)}, bf16[512,1408]{1,0:T(8,128)(2,1)S(1)}, u32[]{:S(2)}, u32[]{:S(2)}) collective-permute-start(bf16[512,1408]{1,0:T(8,128)(2,1)} %convolution_convert_fusion.5), channel_id=1, source_target_pairs={{0,24},{8,16},{16,8},{24,0},{1,25},{9,17},{17,9},{25,1},{2,26},{10... | collective-permute-start | bytes 4325384 | tf_op jit(solution)/shard_map/ppermute | solution.py:500
  414.8 42.7 %collective-permute-start.16 = (bf16[176,2048]{1,0:T(8,128)(2,1)}, bf16[176,2048]{1,0:T(8,128)(2,1)}, u32[]{:S(2)}, u32[]{:S(2)}) collective-permute-start(bf16[176,2048]{1,0:T(8,128)(2,1)} %convolution_convert_fusion.12), channel_id=1, source_target_pairs={{0,8},{8,0},{16,24},{24,16},{1,9},{9,1},{17,25},{25,17},{2,10},{10... | collective-permute-start | bytes 2162696 | tf_op jit(solution)/shard_map/ppermute | solution.py:500
  416.3 41.2 %collective-permute-start.17 = (bf16[176,2048]{1,0:T(8,128)(2,1)}, bf16[176,2048]{1,0:T(8,128)(2,1)}, u32[]{:S(2)}, u32[]{:S(2)}) collective-permute-start(bf16[176,2048]{1,0:T(8,128)(2,1)} %convolution_convert_fusion.11), channel_id=1, source_target_pairs={{0,16},{8,24},{16,0},{24,8},{1,17},{9,25},{17,1},{25,9},{2,18},{10... | collective-permute-start | bytes 2162696 | tf_op jit(solution)/shard_map/ppermute | solution.py:500
  417.8 39.7 %collective-permute-start.18 = (bf16[176,2048]{1,0:T(8,128)(2,1)}, bf16[176,2048]{1,0:T(8,128)(2,1)}, u32[]{:S(2)}, u32[]{:S(2)}) collective-permute-start(bf16[176,2048]{1,0:T(8,128)(2,1)} %convolution_convert_fusion.10), channel_id=1, source_target_pairs={{0,24},{8,16},{16,8},{24,0},{1,25},{9,17},{17,9},{25,1},{2,26},{10... | collective-permute-start | bytes 2162696 | tf_op jit(solution)/shard_map/ppermute | solution.py:500
  422.3 63.7 %all-to-all-start.2 = ((bf16[8,64,1408]{2,1,0:T(8,128)(2,1)}), bf16[8,64,1408]{2,1,0:T(8,128)(2,1)S(1)}, u32[]{:S(2)}, u32[]{:S(2)}) async-start(bf16[8,64,1408]{2,1,0:T(8,128)(2,1)} %bitcast.144), calls=%async_computation.5 | async-start | bytes 2883584 | tf_op jit(solution)/shard_map/all_to_all | solution.py:570
  425.9 153.1 %reduce-scatter.11.cloned.1.call-start = ((), (), s32[]{:S(2)}) async-start(), calls=%async_computation.16 | async-start | bytes 4718592 | tf_op jit(solution)/shard_map/reduce_scatter | solution.py:751
  457.5 25.8 %collective-permute-start.19 = (bf16[512,1024]{1,0:T(8,128)(2,1)}, bf16[512,1024]{1,0:T(8,128)(2,1)}, u32[]{:S(2)}, u32[]{:S(2)}) collective-permute-start(bf16[512,1024]{1,0:T(8,128)(2,1)} %convolution_convert_fusion.17), channel_id=1, source_target_pairs={{0,8},{8,0},{16,24},{24,16},{1,9},{9,1},{17,25},{25,17},{2,10},{10... | collective-permute-start | bytes 3145736 | tf_op jit(solution)/shard_map/ppermute | solution.py:500
  459.0 25.5 %collective-permute-start.20 = (bf16[512,1024]{1,0:T(8,128)(2,1)}, bf16[512,1024]{1,0:T(8,128)(2,1)}, u32[]{:S(2)}, u32[]{:S(2)}) collective-permute-start(bf16[512,1024]{1,0:T(8,128)(2,1)} %convolution_convert_fusion.16), channel_id=1, source_target_pairs={{0,16},{8,24},{16,0},{24,8},{1,17},{9,25},{17,1},{25,9},{2,18},{10... | collective-permute-start | bytes 3145736 | tf_op jit(solution)/shard_map/ppermute | solution.py:500
  492.6 37.9 %collective-permute-start.21 = (bf16[512,1024]{1,0:T(8,128)(2,1)}, bf16[512,1024]{1,0:T(8,128)(2,1)}, u32[]{:S(2)}, u32[]{:S(2)}) collective-permute-start(bf16[512,1024]{1,0:T(8,128)(2,1)} %convolution_convert_fusion.15), channel_id=1, source_target_pairs={{0,24},{8,16},{16,8},{24,0},{1,25},{9,17},{17,9},{25,1},{2,26},{10... | collective-permute-start | bytes 3145736 | tf_op jit(solution)/shard_map/ppermute | solution.py:500
  514.4 7.5 %collective-permute-start.24 = (bf16[512,128]{1,0:T(8,128)(2,1)S(1)}, bf16[512,128]{1,0:T(8,128)(2,1)S(1)}, u32[]{:S(2)}, u32[]{:S(2)}) collective-permute-start(bf16[512,128]{1,0:T(8,128)(2,1)S(1)} %get-tuple-element.232), channel_id=1, source_target_pairs={{0,24},{8,16},{16,8},{24,0},{1,25},{9,17},{17,9},{25,1},{2,26},{10... | collective-permute-start | bytes 393224 | tf_op jit(solution)/shard_map/ppermute | solution.py:500
  515.0 10.4 %collective-permute-start.23 = (bf16[512,128]{1,0:T(8,128)(2,1)S(1)}, bf16[512,128]{1,0:T(8,128)(2,1)S(1)}, u32[]{:S(2)}, u32[]{:S(2)}) collective-permute-start(bf16[512,128]{1,0:T(8,128)(2,1)S(1)} %get-tuple-element.233), channel_id=1, source_target_pairs={{0,16},{8,24},{16,0},{24,8},{1,17},{9,25},{17,1},{25,9},{2,18},{10... | collective-permute-start | bytes 393224 | tf_op jit(solution)/shard_map/ppermute | solution.py:500
  516.5 8.9 %collective-permute-start.22 = (bf16[512,128]{1,0:T(8,128)(2,1)S(1)}, bf16[512,128]{1,0:T(8,128)(2,1)S(1)}, u32[]{:S(2)}, u32[]{:S(2)}) collective-permute-start(bf16[512,128]{1,0:T(8,128)(2,1)S(1)} %get-tuple-element.231), channel_id=1, source_target_pairs={{0,8},{8,0},{16,24},{24,16},{1,9},{9,1},{17,25},{25,17},{2,10},{10... | collective-permute-start | bytes 393224 | tf_op jit(solution)/shard_map/ppermute | solution.py:500
  526.1 13.7 %all-to-all-start.4 = ((bf16[8,64,128]{2,1,0:T(8,128)(2,1)}), bf16[8,64,128]{2,1,0:T(8,128)(2,1)S(1)}, u32[]{:S(2)}, u32[]{:S(2)}) async-start(bf16[8,64,128]{2,1,0:T(8,128)(2,1)} %bitcast.164), calls=%async_computation.8 | async-start | bytes 262144 | tf_op jit(solution)/shard_map/all_to_all | solution.py:570
  539.8 32.1 %all-to-all-start.3 = ((bf16[8,64,1024]{2,1,0:T(8,128)(2,1)}), bf16[8,64,1024]{2,1,0:T(8,128)(2,1)}, u32[]{:S(2)}, u32[]{:S(2)}) async-start(bf16[8,64,1024]{2,1,0:T(8,128)(2,1)} %bitcast.153), calls=%async_computation.7 | async-start | bytes 2097152 | tf_op jit(solution)/shard_map/all_to_all | solution.py:570
  548.6 14.2 %collective-permute-start.28 = (bf16[64,2048]{1,0:T(8,128)(2,1)}, bf16[64,2048]{1,0:T(8,128)(2,1)}, u32[]{:S(2)}, u32[]{:S(2)}) collective-permute-start(bf16[64,2048]{1,0:T(8,128)(2,1)} %get-tuple-element.226), channel_id=1, source_target_pairs={{16,0},{24,1},{18,2},{26,3},{20,4},{28,5},{22,6},{30,7},{0,8},{8,9... | collective-permute-start | bytes 786440 | tf_op jit(solution)/shard_map/ppermute | solution.py:565
  550.1 12.8 %collective-permute-start.27 = (bf16[64,2048]{1,0:T(8,128)(2,1)}, bf16[64,2048]{1,0:T(8,128)(2,1)}, u32[]{:S(2)}, u32[]{:S(2)}) collective-permute-start(bf16[64,2048]{1,0:T(8,128)(2,1)} %get-tuple-element.227), channel_id=1, source_target_pairs={{8,0},{0,1},{10,2},{2,3},{12,4},{4,5},{14,6},{6,7},{24,8},{16,9},{... | collective-permute-start | bytes 786440 | tf_op jit(solution)/shard_map/ppermute | solution.py:565
  551.1 11.7 %collective-permute-start.26 = (bf16[64,2048]{1,0:T(8,128)(2,1)}, bf16[64,2048]{1,0:T(8,128)(2,1)}, u32[]{:S(2)}, u32[]{:S(2)}) collective-permute-start(bf16[64,2048]{1,0:T(8,128)(2,1)} %get-tuple-element.228), channel_id=1, source_target_pairs={{0,0},{8,1},{2,2},{10,3},{4,4},{12,5},{6,6},{14,7},{16,8},{24,9},{... | collective-permute-start | bytes 786440 | tf_op jit(solution)/shard_map/ppermute | solution.py:565
  554.7 11.1 %collective-permute-start.25 = (bf16[64,2048]{1,0:T(8,128)(2,1)}, bf16[64,2048]{1,0:T(8,128)(2,1)}, u32[]{:S(2)}, u32[]{:S(2)}) collective-permute-start(bf16[64,2048]{1,0:T(8,128)(2,1)} %get-tuple-element.225), channel_id=1, source_target_pairs={{24,0},{16,1},{26,2},{18,3},{28,4},{20,5},{30,6},{22,7},{8,8},{0,9... | collective-permute-start | bytes 786440 | tf_op jit(solution)/shard_map/ppermute | solution.py:565
  (52 other events, 397.6 us)
Sparse Core Ops, SparseCore 0:
  57.7 76.5 all-gather.4
  136.5 45.1 all-gather.6
  187.8 48.4 reduce-scatter.4
  240.3 45.2 all-gather.8
  316.1 48.7 reduce-scatter.6
  369.4 45.2 all-gather.10
  417.0 75.5 reduce-scatter.8
  494.9 55.1 reduce-scatter.10
where the time goes:
time: 602 us; the launch traced here: 592 us
  waiting for transfers between devices  254 us (42%)
  matrix products  98.8 us (16%)
  starting transfers between devices  70.3 us (12%)
  local copies, waits for them, and re-layouts  65.3 us (11%)
  Pallas kernels  45.5 us (8%)
  other arithmetic  41.2 us (7%)
  between operations  16.2 us (3%)
    ppermute x21, waiting for transfers between devices, swapped(): return lax.ppermute(value, axis, [(i, i ^ distance) for i in range(count)])  193 us
    dot_general x22, matrix products, dot(): lax.dot_general(left, right, (dims, ((), ())), preferred_element_type=F32)  98.8 us
    ppermute x21, starting transfers between devices, swapped(): return lax.ppermute(value, axis, [(i, i ^ distance) for i in range(count)])  29.8 us
    all_to_all x5, starting transfers between devices, spread(): return lax.all_to_all(value, axis, 0, 0, tiled=True)  23.3 us
    dynamic_update_slice x16, local copies, waits for them, and re-layouts, placed(): whole = lax.dynamic_update_index_in_dim(whole, part, place, 0)  20.9 us
    pallas_call x1, Pallas kernels, mix_backward(): pl.pallas_call(functools.partial(mix_backward_kernel, heads=heads, blocks...  18.6 us
    pallas_call x1, Pallas kernels, mix_forward(): pl.pallas_call(functools.partial(mix_forward_kernel, heads=heads), grid=(...  17.3 us
    all_to_all x5, waiting for transfers between devices, spread(): return lax.all_to_all(value, axis, 0, 0, tiled=True)  16.8 us
  transfers between devices with their start and end apart: 42, of which 25 were waited for; matrix products, arithmetic and copies ran while one was open for 25% of the time, Pallas kernels for 7%

commit v1 on v0

--- a/solution.py
+++ b/solution.py
@@ -11,7 +11,8 @@
 CONV = 4
 HD = 128
 CHUNK = 128
-STEP = 256
+STEP = 512
+SMALL = 64
 EPS = 1e-05
 KEY_EPS = 1e-06
 BF = jnp.bfloat16
@@ -83,12 +84,17 @@
     return raw * scale, scale
 
 
+def conv_inputs(first, second, width):
+    pre = jnp.concatenate([first[:, : 2 * width], second[:, :width]], axis=1)
+    return pre.astype(BF).astype(F32)
+
+
 def mix_forward_kernel(
-    pre_ref, gate_ref, beta_ref, taps_ref, gain_ref, y_ref, core_ref, state_ref, inverse_ref,
-    state_now, rim, *, heads
+    first_ref, second_ref, taps_ref, gain_ref, y_ref, core_ref, state_ref, inverse_ref, state_now,
+    rim, *, heads
 ):
     width = heads * HD
-    step = pre_ref.shape[0]
+    step = first_ref.shape[0]
     chunks = step // CHUNK
 
     @pl.when(pl.program_id(0) == 0)
@@ -96,12 +102,12 @@
         state_now[...] = jnp.zeros_like(state_now)
         rim[...] = jnp.zeros_like(rim)
 
-    pre = pre_ref[...].astype(F32)
+    pre = conv_inputs(first_ref[...], second_ref[...], width)
     extended = jnp.concatenate([rim[...], pre], axis=0)
     rim[...] = pre[step - 8 :]
     conv = conv_taps(extended, taps_ref[...], step)
     mixture = conv * sigmoid(conv)
-    beta = sigmoid(beta_ref[...])
+    beta = sigmoid(first_ref[:, 2 * width : 2 * width + heads])
     row_ids, col_ids = chunk_ids()
     tiles = [(chunk, head) for chunk in range(chunks) for head in range(heads)]
     q_t, k_t, v_t, b_t, score_t, strict_t = [], [], [], [], [], []
@@ -131,18 +137,18 @@
         state_now[head] = state + mm(k_t[index], update, TN)
         core_ref[rows, cols] = core
         scale = lax.rsqrt(jnp.mean(core * core, axis=-1, keepdims=True) + EPS)
-        gate = gate_ref[rows, cols]
+        gate = second_ref[rows, width + head * HD : width + (head + 1) * HD]
         y_ref[rows, cols] = (
             core * scale * gain_ref[...] * (gate * sigmoid(gate))
         ).astype(y_ref.dtype)
 
 
 def mix_backward_kernel(
-    pre_ref, before_ref, gate_ref, beta_ref, dy_ref, core_ref, state_ref, inverse_ref, taps_ref,
-    gain_ref, dproj_ref, dbeta_ref, gtaps_ref, ggain_ref, adjoint, rim, *, heads, blocks
+    first_ref, second_ref, first_before_ref, second_before_ref, dy_ref, core_ref, state_ref,
+    inverse_ref, taps_ref, gain_ref, dproj_ref, dbeta_ref, gtaps_ref, ggain_ref, adjoint, rim, *, heads, blocks
 ):
     width = heads * HD
-    step = pre_ref.shape[0]
+    step = first_ref.shape[0]
     chunks = step // CHUNK
     block = blocks - 1 - pl.program_id(0)
 
@@ -153,14 +159,16 @@
         gtaps_ref[...] = jnp.zeros_like(gtaps_ref)
         ggain_ref[...] = jnp.zeros_like(ggain_ref)
 
-    before = before_ref[...].astype(F32)
+    before = conv_inputs(first_before_ref[...], second_before_ref[...], width)
     before = jnp.where(block > 0, before[before.shape[0] - 8 :], 0.0)
-    extended = jnp.concatenate([before, pre_ref[...].astype(F32)], axis=0)
+    extended = jnp.concatenate(
+        [before, conv_inputs(first_ref[...], second_ref[...], width)], axis=0
+    )
     taps = taps_ref[...]
     conv = conv_taps(extended, taps, step)
     conv_sig = sigmoid(conv)
     mixture = conv * conv_sig
-    beta = sigmoid(beta_ref[...])
+    beta = sigmoid(first_ref[:, 2 * width : 2 * width + heads])
     gain = gain_ref[...]
     row_ids, col_ids = chunk_ids()
     causal, strict = row_ids >= col_ids, row_ids > col_ids
@@ -176,7 +184,7 @@
         b_rows = beta[rows, head : head + 1]
         core = core_ref[rows, cols]
         scale = lax.rsqrt(jnp.mean(core * core, axis=-1, keepdims=True) + EPS)
-        gate = gate_ref[rows, cols]
+        gate = second_ref[rows, width + head * HD : width + (head + 1) * HD]
         gate_sig = sigmoid(gate)
         dy = dy_ref[rows, cols].astype(F32)
         normed = core * scale
@@ -258,9 +266,8 @@
     ggain_ref[0:1] += ggain
 
 
-def mix_forward(pre, gate, beta, taps, gain):
-    extent, width3 = pre.shape
-    width = width3 // 3
+def mix_forward(first, second, taps, gain):
+    extent, width = first.shape[0], second.shape[1] // 2
     heads = width // HD
     step = min(STEP, extent)
     blocks, chunks = extent // step, step // CHUNK
@@ -268,10 +275,9 @@
         functools.partial(mix_forward_kernel, heads=heads),
         grid=(blocks,),
         in_specs=[
-            pl.BlockSpec((step, width3), lambda i: (i, 0)),
-            pl.BlockSpec((step, width), lambda i: (i, 0)),
-            pl.BlockSpec((step, heads), lambda i: (i, 0)),
-            pl.BlockSpec((8, width3), lambda i: (0, 0)),
+            pl.BlockSpec((step, first.shape[1]), lambda i: (i, 0)),
+            pl.BlockSpec((step, 2 * width), lambda i: (i, 0)),
+            pl.BlockSpec((8, 3 * width), lambda i: (0, 0)),
             pl.BlockSpec((1, HD), lambda i: (0, 0)),
         ],
         out_specs=[
@@ -286,7 +292,7 @@
             jax.ShapeDtypeStruct((extent // CHUNK, heads, HD, HD), F32),
             jax.ShapeDtypeStruct((extent // CHUNK, heads, CHUNK, CHUNK), F32),
         ],
-        scratch_shapes=[pltpu.VMEM((heads, HD, HD), F32), pltpu.VMEM((8, width3), F32)],
+        scratch_shapes=[pltpu.VMEM((heads, HD, HD), F32), pltpu.VMEM((8, 3 * width), F32)],
         compiler_params=pltpu.CompilerParams(
             dimension_semantics=("arbitrary",), vmem_limit_bytes=48 * 1024 * 1024
         ),
@@ -294,12 +300,12 @@
             flops=90 * extent * width * CHUNK, bytes_accessed=40 * extent * width, transcendentals=0
         ),
         name="mix_forward",
-    )(pre, gate, beta, taps, gain)
-
-
-def mix_backward(pre, gate, beta, dy, core, states, inverses, taps, gain):
-    extent, width3 = pre.shape
-    width = width3 // 3
+    )(first, second, taps, gain)
+
+
+def mix_backward(first, second, dy, core, states, inverses, taps, gain):
+    extent, width = first.shape[0], second.shape[1] // 2
+    width3 = 3 * width
     heads = width // HD
     step = min(STEP, extent)
     blocks, chunks = extent // step, step // CHUNK
@@ -318,10 +324,10 @@
         functools.partial(mix_backward_kernel, heads=heads, blocks=blocks),
         grid=(blocks,),
         in_specs=[
-            pl.BlockSpec((step, width3), at),
-            pl.BlockSpec((rows_before, width3), just_before),
-            pl.BlockSpec((step, width), at),
-            pl.BlockSpec((step, heads), at),
+            pl.BlockSpec((step, first.shape[1]), at),
+            pl.BlockSpec((step, 2 * width), at),
+            pl.BlockSpec((rows_before, first.shape[1]), just_before),
+            pl.BlockSpec((rows_before, 2 * width), just_before),
             pl.BlockSpec((step, width), at),
             pl.BlockSpec((step, width), at),
             pl.BlockSpec((chunks, heads, HD, HD), at_tiles),
@@ -349,7 +355,7 @@
             flops=90 * extent * width * CHUNK, bytes_accessed=40 * extent * width, transcendentals=0
         ),
         name="mix_backward",
-    )(pre, pre, gate, beta, dy, core, states, inverses, taps, gain)
+    )(first, second, first, second, dy, core, states, inverses, taps, gain)
 
 
 def heads_of(ctx, ctxs, heads, row_part):
@@ -358,37 +364,126 @@
     return [((ctx % blocks) * heads + slot) * groups + ctx // blocks for slot in range(heads)]
 
 
-def pack_mix_kernel(qkv_ref, gate_ref, beta_ref, small_ref, out_ref):
-    ctxs = out_ref.shape[0]
+def pack_mix_kernel(
+    qkv_ref, gate_ref, beta_ref, again_ref, fgain_ref, ogain_ref, taps_ref, first_ref, second_ref
+):
+    ctxs = first_ref.shape[0]
     rows, total = gate_ref.shape
     width = total // ctxs
     heads = beta_ref.shape[1] // ctxs
-    small = small_ref[...]
+    row_ids = lax.broadcasted_iota(jnp.int32, (rows, SMALL), 0)
+
+    def lanes(values):
+        values = values.astype(F32)
+        missing = SMALL - values.shape[1]
+        if missing:
+            values = jnp.concatenate([values, jnp.zeros((1, missing), F32)], axis=1)
+        return values
+
+    lines = [again_ref[...], fgain_ref[...], ogain_ref[...]]
+    taps = taps_ref[...].astype(F32)
+    for tap in range(CONV):
+        for start in range(0, taps.shape[1], SMALL):
+            lines.append(taps[tap : tap + 1, start : start + SMALL])
+    small = jnp.zeros((rows, SMALL), F32)
+    for row, line in enumerate(lines):
+        small = jnp.where(row_ids == row, lanes(line), small)
+    betas = beta_ref[...].astype(F32)
     for ctx in range(ctxs):
-        betas = []
+        own = []
         for slot, head in enumerate(heads_of(ctx, ctxs, heads, rows)):
             to, cols = slot * HD, slice(head * HD, (head + 1) * HD)
             for part in range(3):
-                out_ref[ctx, :, part * width + to : part * width + to + HD] = qkv_ref[
+                out_ref = second_ref if part == 2 else first_ref
+                start = to + (width if part == 1 else 0)
+                out_ref[ctx, :, start : start + HD] = qkv_ref[
                     :, part * total + head * HD : part * total + (head + 1) * HD
                 ]
-            out_ref[ctx, :, 3 * width + to : 3 * width + to + HD] = gate_ref[:, cols]
-            betas.append(beta_ref[:, head : head + 1])
-        out_ref[ctx, :, 4 * width :] = jnp.concatenate(betas + [small], axis=1)
-
-
-def pack_mix(w_qkv, w_gate_o, w_beta, small, ctxs):
+            second_ref[ctx, :, width + to : width + to + HD] = gate_ref[:, cols]
+            own.append(betas[:, head : head + 1])
+        own.append(jnp.zeros((rows, 128 - SMALL - heads), F32))
+        first_ref[ctx, :, 2 * width :] = jnp.concatenate(own + [small], axis=1).astype(
+            first_ref.dtype
+        )
+
+
+def pack_mix(w_qkv, w_gate_o, w_beta, attn_gain, ffn_gain, norm_gain_o, conv_weight, ctxs):
     rows, total = w_gate_o.shape
-    cols = 4 * (total // ctxs) + 128
+    width = total // ctxs
     return pl.pallas_call(
         pack_mix_kernel,
-        out_shape=jax.ShapeDtypeStruct((ctxs, rows, cols), w_qkv.dtype),
+        out_shape=[
+            jax.ShapeDtypeStruct((ctxs, rows, 2 * width + 128), w_qkv.dtype),
+            jax.ShapeDtypeStruct((ctxs, rows, 2 * width), w_qkv.dtype),
+        ],
+        compiler_params=pltpu.CompilerParams(vmem_limit_bytes=48 * 1024 * 1024),
         name="pack_mix",
-    )(w_qkv, w_gate_o, w_beta, small)
+    )(
+        w_qkv, w_gate_o, w_beta, attn_gain[None, :], ffn_gain[None, :], norm_gain_o[None, :],
+        conv_weight,
+    )
+
+
+def read_small_kernel(
+    in_ref, again_ref, fgain_ref, ogain_ref, taps_ref, all_taps, *, row_part, taps_part, gain_part
+):
+    values = in_ref[...].astype(F32)
+    devices = values.shape[0] // row_part
+    lines = -(-taps_part // SMALL)
+
+    def line(row, size):
+        starts = [device * row_part + row for device in range(devices)]
+        return jnp.concatenate(
+            [values[at : at + 1, 128 - SMALL : 128 - SMALL + size] for at in starts], axis=1
+        )
+
+    again_ref[...] = line(0, row_part)
+    fgain_ref[...] = line(1, row_part)
+    ogain_ref[...] = line(2, gain_part)
+    for tap in range(CONV):
+        pieces = []
+        for device in range(devices):
+            for index in range(lines):
+                at = device * row_part + 3 + tap * lines + index
+                size = min(SMALL, taps_part - index * SMALL)
+                pieces.append(values[at : at + 1, 128 - SMALL : 128 - SMALL + size])
+        all_taps[tap : tap + 1] = jnp.concatenate(pieces, axis=1)
+    taps_ref[...] = jnp.zeros_like(taps_ref)
+    total = all_taps.shape[1] // 3
+    width = taps_ref.shape[1] // 3
+    heads = width // HD
+    ctxs = total // width
+    ctx = lax.axis_index("ctx")
+    blocks = HD // row_part
+    for slot in range(heads):
+        head = ((ctx % blocks) * heads + slot) * (ctxs // blocks) + ctx // blocks
+        for part in range(3):
+            start = pl.multiple_of(part * total + head * HD, HD)
+            to = part * width + slot * HD
+            taps_ref[0:CONV, to : to + HD] = all_taps[0:CONV, pl.ds(start, HD)]
+
+
+def read_small(w_small, row_part, taps_part, gain_part, width):
+    rows = w_small.shape[0]
+    total = 3 * rows
+    return pl.pallas_call(
+        functools.partial(
+            read_small_kernel, row_part=row_part, taps_part=taps_part, gain_part=gain_part
+        ),
+        out_shape=[
+            jax.ShapeDtypeStruct((1, rows), F32),
+            jax.ShapeDtypeStruct((1, rows), F32),
+            jax.ShapeDtypeStruct((1, HD), F32),
+            jax.ShapeDtypeStruct((8, 3 * width), F32),
+        ],
+        scratch_shapes=[pltpu.VMEM((8, total), F32)],
+        compiler_params=pltpu.CompilerParams(vmem_limit_bytes=48 * 1024 * 1024),
+        name="read_small",
+    )(w_small)
 
 
 def unpack_mix_kernel(
-    in_ref, small_in_ref, qkv_ref, gate_ref, beta_ref, gqkv_ref, ggate_ref, gbeta_ref, small_ref,
+    in_ref, qkv_ref, gate_ref, beta_ref, gqkv_ref, ggate_ref, gbeta_ref, small_ref,
     rows_ref
 ):
     ctxs = in_ref.shape[0]
@@ -399,7 +494,7 @@
     small_sum = jnp.zeros(small_ref.shape, F32)
     betas = [None] * (heads * ctxs)
     for ctx in range(ctxs):
-        small = small_in_ref[ctx].astype(F32)
+        small = in_ref[ctx, :, 4 * width :].astype(F32)
         small_sum += small
         for slot, head in enumerate(heads_of(ctx, ctxs, heads, rows)):
             betas[head] = small[:, slot : slot + 1]
@@ -421,7 +516,7 @@
     rows_ref[...] = row_sum + jnp.sum(grad * beta_ref[...].astype(F32), axis=1, keepdims=True)
 
 
-def unpack_mix(received, small, w_qkv, w_gate_o, w_beta):
+def unpack_mix(received, w_qkv, w_gate_o, w_beta):
     rows = w_qkv.shape[0]
     return pl.pallas_call(
         unpack_mix_kernel,
@@ -434,7 +529,7 @@
         ],
         compiler_params=pltpu.CompilerParams(vmem_limit_bytes=48 * 1024 * 1024),
         name="unpack_mix",
-    )(received, small, w_qkv, w_gate_o, w_beta)
+    )(received, w_qkv, w_gate_o, w_beta)
 
 
 def pack_ff_kernel(in_ref, out_ref, *, dps):
@@ -519,6 +614,56 @@
 def placed_shards(parts, axis):
     place = lax.axis_index(axis)
     return placed(parts, [place ^ distance for distance in range(len(parts))])
+
+
+def gather_start(shard, axis):
+    if lax.axis_size(axis) != 4:
+        return shards_of(shard, axis)[1:]
+    half = shard.shape[0] // 2
+    return [swapped(shard[:half], axis, 1), swapped(shard[half:], axis, 2)]
+
+
+def gather_end(shard, moved, axis):
+    count, place = lax.axis_size(axis), lax.axis_index(axis)
+    if count != 4:
+        return placed_shards([shard] + moved, axis)
+    half = shard.shape[0] // 2
+    tops = swapped(jnp.stack([shard[:half], moved[0]]), axis, 2)
+    ends = swapped(jnp.stack([shard[half:], moved[1]]), axis, 1)
+    parts = [shard[:half], shard[half:], moved[0], moved[1], tops[0], ends[0], tops[1], ends[1]]
+    order = [(0, 0), (0, 1), (1, 0), (2, 1), (2, 0), (1, 1), (3, 0), (3, 1)]
+    whole = placed(parts, [2 * (place ^ distance) + side for distance, side in order])
+    return whole.reshape((count,) + shard.shape)
+
+
+def reduce_parts(part_of, axis):
+    count, place = lax.axis_size(axis), lax.axis_index(axis)
+    parts = [part_of(place ^ distance) for distance in range(count)]
+    if count != 4:
+        return parts[1:], parts[:1]
+    half = parts[0].shape[0] // 2
+    sent = [
+        jnp.stack([parts[1][:half], parts[3][:half]]), jnp.stack([parts[2][half:], parts[3][half:]])
+    ]
+    return sent, [parts[0], parts[2][:half], parts[1][half:]]
+
+
+def reduce_start(sent, axis):
+    if lax.axis_size(axis) != 4:
+        return [swapped(part, axis, index + 1) for index, part in enumerate(sent)]
+    return [swapped(sent[0], axis, 1), swapped(sent[1], axis, 2)]
+
+
+def reduce_end(moved, kept, axis):
+    if lax.axis_size(axis) != 4:
+        return total_of(moved + kept)
+    own, top, end = kept
+    half = own.shape[0] // 2
+    top = swapped((top.astype(F32) + moved[0][1].astype(F32)).astype(BF), axis, 2)
+    end = swapped((end.astype(F32) + moved[1][1].astype(F32)).astype(BF), axis, 1)
+    top = total_of([moved[0][0], top, own[:half]])
+    end = total_of([moved[1][0], end, own[half:]])
+    return jnp.concatenate([top, end], axis=0)
 
 
 def shard_parts(part_of, axis):
@@ -613,79 +758,62 @@
     gain_part = norm_gain_o.shape[0]
     head_dims = (HD // row_part, heads, ctxs * row_part // HD)
 
-    small = jnp.concatenate(
-        [
-            attn_gain[:, None],
-            ffn_gain[:, None],
-            jnp.pad(norm_gain_o, (0, row_part - gain_part))[:, None],
-            conv_weight.reshape(row_part, taps_cols),
-        ],
-        axis=1,
-    )
-    small = jnp.pad(small, ((0, 0), (0, 128 - heads - small.shape[1])))
-    mix_rows = pack_mix(w_qkv, w_gate_o, w_beta, small, ctxs)
-    mix_half = spread(mix_rows, "ctx").reshape(dp_rows, mix_rows.shape[2])
-    down_parts = shards_of(w_down, "dp")
-    mix_half, *down_parts = lax.optimization_barrier((mix_half, *down_parts))
-    mix_parts = shards_of(mix_half, "dp")
-    x_full = lax.all_gather(after(tokens[0], mix_half), "ctx", axis=0, tiled=True)
-    gate_up_rows = pack_ff(w_gate_up, ctxs, dps)
-    gate_up_half = spread(after(gate_up_rows, mix_half), "ctx").reshape(dp_rows, 2 * ff_local)
-    x_full, gate_up_half, *mix_parts[1:3] = lax.optimization_barrier(
-        (x_full, gate_up_half, *mix_parts[1:3])
-    )
-    out_parts = head_owner_parts(after(w_out, mix_half))
-    w_mix = placed_shards(mix_parts, "dp").reshape(width, mix_rows.shape[2])
-
+    x_full = lax.all_gather(tokens[0], "ctx", axis=0, tiled=True)
     matches = group_ids[:, None] == lax.broadcasted_iota(
         jnp.int32, (group_ids.shape[0], group_scale.shape[0]), 1
     )
     seq_scale = jnp.sum(jnp.where(matches, group_scale[None, :], 0.0), axis=1)
     d_out = cotangent[0].astype(F32) * seq_scale[0]
     d_out_full = lax.all_gather(after(d_out.astype(BF), x_full), "ctx", axis=0, tiled=True)
-
-    w_small = lax.optimization_barrier(w_mix[:, 4 * mix_width :].T)
-    place = heads
-    attn_full = w_small[place].astype(F32)
-    ffn_full = w_small[place + 1].astype(F32)
-    norm_o_full = w_small[place + 2].reshape(devices, row_part)[:, :gain_part]
-    norm_o_full = norm_o_full.reshape(1, HD).astype(F32)
-    conv_full = (
-        w_small[place + 3 : place + 3 + taps_cols]
-        .reshape(taps_cols, devices, row_part)
-        .transpose(1, 2, 0)
-        .reshape(devices, CONV, taps_part)
-        .transpose(1, 0, 2)
-        .reshape(CONV, 3, *head_dims, HD)
-        .transpose(4, 2, 0, 1, 3, 5)
-        .reshape(ctxs, CONV, 3 * mix_width)
-    )
-    taps = lax.dynamic_index_in_dim(conv_full, ctx_place, 0, False)
-    taps = jnp.pad(taps.astype(F32), ((0, 8 - CONV), (0, 0)))
+    first_rows, second_rows = pack_mix(
+        w_qkv, w_gate_o, w_beta, attn_gain, ffn_gain, norm_gain_o, conv_weight, ctxs
+    )
+    first_half = spread(first_rows, "ctx").reshape(dp_rows, first_rows.shape[2])
+    down_parts = shards_of(w_down, "dp")
+    first_half, *down_parts = lax.optimization_barrier((first_half, *down_parts))
+    second_half = spread(after(second_rows, first_half), "ctx").reshape(dp_rows, 2 * mix_width)
+    first_parts = shards_of(first_half, "dp")
+    second_half, *first_parts[1:3] = lax.optimization_barrier((second_half, *first_parts[1:3]))
+    second_parts = shards_of(second_half, "dp")
+    gate_up_rows = pack_ff(w_gate_up, ctxs, dps)
+    gate_up_half = spread(after(gate_up_rows, second_half), "ctx").reshape(dp_rows, 2 * ff_local)
 
     x_rows = x_full.astype(F32)
-    h1_low = (x_rows * rms_scale(x_rows) * attn_full).astype(BF)
-    proj = dot(h1_low, w_mix)
-    pre_low = proj[:, : 3 * mix_width].astype(BF)
-    gate_raw = proj[:, 3 * mix_width : 4 * mix_width]
-    beta_logit = proj[:, 4 * mix_width : 4 * mix_width + heads]
-    pre_low, *out_parts = lax.optimization_barrier((pre_low, *out_parts))
+    x_scale = rms_scale(x_rows)
+    x_scale, *first_parts = lax.optimization_barrier((x_scale, *first_parts))
+    w_first = placed_shards(first_parts, "dp").reshape(width, first_rows.shape[2])
+    w_small = lax.optimization_barrier(w_first[:, 2 * mix_width :])
+    attn_full, ffn_full, norm_o_full, taps = read_small(
+        w_small, row_part, taps_part, gain_part, mix_width
+    )
+
+    h1_low = (x_rows * x_scale * attn_full).astype(BF)
+    first = dot(h1_low, w_first)
+    first, taps, *second_parts = lax.optimization_barrier((first, taps, *second_parts))
+    w_second = placed_shards(second_parts, "dp").reshape(width, 2 * mix_width)
+    second = dot(h1_low, w_second)
+    out_parts = head_owner_parts(after(w_out, *second_parts))
+    y_local, core, states, inverses = mix_forward(first, second, taps, norm_o_full)
+    y_local, d_out_full, gate_up_half, *out_parts = lax.optimization_barrier(
+        (y_local, d_out_full, gate_up_half, *out_parts)
+    )
+    gate_up_moved = gather_start(gate_up_half, "dp")
+    w_dn = placed_shards(down_parts, "dp").reshape(ff_local, width)
     w_out_own = placed_shards(out_parts, "dp").reshape(mix_width, width)
-    y_local, core, states, inverses = mix_forward(pre_low, gate_raw, beta_logit, taps, norm_o_full)
-    gate_up_parts = shards_of(gate_up_half, "dp")
     attn_part = dot(y_local, w_out_own).astype(BF)
-    attn_part, d_out_full = lax.optimization_barrier((attn_part, d_out_full))
     attn_sum = lax.psum_scatter(attn_part, "ctx", scatter_dimension=0, tiled=True)
 
     x_own = tokens[0].astype(F32)
-    attn_sum, *gate_up_parts[1:3] = lax.optimization_barrier((attn_sum, *gate_up_parts[1:3]))
+    w_mix = jnp.concatenate([w_first[:, : 2 * mix_width], w_second, w_small], axis=1)
+    attn_sum, gate_up_moved, w_dn, w_mix = lax.optimization_barrier(
+        (attn_sum, gate_up_moved, w_dn, w_mix)
+    )
     resid = x_own + attn_sum.astype(F32)
     resid_scale = rms_scale(resid)
     h2_own = (resid * resid_scale * ffn_full).astype(BF)
     h2_low = lax.all_gather(h2_own, "ctx", axis=0, tiled=True)
 
-    w_dn = placed_shards(down_parts, "dp").reshape(ff_local, width)
-    w_gu = placed_shards(gate_up_parts, "dp").reshape(width, 2 * ff_local)
+    w_gu = gather_end(gate_up_half, gate_up_moved, "dp").reshape(width, 2 * ff_local)
     gate_up = dot(h2_low, w_gu)
     gate, up = gate_up[:, :ff_local], gate_up[:, ff_local:]
     gate_sig = jax.nn.sigmoid(gate)
@@ -711,41 +839,39 @@
         h2_cols = lax.dynamic_slice_in_dim(h2_low, place * dp_rows, dp_rows, 1)
         return dot(h2_cols, d_gate_up_later, TN).astype(BF)
 
-    g_gate_up_parts = shard_parts(gate_up_part, "dp")
+    g_gate_up_sent, g_gate_up_kept = reduce_parts(gate_up_part, "dp")
     g_down_parts = shard_parts(down_part, "dp")
-    g_gate_up_parts = swapped_parts(g_gate_up_parts, "dp")
-    d_h2, out_part, *parts = lax.optimization_barrier(
-        (d_h2, out_part, *g_gate_up_parts[:2], *g_down_parts)
-    )
-    g_gate_up_parts[:2] = parts[:2]
-    g_down_parts = swapped_parts(parts[2:], "dp")
+    g_gate_up_moved = reduce_start(g_gate_up_sent, "dp")
+    d_h2, out_part, g_gate_up_moved, *g_down_parts = lax.optimization_barrier(
+        (d_h2, out_part, g_gate_up_moved, *g_down_parts)
+    )
+    g_down_parts = swapped_parts(g_down_parts, "dp")
 
     d_resid = d_out + norm_pull(resid, resid_scale, ffn_full, d_h2.astype(F32))
     d_attn = lax.all_gather(d_resid.astype(BF), "ctx", axis=0, tiled=True)
-    d_attn, *g_gate_up_parts = lax.optimization_barrier((d_attn, *g_gate_up_parts))
+    g_gate_up = reduce_end(g_gate_up_moved, g_gate_up_kept, "dp").astype(BF)
+    d_attn, g_gate_up = lax.optimization_barrier((d_attn, g_gate_up))
     out_sum = lax.psum_scatter(after(out_part, d_attn), "ctx", scatter_dimension=0, tiled=True)
     d_y = dot(d_attn, w_out_own, NT).astype(BF)
-    g_gate_up = total_of(g_gate_up_parts).astype(BF)
     g_gate_up = spread(g_gate_up.reshape(ctxs, row_part, 2 * ff_local), "ctx")
 
     d_proj, d_beta, g_taps, g_gain_o = mix_backward(
-        pre_low, gate_raw, beta_logit, d_y, core, states, inverses, taps, norm_o_full
+        first, second, d_y, core, states, inverses, taps, norm_o_full
     )
 
     def mix_part(place):
         h1_cols = lax.dynamic_slice_in_dim(h1_low, place * dp_rows, dp_rows, 1)
         return dot(h1_cols, d_proj, TN).astype(BF)
 
-    g_mix_parts = shard_parts(mix_part, "dp")
-    d_proj_later, *parts = lax.optimization_barrier(
-        (d_proj, *g_mix_parts[:-1], *g_down_parts)
-    )
-    g_mix_parts = swapped_parts(parts[: dps - 1] + g_mix_parts[-1:], "dp")
-    g_down_parts = parts[dps - 1 :]
+    g_mix_sent, g_mix_kept = reduce_parts(mix_part, "dp")
+    d_proj_later, g_mix_sent, *g_down_parts = lax.optimization_barrier(
+        (d_proj, g_mix_sent, *g_down_parts)
+    )
+    g_mix_moved = reduce_start(g_mix_sent, "dp")
     d_beta_low = jnp.pad(d_beta.astype(BF), ((0, 0), (0, 128 - heads)))
     d_h1_part = dot(jnp.concatenate([d_proj_later, d_beta_low], axis=1), w_mix, NT).astype(BF)
-    d_h1_part, out_sum, g_gate_up, *g_mix_parts[:2] = lax.optimization_barrier(
-        (d_h1_part, out_sum, g_gate_up, *g_mix_parts[:2])
+    d_h1_part, out_sum, g_gate_up, g_mix_moved = lax.optimization_barrier(
+        (d_h1_part, out_sum, g_gate_up, g_mix_moved)
     )
     block_out = (resid + out_sum.astype(F32)).astype(BF)[None]
     d_h1 = lax.psum_scatter(d_h1_part, "ctx", scatter_dimension=0, tiled=True).astype(F32)
@@ -772,17 +898,20 @@
         return lax.dynamic_index_in_dim(small_grad, place, 0, False)
 
     g_small = total_of(swapped_parts(shard_parts(small_part, "dp"), "dp")).astype(BF)
-    g_small = spread(g_small.reshape(ctxs, row_part, 128), "ctx")
-    g_out = dot(y_local, after(d_attn, *g_mix_parts[:2]), TN).astype(BF)
+    g_mix = reduce_end(g_mix_moved, g_mix_kept, "dp").astype(BF)
+    g_mix = jnp.concatenate([g_mix, g_small], axis=1)
+    g_out = dot(y_local, after(d_attn, g_mix), TN).astype(BF)
     g_w_out = total_of(row_owner_parts(g_out.reshape(dps, row_part, width)))
     g_w_down = total_of(g_down_parts)
 
     g_w_gate_up, ffn_sum = unpack_ff(g_gate_up, w_gate_up, dps)
     g_ffn_gain = ffn_sum[:, 0] / ffn_gain.astype(F32)
-    g_mix = total_of(g_mix_parts).astype(BF)
     g_mix = spread(g_mix.reshape(ctxs, row_part, g_mix.shape[1]), "ctx")
+    g_mix, d_tokens, g_w_gate_up, g_w_down, g_w_out = lax.optimization_barrier(
+        (g_mix, d_tokens, g_w_gate_up, g_w_down, g_w_out)
+    )
     g_w_qkv, g_w_gate_o, g_w_beta, small_sum, attn_row_sum = unpack_mix(
-        g_mix, g_small, w_qkv, w_gate_o, w_beta
+        g_mix, w_qkv, w_gate_o, w_beta
     )
     g_attn_gain = attn_row_sum[:, 0] / attn_gain.astype(F32)
     g_norm_gain_o = small_sum[:gain_part, heads]

time: 602 us -> 569 us (0.945)
  waiting for transfers between devices: 254 us -> 222 us
  matrix products: 98.8 us -> 86.3 us
  other arithmetic: 41.2 us -> 52.1 us
  starting transfers between devices: 70.3 us -> 76.6 us
    ppermute x21 -> x27, waiting for transfers between devices: 193 us -> 155 us  [swapped(): return lax.ppermute(value, axis, [(i, i ^ distance) for i in range(count)])]
    all_to_all x5, waiting for transfers between devices: 16.8 us -> 3.33 us  [spread(): return lax.all_to_all(value, axis, 0, 0, tiled=True)]
    all_gather x1, waiting for transfers between devices: 8.01 us -> 20.8 us  [per_device(): d_attn = lax.all_gather(d_resid.astype(BF), 'ctx', axis=0, tiled=True)]
    dot_general x22 -> x23, matrix products: 98.8 us -> 86.3 us  [dot(): lax.dot_general(left, right, (dims, ((), ())), preferred_element_type=F32)]
    reduce_scatter x1, waiting for transfers between devices: 14 us -> 26 us  [per_device(): lax.psum_scatter(attn_part, 'ctx', scatter_dimension=0, tiled=True)]
    another operation x0 -> x7, other arithmetic: none -> 9.65 us
    ppermute x21 -> x27, starting transfers between devices: 29.8 us -> 35.2 us  [swapped(): return lax.ppermute(value, axis, [(i, i ^ distance) for i in range(count)])]
    dynamic_update_slice x16 -> x24, local copies, waits for them, and re-layouts: 20.9 us -> 23.4 us  [placed(): whole = lax.dynamic_update_index_in_dim(whole, part, place, 0)]
  transfers between devices with their start and end apart: 42 -> 48, of which waited for: 25 -> 26; matrix products, arithmetic and copies ran while one was open for 25% -> 25% of each run, Pallas kernels for 7% -> 7%
where the time goes in v1:
time: 569 us; the launch traced here: 561 us
  waiting for transfers between devices  222 us (39%)
  matrix products  86.3 us (15%)
  starting transfers between devices  76.6 us (13%)
  local copies, waits for them, and re-layouts  64.7 us (11%)
  other arithmetic  52.1 us (9%)
  Pallas kernels  42.4 us (7%)
  between operations  16.6 us (3%)
    ppermute x27, waiting for transfers between devices, swapped(): return lax.ppermute(value, axis, [(i, i ^ distance) for i in range(count)])  155 us
    dot_general x23, matrix products, dot(): lax.dot_general(left, right, (dims, ((), ())), preferred_element_type=F32)  86.3 us
    ppermute x27, starting transfers between devices, swapped(): return lax.ppermute(value, axis, [(i, i ^ distance) for i in range(count)])  35.2 us
    reduce_scatter x1, waiting for transfers between devices, per_device(): lax.psum_scatter(attn_part, 'ctx', scatter_dimension=0, tiled=True)  26 us
    all_to_all x5, starting transfers between devices, spread(): return lax.all_to_all(value, axis, 0, 0, tiled=True)  24 us
    dynamic_update_slice x24, local copies, waits for them, and re-layouts, placed(): whole = lax.dynamic_update_index_in_dim(whole, part, place, 0)  23.4 us
    all_gather x1, waiting for transfers between devices, per_device(): d_attn = lax.all_gather(d_resid.astype(BF), 'ctx', axis=0, tiled=True)  20.8 us
    pallas_call x1, Pallas kernels, mix_backward(): pl.pallas_call(functools.partial(mix_backward_kernel, heads=heads, blocks...  19.2 us
  transfers between devices with their start and end apart: 48, of which 26 were waited for; matrix products, arithmetic and copies ran while one was open for 25% of the time, Pallas kernels for 7%

profile of v1, /device:TPU:0, one launch (start us, length us, event | category | flops | bytes accessed | tf_op | source)
XLA Modules:
  0.0 560.6 jit_solution(6356680475026772158)
XLA Ops:
  9.9 2.6 bitcast_convert_fusion
  19.7 6.3 %all-to-all-start = ((bf16[8,64,640]{2,1,0:T(8,128)(2,1)}), bf16[8,64,640]{2,1,0:T(8,128)(2,1)S(1)}, u32[]{:S(2)}, u32[]{:S(2)}) async-start(bf16[8,64,640]{2,1,0:T(8,128)(2,1)} %get-tuple-element.99), calls=%async_computation | async-start | bytes 1310720 | tf_op jit(solution)/shard_map/all_to_all | solution.py:715
  29.6 15.7 %collective-permute-done = bf16[176,2048]{1,0:T(8,128)(2,1)S(1)} collective-permute-done((bf16[176,2048]{1,0:T(8,128)(2,1)}, bf16[176,2048]{1,0:T(8,128)(2,1)S(1)}, u32[]{:S(2)}, u32[]{:S(2)}) %collective-permute-start) | collective-permute-done | bytes 720928 | tf_op jit(solution)/shard_map/ppermute | solution.py:595
  45.2 16.3 %collective-permute-done.1 = bf16[176,2048]{1,0:T(8,128)(2,1)S(1)} collective-permute-done((bf16[176,2048]{1,0:T(8,128)(2,1)}, bf16[176,2048]{1,0:T(8,128)(2,1)S(1)}, u32[]{:S(2)}, u32[]{:S(2)}) %collective-permute-start.1) | collective-permute-done | bytes 720928 | tf_op jit(solution)/shard_map/ppermute | solution.py:595
  62.5 4.6 all-to-all-start.1
  72.3 12.4 %collective-permute-done.3 = bf16[512,640]{1,0:T(8,128)(2,1)} collective-permute-done((bf16[512,640]{1,0:T(8,128)(2,1)S(1)}, bf16[512,640]{1,0:T(8,128)(2,1)}, u32[]{:S(2)}, u32[]{:S(2)}) %collective-permute-start.3) | collective-permute-done | bytes 655392 | tf_op jit(solution)/shard_map/ppermute | solution.py:595
  84.8 13.1 %collective-permute-done.4 = bf16[512,640]{1,0:T(8,128)(2,1)} collective-permute-done((bf16[512,640]{1,0:T(8,128)(2,1)S(1)}, bf16[512,640]{1,0:T(8,128)(2,1)}, u32[]{:S(2)}, u32[]{:S(2)}) %collective-permute-start.4) | collective-permute-done | bytes 655392 | tf_op jit(solution)/shard_map/ppermute | solution.py:595
  102.0 5.2 all-to-all-start.2
  107.3 3.2 fusion
  116.4 5.0 fusion.63.first_ref.first_before_ref
  121.4 2.7 collective-permute-done.7
  124.1 3.6 collective-permute-start.9
  129.2 3.5 collective-permute-start.12
  139.6 14.1 %mix_forward.1 = (bf16[1024,256]{1,0:T(8,128)(2,1)S(1)}, f32[1024,256]{1,0:T(8,128)S(1)}, f32[8,2,128,128]{3,2,1,0:T(8,128)S(1)}, f32[8,2,128,128]{3,2,1,0:T(8,128)S(1)}) custom-call(f32[1024,640]{1,0:T(8,128)} %fusion.63.first_ref.first_before_ref, f32[1024,512]{1,0:T(8,128)S(1)} %fusion.64.second_ref.second_before_ref, ...), custom_call_target="tpu_custom_call" | custom-call | flops 3019898880 | bytes 10485760 | tf_op jit(solution)/shard_map/mix_forward/pallas_call | solution.py:274
  162.6 3.4 convolution_convert_fusion.3
  167.6 2.8 slice_bitcast_fusion.9
  175.7 11.6 %collective-permute-done.13 = bf16[256,1408]{1,0:T(8,128)(2,1)S(1)} collective-permute-done((bf16[256,1408]{1,0:T(8,128)(2,1)S(1)}, bf16[256,1408]{1,0:T(8,128)(2,1)S(1)}, u32[]{:S(2)}, u32[]{:S(2)}) %collective-permute-start.13) | collective-permute-done | bytes 720928 | tf_op jit(solution)/shard_map/ppermute | solution.py:595
  188.9 26.0 %reduce-scatter.5.cloned.1.call-done = bf16[128,2048]{1,0:T(8,128)(2,1)} async-done(((bf16[1024,2048]{1,0:T(8,128)(2,1)}), bf16[128,2048]{1,0:T(8,128)(2,1)}) %reduce-scatter.5.cloned.1.call-update) | async-done | bytes 524304 | tf_op jit(solution)/shard_map/reduce_scatter | solution.py:804
  218.6 2.9 broadcast_in_dim.144
  233.1 21.9 %collective-permute-done.15 = bf16[2,256,1408]{2,1,0:T(8,128)(2,1)S(1)} collective-permute-done((bf16[2,256,1408]{2,1,0:T(8,128)(2,1)S(1)}, bf16[2,256,1408]{2,1,0:T(8,128)(2,1)S(1)}, u32[]{:S(2)}, u32[]{:S(2)}) %collective-permute-start.15) | collective-permute-done | bytes 1441824 | tf_op jit(solution)/shard_map/ppermute | solution.py:595
  255.9 3.8 collective-permute-done.16
  263.7 10.3 %fusion.65 = f32[1024,1408]{0,1:T(8,128)S(1)} fusion(bf16[1024,2048]{1,0:T(8,128)(2,1)} %all-gather.8.cloned.1.call-done, bf16[2048,1408]{1,0:T(8,128)(2,1)} %bitcast.38), kind=kOutput, calls=%fused_computation.178 | convolution fusion | flops 5905580032 | bytes 15728640 | tf_op jit(solution)/shard_map/dot_general | solution.py:586
  274.1 5.2 fusion.4
  280.8 10.9 %convolution_convert_fusion.2 = bf16[1024,2048]{1,0:T(8,128)(2,1)} fusion(bf16[2048,1408]{1,0:T(8,128)(2,1)} %bitcast.38, bf16[1024,704]{0,1:T(8,128)(2,1)S(1)} %get-tuple-element.249, bf16[1024,704]{0,1:T(8,128)(2,1)S(1)} %get-tuple-element.248), kind=kOutput, calls=%fused_computation.8 | convolution fusion | flops 5913444352 | bytes 12845056 | tf_op jit(solution)/shard_map/dot_general | solution.py:586
  315.6 5.2 convolution_convert_fusion.1
  320.8 14.9 %collective-permute-done.17 = bf16[2,256,1408]{2,1,0:T(8,128)(2,1)} collective-permute-done((bf16[2,256,1408]{2,1,0:T(8,128)(2,1)}, bf16[2,256,1408]{2,1,0:T(8,128)(2,1)}, u32[]{:S(2)}, u32[]{:S(2)}) %collective-permute-start.17) | collective-permute-done | bytes 1441824 | tf_op jit(solution)/shard_map/ppermute | solution.py:595
  335.7 4.4 collective-permute-done.18
  342.0 3.1 fusion.61
  351.2 4.3 convolution_convert_fusion.4
  355.5 7.9 %collective-permute-done.19 = bf16[256,1408]{1,0:T(8,128)(2,1)} collective-permute-done((bf16[256,1408]{1,0:T(8,128)(2,1)S(1)}, bf16[256,1408]{1,0:T(8,128)(2,1)}, u32[]{:S(2)}, u32[]{:S(2)}) %collective-permute-start.19) | collective-permute-done | bytes 720928 | tf_op jit(solution)/shard_map/ppermute | solution.py:595
  363.4 2.8 collective-permute-done.20
  369.7 20.8 %all-gather.10.cloned.1.call-done = bf16[1024,2048]{1,0:T(8,128)(2,1)} async-done(((bf16[128,2048]{1,0:T(8,128)(2,1)}), bf16[1024,2048]{1,0:T(8,128)(2,1)}) %all-gather.10.cloned.1.call-update) | async-done | bytes 4194320 | tf_op jit(solution)/shard_map/all_gather | solution.py:851
  394.1 3.6 all-to-all-start.3
  397.8 3.9 convolution_convert_fusion.18.dy_ref
  401.8 19.2 %mix_backward.1 = (bf16[1024,1024]{1,0:T(8,128)(2,1)}, f32[1024,2]{1,0:T(8,128)S(1)}, f32[8,768]{1,0:T(8,128)S(1)}, f32[8,128]{1,0:T(8,128)S(1)}) custom-call(f32[1024,640]{1,0:T(8,128)} %fusion.63.first_ref.first_before_ref, f32[1024,512]{1,0:T(8,128)} %copy-done, f32[1024,640]{1,0:T(8,128)} %fusion.63.first_ref.first_before_ref, f32[1024,512]{1,0:T(8,128)} %copy-done, ...), custom_call_target="tpu_custom_call" | custom-call | flops 3019898880 | bytes 10485760 | tf_op jit(solution)/shard_map/mix_backward/pallas_call | solution.py:323
  421.0 3.1 convolution_convert_fusion.16
  432.3 7.4 %convolution_convert_fusion = bf16[1024,2048]{1,0:T(8,128)(2,1)} fusion(bf16[2048,1152]{1,0:T(8,128)(2,1)S(1)} %bitcast.202, bf16[1024,128]{1,0:T(8,128)(2,1)S(1)} %pad.12, bf16[1024,1024]{1,0:T(8,128)(2,1)S(1)} %copy-done.34), kind=kOutput, calls=%fused_computation.6 | convolution fusion | flops 4838653952 | bytes 11272192 | tf_op jit(solution)/shard_map/dot_general | solution.py:586
  439.8 14.6 %collective-permute-done.24 = bf16[2,256,1024]{2,1,0:T(8,128)(2,1)} collective-permute-done((bf16[2,256,1024]{2,1,0:T(8,128)(2,1)}, bf16[2,256,1024]{2,1,0:T(8,128)(2,1)}, u32[]{:S(2)}, u32[]{:S(2)}) %collective-permute-start.24) | collective-permute-done | bytes 1048608 | tf_op jit(solution)/shard_map/ppermute | solution.py:595
  457.7 10.4 %reduce-scatter.9.cloned.1.call-done = bf16[128,2048]{1,0:T(8,128)(2,1)} async-done(((bf16[1024,2048]{1,0:T(8,128)(2,1)}), bf16[128,2048]{1,0:T(8,128)(2,1)}) %reduce-scatter.9.cloned.1.call-update) | async-done | bytes 524304 | tf_op jit(solution)/shard_map/reduce_scatter | solution.py:854
  483.8 3.7 fusion.7
  499.0 9.8 %collective-permute-done.26 = bf16[256,1024]{1,0:T(8,128)(2,1)S(1)} collective-permute-done((bf16[256,1024]{1,0:T(8,128)(2,1)S(1)}, bf16[256,1024]{1,0:T(8,128)(2,1)S(1)}, u32[]{:S(2)}, u32[]{:S(2)}) %collective-permute-start.26) | collective-permute-done | bytes 524320 | tf_op jit(solution)/shard_map/ppermute | solution.py:595
  512.6 4.3 all-to-all-start.4
  516.9 3.5 convolution_convert_fusion.8
  523.1 3.6 collective-permute-start.32
  529.1 3.1 convert_add_fusion.5
  535.2 3.5 collective-permute-done.31
  542.3 4.0 fusion.21
  547.3 3.2 unpack_mix.1
  (344 shorter events, 172.8 us)
Async XLA Ops:
  7.2 100.1 %all-gather.12.cloned.1.call-start = ((), (), s32[]{:S(2)}) async-start(), calls=%async_computation.16 | async-start | bytes 4718592 | tf_op jit(solution)/shard_map/all_gather | solution.py:761
  7.9 149.6 %all-gather.6.cloned.1.call-start = ((), (), s32[]{:S(2)}) async-start(), calls=%async_computation.9 | async-start | bytes 4718592 | tf_op jit(solution)/shard_map/all_gather | solution.py:767
  19.7 42.8 %all-to-all-start = ((bf16[8,64,640]{2,1,0:T(8,128)(2,1)}), bf16[8,64,640]{2,1,0:T(8,128)(2,1)S(1)}, u32[]{:S(2)}, u32[]{:S(2)}) async-start(bf16[8,64,640]{2,1,0:T(8,128)(2,1)} %get-tuple-element.99), calls=%async_computation | async-start | bytes 1310720 | tf_op jit(solution)/shard_map/all_to_all | solution.py:715
  26.1 19.1 %collective-permute-start = (bf16[176,2048]{1,0:T(8,128)(2,1)}, bf16[176,2048]{1,0:T(8,128)(2,1)S(1)}, u32[]{:S(2)}, u32[]{:S(2)}) collective-permute-start(bf16[176,2048]{1,0:T(8,128)(2,1)} %param.27), channel_id=1, source_target_pairs={{0,8},{8,0},{16,24},{24,16},{1,9},{9,1},{17,25},{25,17},{2,10},{10... | collective-permute-start | bytes 2162696 | tf_op jit(solution)/shard_map/ppermute | solution.py:595
  27.6 33.9 %collective-permute-start.1 = (bf16[176,2048]{1,0:T(8,128)(2,1)}, bf16[176,2048]{1,0:T(8,128)(2,1)S(1)}, u32[]{:S(2)}, u32[]{:S(2)}) collective-permute-start(bf16[176,2048]{1,0:T(8,128)(2,1)} %param.27), channel_id=1, source_target_pairs={{0,16},{8,24},{16,0},{24,8},{1,17},{9,25},{17,1},{25,9},{2,18},{10... | collective-permute-start | bytes 2162696 | tf_op jit(solution)/shard_map/ppermute | solution.py:595
  29.1 33.3 %collective-permute-start.2 = (bf16[176,2048]{1,0:T(8,128)(2,1)}, bf16[176,2048]{1,0:T(8,128)(2,1)S(1)}, u32[]{:S(2)}, u32[]{:S(2)}) collective-permute-start(bf16[176,2048]{1,0:T(8,128)(2,1)} %param.27), channel_id=1, source_target_pairs={{0,24},{8,16},{16,8},{24,0},{1,25},{9,17},{17,9},{25,1},{2,26},{10... | collective-permute-start | bytes 2162696 | tf_op jit(solution)/shard_map/ppermute | solution.py:595
  62.5 35.4 %all-to-all-start.1 = ((bf16[8,64,512]{2,1,0:T(8,128)(2,1)}), bf16[8,64,512]{2,1,0:T(8,128)(2,1)}, u32[]{:S(2)}, u32[]{:S(2)}) async-start(bf16[8,64,512]{2,1,0:T(8,128)(2,1)} %get-tuple-element.102), calls=%async_computation.1 | async-start | bytes 1048576 | tf_op jit(solution)/shard_map/all_to_all | solution.py:715
  67.1 17.6 %collective-permute-start.3 = (bf16[512,640]{1,0:T(8,128)(2,1)S(1)}, bf16[512,640]{1,0:T(8,128)(2,1)}, u32[]{:S(2)}, u32[]{:S(2)}) collective-permute-start(bf16[512,640]{1,0:T(8,128)(2,1)S(1)} %bitcast.211), channel_id=1, source_target_pairs={{0,8},{8,0},{16,24},{24,16},{1,9},{9,1},{17,25},{25,17},{2,10},{10... | collective-permute-start | bytes 1966088 | tf_op jit(solution)/shard_map/ppermute | solution.py:595
  68.2 29.7 %collective-permute-start.4 = (bf16[512,640]{1,0:T(8,128)(2,1)S(1)}, bf16[512,640]{1,0:T(8,128)(2,1)}, u32[]{:S(2)}, u32[]{:S(2)}) collective-permute-start(bf16[512,640]{1,0:T(8,128)(2,1)S(1)} %bitcast.212), channel_id=1, source_target_pairs={{0,16},{8,24},{16,0},{24,8},{1,17},{9,25},{17,1},{25,9},{2,18},{10... | collective-permute-start | bytes 1966088 | tf_op jit(solution)/shard_map/ppermute | solution.py:595
  69.7 40.8 %collective-permute-start.5 = (bf16[512,640]{1,0:T(8,128)(2,1)S(1)}, bf16[512,640]{1,0:T(8,128)(2,1)}, u32[]{:S(2)}, u32[]{:S(2)}) collective-permute-start(bf16[512,640]{1,0:T(8,128)(2,1)S(1)} %bitcast.213), channel_id=1, source_target_pairs={{0,24},{8,16},{16,8},{24,0},{1,25},{9,17},{17,9},{25,1},{2,26},{10... | collective-permute-start | bytes 1966088 | tf_op jit(solution)/shard_map/ppermute | solution.py:595
  97.9 23.4 %collective-permute-start.6 = (bf16[512,512]{1,0:T(8,128)(2,1)}, bf16[512,512]{1,0:T(8,128)(2,1)}, u32[]{:S(2)}, u32[]{:S(2)}) collective-permute-start(bf16[512,512]{1,0:T(8,128)(2,1)} %bitcast.7), channel_id=1, source_target_pairs={{0,8},{8,0},{16,24},{24,16},{1,9},{9,1},{17,25},{25,17},{2,10},{10... | collective-permute-start | bytes 1572872 | tf_op jit(solution)/shard_map/ppermute | solution.py:595
  99.2 24.9 %collective-permute-start.7 = (bf16[512,512]{1,0:T(8,128)(2,1)}, bf16[512,512]{1,0:T(8,128)(2,1)}, u32[]{:S(2)}, u32[]{:S(2)}) collective-permute-start(bf16[512,512]{1,0:T(8,128)(2,1)} %bitcast.7), channel_id=1, source_target_pairs={{0,16},{8,24},{16,0},{24,8},{1,17},{9,25},{17,1},{25,9},{2,18},{10... | collective-permute-start | bytes 1572872 | tf_op jit(solution)/shard_map/ppermute | solution.py:595
  101.7 22.3 %collective-permute-start.8 = (bf16[512,512]{1,0:T(8,128)(2,1)}, bf16[512,512]{1,0:T(8,128)(2,1)}, u32[]{:S(2)}, u32[]{:S(2)}) collective-permute-start(bf16[512,512]{1,0:T(8,128)(2,1)} %bitcast.7), channel_id=1, source_target_pairs={{0,24},{8,16},{16,8},{24,0},{1,25},{9,17},{17,9},{25,1},{2,26},{10... | collective-permute-start | bytes 1572872 | tf_op jit(solution)/shard_map/ppermute | solution.py:595
  102.0 55.5 %all-to-all-start.2 = ((bf16[8,64,1408]{2,1,0:T(8,128)(2,1)}), bf16[8,64,1408]{2,1,0:T(8,128)(2,1)}, u32[]{:S(2)}, u32[]{:S(2)}) async-start(bf16[8,64,1408]{2,1,0:T(8,128)(2,1)} %pack_ff.1), calls=%async_computation.2 | async-start | bytes 2883584 | tf_op jit(solution)/shard_map/all_to_all | solution.py:715
  107.2 107.7 %reduce-scatter.5.cloned.1.call-start = ((), (), s32[]{:S(2)}) async-start(), calls=%async_computation.10 | async-start | bytes 4718592 | tf_op jit(solution)/shard_map/reduce_scatter | solution.py:804
  124.1 33.5 %collective-permute-start.9 = (bf16[64,2048]{1,0:T(8,128)(2,1)}, bf16[64,2048]{1,0:T(8,128)(2,1)}, u32[]{:S(2)}, u32[]{:S(2)}) collective-permute-start(bf16[64,2048]{1,0:T(8,128)(2,1)} %param.24), channel_id=1, source_target_pairs={{0,0},{1,8},{2,2},{3,10},{4,4},{5,12},{6,6},{7,14},{8,16},{9,24},{... | collective-permute-start | bytes 786440 | tf_op jit(solution)/shard_map/ppermute | solution.py:701
  127.6 29.9 %collective-permute-start.10 = (bf16[64,2048]{1,0:T(8,128)(2,1)}, bf16[64,2048]{1,0:T(8,128)(2,1)}, u32[]{:S(2)}, u32[]{:S(2)}) collective-permute-start(bf16[64,2048]{1,0:T(8,128)(2,1)} %param.24), channel_id=1, source_target_pairs={{0,8},{1,0},{2,10},{3,2},{4,12},{5,4},{6,14},{7,6},{8,24},{9,16},{... | collective-permute-start | bytes 786440 | tf_op jit(solution)/shard_map/ppermute | solution.py:701
  129.2 28.3 %collective-permute-start.11 = (bf16[64,2048]{1,0:T(8,128)(2,1)}, bf16[64,2048]{1,0:T(8,128)(2,1)}, u32[]{:S(2)}, u32[]{:S(2)}) collective-permute-start(bf16[64,2048]{1,0:T(8,128)(2,1)} %param.24), channel_id=1, source_target_pairs={{0,16},{1,24},{2,18},{3,26},{4,20},{5,28},{6,22},{7,30},{8,0},{9,8... | collective-permute-start | bytes 786440 | tf_op jit(solution)/shard_map/ppermute | solution.py:701
  129.2 28.4 %collective-permute-start.12 = (bf16[64,2048]{1,0:T(8,128)(2,1)}, bf16[64,2048]{1,0:T(8,128)(2,1)}, u32[]{:S(2)}, u32[]{:S(2)}) collective-permute-start(bf16[64,2048]{1,0:T(8,128)(2,1)} %param.24), channel_id=1, source_target_pairs={{0,24},{1,16},{2,26},{3,18},{4,28},{5,20},{6,30},{7,22},{8,8},{9,0... | collective-permute-start | bytes 786440 | tf_op jit(solution)/shard_map/ppermute | solution.py:701
  166.0 97.7 %all-gather.8.cloned.1.call-start = ((), (), s32[]{:S(2)}) async-start(), calls=%async_computation.11 | async-start | bytes 4718592 | tf_op jit(solution)/shard_map/all_gather | solution.py:814
  170.4 17.0 %collective-permute-start.13 = (bf16[256,1408]{1,0:T(8,128)(2,1)S(1)}, bf16[256,1408]{1,0:T(8,128)(2,1)S(1)}, u32[]{:S(2)}, u32[]{:S(2)}) collective-permute-start(bf16[256,1408]{1,0:T(8,128)(2,1)S(1)} %get-tuple-element.258), channel_id=1, source_target_pairs={{0,8},{8,0},{16,24},{24,16},{1,9},{9,1},{17,25},{25,17},{2,10},{10... | collective-permute-start | bytes 2162696 | tf_op jit(solution)/shard_map/ppermute | solution.py:595
  172.6 16.3 %collective-permute-start.14 = (bf16[256,1408]{1,0:T(8,128)(2,1)S(1)}, bf16[256,1408]{1,0:T(8,128)(2,1)}, u32[]{:S(2)}, u32[]{:S(2)}) collective-permute-start(bf16[256,1408]{1,0:T(8,128)(2,1)S(1)} %get-tuple-element.257), channel_id=1, source_target_pairs={{0,16},{8,24},{16,0},{24,8},{1,17},{9,25},{17,1},{25,9},{2,18},{10... | collective-permute-start | bytes 2162696 | tf_op jit(solution)/shard_map/ppermute | solution.py:595
  218.3 122.3 %reduce-scatter.7.cloned.1.call-start = ((), (), s32[]{:S(2)}) async-start(), calls=%async_computation.12 | async-start | bytes 4718592 | tf_op jit(solution)/shard_map/reduce_scatter | solution.py:830
  223.8 31.2 %collective-permute-start.15 = (bf16[2,256,1408]{2,1,0:T(8,128)(2,1)S(1)}, bf16[2,256,1408]{2,1,0:T(8,128)(2,1)S(1)}, u32[]{:S(2)}, u32[]{:S(2)}) collective-permute-start(bf16[2,256,1408]{2,1,0:T(8,128)(2,1)S(1)} %pad_maximum_fusion.2), channel_id=1, source_target_pairs={{0,16},{8,24},{16,0},{24,8},{1,17},{9,25},{17,1},{25,9},{2,18},{10... | collective-permute-start | bytes 4325384 | tf_op jit(solution)/shard_map/ppermute | solution.py:595
  228.5 31.2 %collective-permute-start.16 = (bf16[2,256,1408]{2,1,0:T(8,128)(2,1)S(1)}, bf16[2,256,1408]{2,1,0:T(8,128)(2,1)S(1)}, u32[]{:S(2)}, u32[]{:S(2)}) collective-permute-start(bf16[2,256,1408]{2,1,0:T(8,128)(2,1)S(1)} %pad_maximum_fusion.3), channel_id=1, source_target_pairs={{0,8},{8,0},{16,24},{24,16},{1,9},{9,1},{17,25},{25,17},{2,10},{10... | collective-permute-start | bytes 4325384 | tf_op jit(solution)/shard_map/ppermute | solution.py:595
  291.7 98.8 %all-gather.10.cloned.1.call-start = ((), (), s32[]{:S(2)}) async-start(), calls=%async_computation.13 | async-start | bytes 4718592 | tf_op jit(solution)/shard_map/all_gather | solution.py:851
  301.6 34.0 %collective-permute-start.17 = (bf16[2,256,1408]{2,1,0:T(8,128)(2,1)}, bf16[2,256,1408]{2,1,0:T(8,128)(2,1)}, u32[]{:S(2)}, u32[]{:S(2)}) collective-permute-start(bf16[2,256,1408]{2,1,0:T(8,128)(2,1)} %pad_maximum_fusion.4), channel_id=1, source_target_pairs={{0,8},{8,0},{16,24},{24,16},{1,9},{9,1},{17,25},{25,17},{2,10},{10... | collective-permute-start | bytes 4325384 | tf_op jit(solution)/shard_map/ppermute | solution.py:595
  306.3 33.8 %collective-permute-start.18 = (bf16[2,256,1408]{2,1,0:T(8,128)(2,1)}, bf16[2,256,1408]{2,1,0:T(8,128)(2,1)}, u32[]{:S(2)}, u32[]{:S(2)}) collective-permute-start(bf16[2,256,1408]{2,1,0:T(8,128)(2,1)} %pad_maximum_fusion.5), channel_id=1, source_target_pairs={{0,16},{8,24},{16,0},{24,8},{1,17},{9,25},{17,1},{25,9},{2,18},{10... | collective-permute-start | bytes 4325384 | tf_op jit(solution)/shard_map/ppermute | solution.py:595
  345.1 123.0 %reduce-scatter.9.cloned.1.call-start = ((), (), s32[]{:S(2)}) async-start(), calls=%async_computation.14 | async-start | bytes 4718592 | tf_op jit(solution)/shard_map/reduce_scatter | solution.py:854
  346.6 16.8 %collective-permute-start.19 = (bf16[256,1408]{1,0:T(8,128)(2,1)S(1)}, bf16[256,1408]{1,0:T(8,128)(2,1)}, u32[]{:S(2)}, u32[]{:S(2)}) collective-permute-start(bf16[256,1408]{1,0:T(8,128)(2,1)S(1)} %fusion.14), channel_id=1, source_target_pairs={{0,16},{8,24},{16,0},{24,8},{1,17},{9,25},{17,1},{25,9},{2,18},{10... | collective-permute-start | bytes 2162696 | tf_op jit(solution)/shard_map/ppermute | solution.py:595
  349.7 16.5 %collective-permute-start.20 = (bf16[256,1408]{1,0:T(8,128)(2,1)S(1)}, bf16[256,1408]{1,0:T(8,128)(2,1)}, u32[]{:S(2)}, u32[]{:S(2)}) collective-permute-start(bf16[256,1408]{1,0:T(8,128)(2,1)S(1)} %fusion.11), channel_id=1, source_target_pairs={{0,8},{8,0},{16,24},{24,16},{1,9},{9,1},{17,25},{25,17},{2,10},{10... | collective-permute-start | bytes 2162696 | tf_op jit(solution)/shard_map/ppermute | solution.py:595
  390.6 37.9 %collective-permute-start.21 = (bf16[176,2048]{1,0:T(8,128)(2,1)}, bf16[176,2048]{1,0:T(8,128)(2,1)}, u32[]{:S(2)}, u32[]{:S(2)}) collective-permute-start(bf16[176,2048]{1,0:T(8,128)(2,1)} %convolution_convert_fusion.12), channel_id=1, source_target_pairs={{0,8},{8,0},{16,24},{24,16},{1,9},{9,1},{17,25},{25,17},{2,10},{10... | collective-permute-start | bytes 2162696 | tf_op jit(solution)/shard_map/ppermute | solution.py:595
  392.1 36.4 %collective-permute-start.22 = (bf16[176,2048]{1,0:T(8,128)(2,1)}, bf16[176,2048]{1,0:T(8,128)(2,1)}, u32[]{:S(2)}, u32[]{:S(2)}) collective-permute-start(bf16[176,2048]{1,0:T(8,128)(2,1)} %convolution_convert_fusion.11), channel_id=1, source_target_pairs={{0,16},{8,24},{16,0},{24,8},{1,17},{9,25},{17,1},{25,9},{2,18},{10... | collective-permute-start | bytes 2162696 | tf_op jit(solution)/shard_map/ppermute | solution.py:595
  393.6 34.9 %collective-permute-start.23 = (bf16[176,2048]{1,0:T(8,128)(2,1)}, bf16[176,2048]{1,0:T(8,128)(2,1)}, u32[]{:S(2)}, u32[]{:S(2)}) collective-permute-start(bf16[176,2048]{1,0:T(8,128)(2,1)} %convolution_convert_fusion.10), channel_id=1, source_target_pairs={{0,24},{8,16},{16,8},{24,0},{1,25},{9,17},{17,9},{25,1},{2,26},{10... | collective-permute-start | bytes 2162696 | tf_op jit(solution)/shard_map/ppermute | solution.py:595
  394.1 63.6 %all-to-all-start.3 = ((bf16[8,64,1408]{2,1,0:T(8,128)(2,1)}), bf16[8,64,1408]{2,1,0:T(8,128)(2,1)S(1)}, u32[]{:S(2)}, u32[]{:S(2)}) async-start(bf16[8,64,1408]{2,1,0:T(8,128)(2,1)} %bitcast.200), calls=%async_computation.6 | async-start | bytes 2883584 | tf_op jit(solution)/shard_map/all_to_all | solution.py:715
  397.7 143.1 %reduce-scatter.11.cloned.1.call-start = ((), (), s32[]{:S(2)}) async-start(), calls=%async_computation.15 | async-start | bytes 4718592 | tf_op jit(solution)/shard_map/reduce_scatter | solution.py:877
  428.5 25.9 %collective-permute-start.24 = (bf16[2,256,1024]{2,1,0:T(8,128)(2,1)}, bf16[2,256,1024]{2,1,0:T(8,128)(2,1)}, u32[]{:S(2)}, u32[]{:S(2)}) collective-permute-start(bf16[2,256,1024]{2,1,0:T(8,128)(2,1)} %get-tuple-element.160), channel_id=1, source_target_pairs={{0,8},{8,0},{16,24},{24,16},{1,9},{9,1},{17,25},{25,17},{2,10},{10... | collective-permute-start | bytes 3145736 | tf_op jit(solution)/shard_map/ppermute | solution.py:595
  430.0 25.5 %collective-permute-start.25 = (bf16[2,256,1024]{2,1,0:T(8,128)(2,1)}, bf16[2,256,1024]{2,1,0:T(8,128)(2,1)}, u32[]{:S(2)}, u32[]{:S(2)}) collective-permute-start(bf16[2,256,1024]{2,1,0:T(8,128)(2,1)} %get-tuple-element.161), channel_id=1, source_target_pairs={{0,16},{8,24},{16,0},{24,8},{1,17},{9,25},{17,1},{25,9},{2,18},{10... | collective-permute-start | bytes 3145736 | tf_op jit(solution)/shard_map/ppermute | solution.py:595
  487.5 11.4 %collective-permute-start.30 = (bf16[512,128]{1,0:T(8,128)(2,1)S(1)}, bf16[512,128]{1,0:T(8,128)(2,1)S(1)}, u32[]{:S(2)}, u32[]{:S(2)}) collective-permute-start(bf16[512,128]{1,0:T(8,128)(2,1)S(1)} %get-tuple-element.270), channel_id=1, source_target_pairs={{0,24},{8,16},{16,8},{24,0},{1,25},{9,17},{17,9},{25,1},{2,26},{10... | collective-permute-start | bytes 393224 | tf_op jit(solution)/shard_map/ppermute | solution.py:595
  489.7 9.2 %collective-permute-start.29 = (bf16[512,128]{1,0:T(8,128)(2,1)S(1)}, bf16[512,128]{1,0:T(8,128)(2,1)S(1)}, u32[]{:S(2)}, u32[]{:S(2)}) collective-permute-start(bf16[512,128]{1,0:T(8,128)(2,1)S(1)} %get-tuple-element.271), channel_id=1, source_target_pairs={{0,16},{8,24},{16,0},{24,8},{1,17},{9,25},{17,1},{25,9},{2,18},{10... | collective-permute-start | bytes 393224 | tf_op jit(solution)/shard_map/ppermute | solution.py:595
  490.3 8.7 %collective-permute-start.28 = (bf16[512,128]{1,0:T(8,128)(2,1)S(1)}, bf16[512,128]{1,0:T(8,128)(2,1)S(1)}, u32[]{:S(2)}, u32[]{:S(2)}) collective-permute-start(bf16[512,128]{1,0:T(8,128)(2,1)S(1)} %get-tuple-element.269), channel_id=1, source_target_pairs={{0,8},{8,0},{16,24},{24,16},{1,9},{9,1},{17,25},{25,17},{2,10},{10... | collective-permute-start | bytes 393224 | tf_op jit(solution)/shard_map/ppermute | solution.py:595
  492.3 16.5 %collective-permute-start.26 = (bf16[256,1024]{1,0:T(8,128)(2,1)S(1)}, bf16[256,1024]{1,0:T(8,128)(2,1)S(1)}, u32[]{:S(2)}, u32[]{:S(2)}) collective-permute-start(bf16[256,1024]{1,0:T(8,128)(2,1)S(1)} %fusion.25), channel_id=1, source_target_pairs={{0,16},{8,24},{16,0},{24,8},{1,17},{9,25},{17,1},{25,9},{2,18},{10... | collective-permute-start | bytes 1572872 | tf_op jit(solution)/shard_map/ppermute | solution.py:595
  494.9 14.8 %collective-permute-start.27 = (bf16[256,1024]{1,0:T(8,128)(2,1)S(1)}, bf16[256,1024]{1,0:T(8,128)(2,1)S(1)}, u32[]{:S(2)}, u32[]{:S(2)}) collective-permute-start(bf16[256,1024]{1,0:T(8,128)(2,1)S(1)} %fusion.22), channel_id=1, source_target_pairs={{0,8},{8,0},{16,24},{24,16},{1,9},{9,1},{17,25},{25,17},{2,10},{10... | collective-permute-start | bytes 1572872 | tf_op jit(solution)/shard_map/ppermute | solution.py:595
  512.6 34.7 %all-to-all-start.4 = ((bf16[8,64,1152]{2,1,0:T(8,128)(2,1)}), bf16[8,64,1152]{2,1,0:T(8,128)(2,1)}, u32[]{:S(2)}, u32[]{:S(2)}) async-start(bf16[8,64,1152]{2,1,0:T(8,128)(2,1)} %bitcast.203), calls=%async_computation.7 | async-start | bytes 2359296 | tf_op jit(solution)/shard_map/all_to_all | solution.py:715
  521.4 13.8 %collective-permute-start.34 = (bf16[64,2048]{1,0:T(8,128)(2,1)}, bf16[64,2048]{1,0:T(8,128)(2,1)}, u32[]{:S(2)}, u32[]{:S(2)}) collective-permute-start(bf16[64,2048]{1,0:T(8,128)(2,1)} %get-tuple-element.260), channel_id=1, source_target_pairs={{16,0},{24,1},{18,2},{26,3},{20,4},{28,5},{22,6},{30,7},{0,8},{8,9... | collective-permute-start | bytes 786440 | tf_op jit(solution)/shard_map/ppermute | solution.py:710
  523.0 12.1 %collective-permute-start.33 = (bf16[64,2048]{1,0:T(8,128)(2,1)}, bf16[64,2048]{1,0:T(8,128)(2,1)}, u32[]{:S(2)}, u32[]{:S(2)}) collective-permute-start(bf16[64,2048]{1,0:T(8,128)(2,1)} %get-tuple-element.261), channel_id=1, source_target_pairs={{8,0},{0,1},{10,2},{2,3},{12,4},{4,5},{14,6},{6,7},{24,8},{16,9},{... | collective-permute-start | bytes 786440 | tf_op jit(solution)/shard_map/ppermute | solution.py:710
  523.1 12.0 %collective-permute-start.32 = (bf16[64,2048]{1,0:T(8,128)(2,1)}, bf16[64,2048]{1,0:T(8,128)(2,1)}, u32[]{:S(2)}, u32[]{:S(2)}) collective-permute-start(bf16[64,2048]{1,0:T(8,128)(2,1)} %get-tuple-element.262), channel_id=1, source_target_pairs={{0,0},{8,1},{2,2},{10,3},{4,4},{12,5},{6,6},{14,7},{16,8},{24,9},{... | collective-permute-start | bytes 786440 | tf_op jit(solution)/shard_map/ppermute | solution.py:710
  526.7 12.0 %collective-permute-start.31 = (bf16[64,2048]{1,0:T(8,128)(2,1)}, bf16[64,2048]{1,0:T(8,128)(2,1)}, u32[]{:S(2)}, u32[]{:S(2)}) collective-permute-start(bf16[64,2048]{1,0:T(8,128)(2,1)} %get-tuple-element.259), channel_id=1, source_target_pairs={{24,0},{16,1},{26,2},{18,3},{28,4},{20,5},{30,6},{22,7},{8,8},{0,9... | collective-permute-start | bytes 786440 | tf_op jit(solution)/shard_map/ppermute | solution.py:710
  (79 other events, 804.3 us)
Sparse Core Ops, SparseCore 0:
  9.6 65.1 all-gather.11
  77.0 61.7 all-gather.5
  166.1 48.7 reduce-scatter.4
  218.4 45.2 all-gather.7
  291.9 48.7 reduce-scatter.6
  345.2 45.2 all-gather.9
  392.8 75.2 reduce-scatter.8
  470.4 52.8 reduce-scatter.10

commit v2 on v1

--- a/solution.py
+++ b/solution.py
@@ -13,6 +13,7 @@
 CHUNK = 128
 STEP = 512
 SMALL = 64
+FF_STEP = 256
 EPS = 1e-05
 KEY_EPS = 1e-06
 BF = jnp.bfloat16
@@ -288,9 +289,9 @@
         ],
         out_shape=[
             jax.ShapeDtypeStruct((extent, width), BF),
-            jax.ShapeDtypeStruct((extent, width), F32),
-            jax.ShapeDtypeStruct((extent // CHUNK, heads, HD, HD), F32),
-            jax.ShapeDtypeStruct((extent // CHUNK, heads, CHUNK, CHUNK), F32),
+            pltpu.HBM((extent, width), F32),
+            pltpu.HBM((extent // CHUNK, heads, HD, HD), F32),
+            pltpu.HBM((extent // CHUNK, heads, CHUNK, CHUNK), F32),
         ],
         scratch_shapes=[pltpu.VMEM((heads, HD, HD), F32), pltpu.VMEM((8, 3 * width), F32)],
         compiler_params=pltpu.CompilerParams(
@@ -582,6 +583,56 @@
     )(received, w_gate_up)
 
 
+def gate_up_kernel(h2_ref, dhidden_ref, weight_ref, hidden_ref, dgate_up_ref, dh2_ref):
+    half = hidden_ref.shape[1]
+    weight = weight_ref[...]
+    gate_up = lax.dot_general(h2_ref[...], weight, (NN, ((), ())), preferred_element_type=F32)
+    gate, up = gate_up[:, :half], gate_up[:, half:]
+    gate_sig = sigmoid(gate)
+    gate_act = gate * gate_sig
+    dhidden = dhidden_ref[...].astype(F32)
+    hidden_ref[...] = (gate_act * up).astype(BF)
+    dgate = dhidden * up * (gate_sig * (1.0 + gate * (1.0 - gate_sig)))
+    dgate_up = jnp.concatenate([dgate, dhidden * gate_act], axis=1).astype(BF)
+    dgate_up_ref[...] = dgate_up
+    dh2_ref[...] = lax.dot_general(
+        dgate_up, weight, (NT, ((), ())), preferred_element_type=F32
+    ).astype(BF)
+
+
+def gate_up_both_ways(h2_low, d_hidden, w_gu):
+    extent, width = h2_low.shape
+    cols = w_gu.shape[1]
+    half = cols // 2
+    step = min(FF_STEP, extent)
+
+    def rows(size):
+        return pl.BlockSpec((step, size), lambda i: (i, 0))
+
+    return pl.pallas_call(
+        gate_up_kernel,
+        grid=(extent // step,),
+        in_specs=[
+            rows(width),
+            rows(half),
+            pl.BlockSpec((width, cols), lambda i: (0, 0), pipeline_mode=pl.Buffered(1)),
+        ],
+        out_specs=[rows(half), rows(cols), rows(width)],
+        out_shape=[
+            jax.ShapeDtypeStruct((extent, half), BF),
+            jax.ShapeDtypeStruct((extent, cols), BF),
+            jax.ShapeDtypeStruct((extent, width), BF),
+        ],
+        compiler_params=pltpu.CompilerParams(
+            dimension_semantics=("arbitrary",), vmem_limit_bytes=52 * 1024 * 1024
+        ),
+        cost_estimate=pl.CostEstimate(
+            flops=4 * extent * width * cols, bytes_accessed=6 * extent * width, transcendentals=0
+        ),
+        name="gate_up_both_ways",
+    )(h2_low, d_hidden, w_gu)
+
+
 def dot(left, right, dims=NN):
     return lax.dot_general(left, right, (dims, ((), ())), preferred_element_type=F32)
 
@@ -759,28 +810,33 @@
     head_dims = (HD // row_part, heads, ctxs * row_part // HD)
 
     x_full = lax.all_gather(tokens[0], "ctx", axis=0, tiled=True)
+    first_rows, second_rows = pack_mix(
+        w_qkv, w_gate_o, w_beta, attn_gain, ffn_gain, norm_gain_o, conv_weight, ctxs
+    )
     matches = group_ids[:, None] == lax.broadcasted_iota(
         jnp.int32, (group_ids.shape[0], group_scale.shape[0]), 1
     )
     seq_scale = jnp.sum(jnp.where(matches, group_scale[None, :], 0.0), axis=1)
-    d_out = cotangent[0].astype(F32) * seq_scale[0]
+    d_out = after(cotangent[0], first_rows).astype(F32) * seq_scale[0]
     d_out_full = lax.all_gather(after(d_out.astype(BF), x_full), "ctx", axis=0, tiled=True)
-    first_rows, second_rows = pack_mix(
-        w_qkv, w_gate_o, w_beta, attn_gain, ffn_gain, norm_gain_o, conv_weight, ctxs
-    )
     first_half = spread(first_rows, "ctx").reshape(dp_rows, first_rows.shape[2])
     down_parts = shards_of(w_down, "dp")
+    out_parts = head_owner_parts(after(w_out, *down_parts[1:3]))
     first_half, *down_parts = lax.optimization_barrier((first_half, *down_parts))
     second_half = spread(after(second_rows, first_half), "ctx").reshape(dp_rows, 2 * mix_width)
     first_parts = shards_of(first_half, "dp")
-    second_half, *first_parts[1:3] = lax.optimization_barrier((second_half, *first_parts[1:3]))
+    second_half, *parts = lax.optimization_barrier((second_half, *first_parts[1:3], *out_parts))
+    first_parts[1:3], out_parts = parts[:2], parts[2:]
     second_parts = shards_of(second_half, "dp")
     gate_up_rows = pack_ff(w_gate_up, ctxs, dps)
     gate_up_half = spread(after(gate_up_rows, second_half), "ctx").reshape(dp_rows, 2 * ff_local)
 
     x_rows = x_full.astype(F32)
     x_scale = rms_scale(x_rows)
-    x_scale, *first_parts = lax.optimization_barrier((x_scale, *first_parts))
+    w_out_own = placed_shards(out_parts, "dp").reshape(mix_width, width)
+    x_scale, w_out_own, *first_parts = lax.optimization_barrier(
+        (x_scale, w_out_own, *first_parts)
+    )
     w_first = placed_shards(first_parts, "dp").reshape(width, first_rows.shape[2])
     w_small = lax.optimization_barrier(w_first[:, 2 * mix_width :])
     attn_full, ffn_full, norm_o_full, taps = read_small(
@@ -792,14 +848,12 @@
     first, taps, *second_parts = lax.optimization_barrier((first, taps, *second_parts))
     w_second = placed_shards(second_parts, "dp").reshape(width, 2 * mix_width)
     second = dot(h1_low, w_second)
-    out_parts = head_owner_parts(after(w_out, *second_parts))
     y_local, core, states, inverses = mix_forward(first, second, taps, norm_o_full)
-    y_local, d_out_full, gate_up_half, *out_parts = lax.optimization_barrier(
-        (y_local, d_out_full, gate_up_half, *out_parts)
+    y_local, d_out_full, gate_up_half = lax.optimization_barrier(
+        (y_local, d_out_full, gate_up_half)
     )
     gate_up_moved = gather_start(gate_up_half, "dp")
     w_dn = placed_shards(down_parts, "dp").reshape(ff_local, width)
-    w_out_own = placed_shards(out_parts, "dp").reshape(mix_width, width)
     attn_part = dot(y_local, w_out_own).astype(BF)
     attn_sum = lax.psum_scatter(attn_part, "ctx", scatter_dimension=0, tiled=True)
 
@@ -814,19 +868,9 @@
     h2_low = lax.all_gather(h2_own, "ctx", axis=0, tiled=True)
 
     w_gu = gather_end(gate_up_half, gate_up_moved, "dp").reshape(width, 2 * ff_local)
-    gate_up = dot(h2_low, w_gu)
-    gate, up = gate_up[:, :ff_local], gate_up[:, ff_local:]
-    gate_sig = jax.nn.sigmoid(gate)
-    hidden_low = (gate * gate_sig * up).astype(BF)
-    d_hidden = dot(d_out_full, w_dn, NT).astype(BF).astype(F32)
-    d_gate_up = jnp.concatenate(
-        [
-            (d_hidden * up * (gate_sig * (1.0 + gate * (1.0 - gate_sig)))).astype(BF),
-            (d_hidden * (gate * gate_sig)).astype(BF),
-        ],
-        axis=1,
-    )
-    d_h2_part = dot(d_gate_up, w_gu, NT).astype(BF)
+    d_hidden = dot(d_out_full, w_dn, NT).astype(BF)
+    h2_low, d_hidden = lax.optimization_barrier((h2_low, d_hidden))
+    hidden_low, d_gate_up, d_h2_part = gate_up_both_ways(h2_low, d_hidden, w_gu)
     d_h2 = lax.psum_scatter(d_h2_part, "ctx", scatter_dimension=0, tiled=True)
     hidden_later, d_gate_up_later = lax.optimization_barrier((hidden_low, d_gate_up, d_h2_part))[:2]
     out_part = dot(hidden_later, w_dn).astype(BF)
@@ -842,15 +886,15 @@
     g_gate_up_sent, g_gate_up_kept = reduce_parts(gate_up_part, "dp")
     g_down_parts = shard_parts(down_part, "dp")
     g_gate_up_moved = reduce_start(g_gate_up_sent, "dp")
-    d_h2, out_part, g_gate_up_moved, *g_down_parts = lax.optimization_barrier(
-        (d_h2, out_part, g_gate_up_moved, *g_down_parts)
-    )
-    g_down_parts = swapped_parts(g_down_parts, "dp")
+    d_h2, g_gate_up_moved = lax.optimization_barrier((d_h2, g_gate_up_moved))
 
     d_resid = d_out + norm_pull(resid, resid_scale, ffn_full, d_h2.astype(F32))
     d_attn = lax.all_gather(d_resid.astype(BF), "ctx", axis=0, tiled=True)
     g_gate_up = reduce_end(g_gate_up_moved, g_gate_up_kept, "dp").astype(BF)
-    d_attn, g_gate_up = lax.optimization_barrier((d_attn, g_gate_up))
+    g_down_moved = swapped_parts(g_down_parts, "dp")
+    d_attn, g_gate_up, out_part, *g_down_moved[:2] = lax.optimization_barrier(
+        (d_attn, g_gate_up, out_part, *g_down_moved[:2])
+    )
     out_sum = lax.psum_scatter(after(out_part, d_attn), "ctx", scatter_dimension=0, tiled=True)
     d_y = dot(d_attn, w_out_own, NT).astype(BF)
     g_gate_up = spread(g_gate_up.reshape(ctxs, row_part, 2 * ff_local), "ctx")
@@ -864,19 +908,12 @@
         return dot(h1_cols, d_proj, TN).astype(BF)
 
     g_mix_sent, g_mix_kept = reduce_parts(mix_part, "dp")
-    d_proj_later, g_mix_sent, *g_down_parts = lax.optimization_barrier(
-        (d_proj, g_mix_sent, *g_down_parts)
+    d_proj_later, g_mix_sent, d_beta, g_taps, g_gain_o, d_attn_later = lax.optimization_barrier(
+        (d_proj, g_mix_sent, d_beta, g_taps, g_gain_o, d_attn)
     )
     g_mix_moved = reduce_start(g_mix_sent, "dp")
     d_beta_low = jnp.pad(d_beta.astype(BF), ((0, 0), (0, 128 - heads)))
     d_h1_part = dot(jnp.concatenate([d_proj_later, d_beta_low], axis=1), w_mix, NT).astype(BF)
-    d_h1_part, out_sum, g_gate_up, g_mix_moved = lax.optimization_barrier(
-        (d_h1_part, out_sum, g_gate_up, g_mix_moved)
-    )
-    block_out = (resid + out_sum.astype(F32)).astype(BF)[None]
-    d_h1 = lax.psum_scatter(d_h1_part, "ctx", scatter_dimension=0, tiled=True).astype(F32)
-    d_tokens = (d_resid + norm_pull(x_own, rms_scale(x_own), attn_full, d_h1))[None]
-
     taps_grad = jnp.zeros((ctxs, CONV, 3 * mix_width), F32)
     taps_grad = lax.dynamic_update_index_in_dim(taps_grad, g_taps[:CONV], ctx_place, 0)
     taps_grad = (
@@ -894,15 +931,23 @@
     small_grad = (small_grad + dot(h1_low, d_beta_low, TN)).astype(BF)
     small_grad = small_grad.reshape(dps, dp_rows, 128)
 
+    g_out = dot(y_local, d_attn_later, TN).astype(BF)
+    g_out_parts = row_owner_parts(g_out.reshape(dps, row_part, width))
+    d_h1_part, out_sum, g_gate_up, g_mix_moved, small_grad, *g_out_parts = lax.optimization_barrier(
+        (d_h1_part, out_sum, g_gate_up, g_mix_moved, small_grad, *g_out_parts)
+    )
+    block_out = (resid + out_sum.astype(F32)).astype(BF)[None]
+    d_h1 = lax.psum_scatter(d_h1_part, "ctx", scatter_dimension=0, tiled=True).astype(F32)
+    d_tokens = (d_resid + norm_pull(x_own, rms_scale(x_own), attn_full, d_h1))[None]
+
     def small_part(place):
         return lax.dynamic_index_in_dim(small_grad, place, 0, False)
 
     g_small = total_of(swapped_parts(shard_parts(small_part, "dp"), "dp")).astype(BF)
     g_mix = reduce_end(g_mix_moved, g_mix_kept, "dp").astype(BF)
     g_mix = jnp.concatenate([g_mix, g_small], axis=1)
-    g_out = dot(y_local, after(d_attn, g_mix), TN).astype(BF)
-    g_w_out = total_of(row_owner_parts(g_out.reshape(dps, row_part, width)))
-    g_w_down = total_of(g_down_parts)
+    g_w_out = total_of(g_out_parts)
+    g_w_down = total_of(g_down_moved)
 
     g_w_gate_up, ffn_sum = unpack_ff(g_gate_up, w_gate_up, dps)
     g_ffn_gain = ffn_sum[:, 0] / ffn_gain.astype(F32)

time: 569 us -> 556 us (0.977)
  waiting for transfers between devices: 222 us -> 202 us
  Pallas kernels: 42.4 us -> 59 us
  starting transfers between devices: 76.6 us -> 87.6 us
  matrix products: 86.3 us -> 76.1 us
  local copies, waits for them, and re-layouts: 64.7 us -> 56.5 us
    ppermute x27, waiting for transfers between devices: 155 us -> 131 us  [swapped(): return lax.ppermute(value, axis, [(i, i ^ distance) for i in range(count)])]
    all_gather x1, waiting for transfers between devices: 20.8 us -> 1.86 us  [per_device(): d_attn = lax.all_gather(d_resid.astype(BF), 'ctx', axis=0, tiled=True)]
    pallas_call x0 -> x1, Pallas kernels: none -> 18.9 us  [gate_up_both_ways(): pl.pallas_call(gate_up_kernel, grid=(extent // step,), in_specs=[rows(wid...]
    all_to_all x5, waiting for transfers between devices: 3.33 us -> 21.7 us  [spread(): return lax.all_to_all(value, axis, 0, 0, tiled=True)]
    ppermute x27, starting transfers between devices: 35.2 us -> 46.8 us  [swapped(): return lax.ppermute(value, axis, [(i, i ^ distance) for i in range(count)])]
    reduce_scatter x1, waiting for transfers between devices: 10.4 us -> 0.01 us  [per_device(): lax.psum_scatter(after(out_part, d_attn), 'ctx', scatter_dimension=0, til...]
    dot_general x23 -> x21, matrix products: 86.3 us -> 76.1 us  [dot(): lax.dot_general(left, right, (dims, ((), ())), preferred_element_type=F32)]
    reduce_scatter x1, waiting for transfers between devices: 0.01 us -> 6.99 us  [per_device(): lax.psum_scatter(d_h1_part, 'ctx', scatter_dimension=0, tiled=True)]
  transfers between devices with their start and end apart: 48 -> 48, of which waited for: 26 -> 23; matrix products, arithmetic and copies ran while one was open for 25% -> 28% of each run, Pallas kernels for 7% -> 7%
where the time goes in v2:
time: 556 us; the launch traced here: 545 us
  waiting for transfers between devices  202 us (36%)
  starting transfers between devices  87.6 us (16%)
  matrix products  76.1 us (14%)
  Pallas kernels  59 us (11%)
  local copies, waits for them, and re-layouts  56.5 us (10%)
  other arithmetic  47.3 us (9%)
  between operations  16.5 us (3%)
    ppermute x27, waiting for transfers between devices, swapped(): return lax.ppermute(value, axis, [(i, i ^ distance) for i in range(count)])  131 us
    dot_general x21, matrix products, dot(): lax.dot_general(left, right, (dims, ((), ())), preferred_element_type=F32)  76.1 us
    ppermute x27, starting transfers between devices, swapped(): return lax.ppermute(value, axis, [(i, i ^ distance) for i in range(count)])  46.8 us
    reduce_scatter x1, waiting for transfers between devices, per_device(): lax.psum_scatter(attn_part, 'ctx', scatter_dimension=0, tiled=True)  25 us
    all_to_all x5, starting transfers between devices, spread(): return lax.all_to_all(value, axis, 0, 0, tiled=True)  23.9 us
    all_to_all x5, waiting for transfers between devices, spread(): return lax.all_to_all(value, axis, 0, 0, tiled=True)  21.7 us
    dynamic_update_slice x24, local copies, waits for them, and re-layouts, placed(): whole = lax.dynamic_update_index_in_dim(whole, part, place, 0)  21.4 us
    pallas_call x1, Pallas kernels, mix_backward(): pl.pallas_call(functools.partial(mix_backward_kernel, heads=heads, blocks...  19.2 us
  transfers between devices with their start and end apart: 48, of which 23 were waited for; matrix products, arithmetic and copies ran while one was open for 28% of the time, Pallas kernels for 7%

profile of v2, /device:TPU:0, one launch (start us, length us, event | category | flops | bytes accessed | tf_op | source)
XLA Modules:
  0.0 544.9 jit_solution(11421794776596161270)
XLA Ops:
  15.3 6.3 %all-to-all-start = ((bf16[8,64,640]{2,1,0:T(8,128)(2,1)}), bf16[8,64,640]{2,1,0:T(8,128)(2,1)S(1)}, u32[]{:S(2)}, u32[]{:S(2)}) async-start(bf16[8,64,640]{2,1,0:T(8,128)(2,1)} %get-tuple-element.111), calls=%async_computation | async-start | bytes 1310720 | tf_op jit(solution)/shard_map/all_to_all | solution.py:766
  27.0 13.7 %collective-permute-done = bf16[176,2048]{1,0:T(8,128)(2,1)S(1)} collective-permute-done((bf16[176,2048]{1,0:T(8,128)(2,1)}, bf16[176,2048]{1,0:T(8,128)(2,1)S(1)}, u32[]{:S(2)}, u32[]{:S(2)}) %collective-permute-start) | collective-permute-done | bytes 720928 | tf_op jit(solution)/shard_map/ppermute | solution.py:646
  40.8 16.3 %collective-permute-done.1 = bf16[176,2048]{1,0:T(8,128)(2,1)S(1)} collective-permute-done((bf16[176,2048]{1,0:T(8,128)(2,1)}, bf16[176,2048]{1,0:T(8,128)(2,1)S(1)}, u32[]{:S(2)}, u32[]{:S(2)}) %collective-permute-start.1) | collective-permute-done | bytes 720928 | tf_op jit(solution)/shard_map/ppermute | solution.py:646
  57.1 3.6 collective-permute-start.5
  62.1 4.7 all-to-all-start.1
  75.2 6.8 %collective-permute-done.6 = bf16[64,2048]{1,0:T(8,128)(2,1)S(1)} collective-permute-done((bf16[64,2048]{1,0:T(8,128)(2,1)}, bf16[64,2048]{1,0:T(8,128)(2,1)S(1)}, u32[]{:S(2)}, u32[]{:S(2)}) %collective-permute-start.6) | collective-permute-done | bytes 262176 | tf_op jit(solution)/shard_map/ppermute | solution.py:752
  81.9 14.7 %collective-permute-start.9 = (bf16[512,640]{1,0:T(8,128)(2,1)S(1)}, bf16[512,640]{1,0:T(8,128)(2,1)S(1)}, u32[]{:S(2)}, u32[]{:S(2)}) collective-permute-start(bf16[512,640]{1,0:T(8,128)(2,1)S(1)} %bitcast.205), channel_id=1, source_target_pairs={{0,24},{8,16},{16,8},{24,0},{1,25},{9,17},{17,9},{25,1},{2,26},{10... | collective-permute-start | bytes 1966088 | tf_op jit(solution)/shard_map/ppermute | solution.py:646
  97.3 2.9 collective-permute-start.12
  103.3 4.3 all-to-all-start.2
  107.7 3.1 fusion
  117.1 3.4 fusion.61.first_ref.first_before_ref
  120.5 3.6 collective-permute-done.12
  131.0 13.0 %mix_forward.1 = (bf16[1024,256]{1,0:T(8,128)(2,1)S(1)}, f32[1024,256]{1,0:T(8,128)}, f32[8,2,128,128]{3,2,1,0:T(8,128)}, f32[8,2,128,128]{3,2,1,0:T(8,128)}) custom-call(f32[1024,640]{1,0:T(8,128)S(1)} %fusion.61.first_ref.first_before_ref, f32[1024,512]{1,0:T(8,128)S(1)} %fusion.62.second_ref.second_before_ref, f32[8,768]{1,0:T(8,128)S(1)} %get-tuple-element.134.taps_ref, ...), custom_call_target="tpu_custom_call" | custom-call | flops 3019898880 | bytes 10485760 | tf_op jit(solution)/shard_map/mix_forward/pallas_call | solution.py:275
  146.1 10.8 %all-to-all-done.2 = bf16[8,64,1408]{2,1,0:T(8,128)(2,1)} async-done(((bf16[8,64,1408]{2,1,0:T(8,128)(2,1)}), bf16[8,64,1408]{2,1,0:T(8,128)(2,1)}, u32[]{:S(2)}, u32[]{:S(2)}) %all-to-all-start.2) | async-done | bytes 1441824 | tf_op jit(solution)/shard_map/all_to_all | solution.py:766
  156.9 4.7 convolution_convert_fusion.2
  163.2 2.8 slice_bitcast_fusion.9
  172.0 11.9 %collective-permute-done.13 = bf16[256,1408]{1,0:T(8,128)(2,1)S(1)} collective-permute-done((bf16[256,1408]{1,0:T(8,128)(2,1)S(1)}, bf16[256,1408]{1,0:T(8,128)(2,1)S(1)}, u32[]{:S(2)}, u32[]{:S(2)}) %collective-permute-start.13) | collective-permute-done | bytes 720928 | tf_op jit(solution)/shard_map/ppermute | solution.py:646
  185.4 25.0 %reduce-scatter.5.cloned.1.call-done = bf16[128,2048]{1,0:T(8,128)(2,1)} async-done(((bf16[1024,2048]{1,0:T(8,128)(2,1)}), bf16[128,2048]{1,0:T(8,128)(2,1)}) %reduce-scatter.5.cloned.1.call-update) | async-done | bytes 524304 | tf_op jit(solution)/shard_map/reduce_scatter | solution.py:858
  213.9 2.9 broadcast_in_dim.144
  228.6 5.0 convolution_convert_fusion.12.dhidden_ref
  233.6 18.8 %collective-permute-done.15 = bf16[2,256,1408]{2,1,0:T(8,128)(2,1)S(1)} collective-permute-done((bf16[2,256,1408]{2,1,0:T(8,128)(2,1)S(1)}, bf16[2,256,1408]{2,1,0:T(8,128)(2,1)S(1)}, u32[]{:S(2)}, u32[]{:S(2)}) %collective-permute-start.15) | collective-permute-done | bytes 1441824 | tf_op jit(solution)/shard_map/ppermute | solution.py:646
  259.2 18.9 %gate_up_both_ways.1 = (bf16[1024,704]{1,0:T(8,128)(2,1)S(1)}, bf16[1024,1408]{1,0:T(8,128)(2,1)}, bf16[1024,2048]{1,0:T(8,128)(2,1)}) custom-call(bf16[1024,2048]{1,0:T(8,128)(2,1)} %all-gather.8.cloned.1.call-done.h2_ref, bf16[1024,704]{1,0:T(8,128)(2,1)} %convolution_convert_fusion.12.dhidden_ref, bf16[2048,1408]{1,0:T(8,128)(2,1)} %bitcast.38.weight_ref), custom_call_target="tpu_custom_call" | custom-call | flops 11811160064 | bytes 12582912 | tf_op jit(solution)/shard_map/gate_up_both_ways/pallas_call | solution.py:612
  278.3 4.1 convolution_convert_fusion.5
  282.4 3.8 convolution_convert_fusion.6
  293.8 27.7 %collective-permute-done.17 = bf16[2,256,1408]{2,1,0:T(8,128)(2,1)S(1)} collective-permute-done((bf16[2,256,1408]{2,1,0:T(8,128)(2,1)S(1)}, bf16[2,256,1408]{2,1,0:T(8,128)(2,1)S(1)}, u32[]{:S(2)}, u32[]{:S(2)}) %collective-permute-start.17) | collective-permute-done | bytes 1441824 | tf_op jit(solution)/shard_map/ppermute | solution.py:646
  322.6 3.5 collective-permute-done.18
  328.5 3.1 fusion.59
  331.8 4.3 convolution_convert_fusion.11
  341.0 4.2 convolution_convert_fusion.3
  349.9 5.0 convolution_convert_fusion.1
  354.9 16.6 %collective-permute-done.19 = bf16[256,1408]{1,0:T(8,128)(2,1)} collective-permute-done((bf16[256,1408]{1,0:T(8,128)(2,1)}, bf16[256,1408]{1,0:T(8,128)(2,1)}, u32[]{:S(2)}, u32[]{:S(2)}) %collective-permute-start.19) | collective-permute-done | bytes 720928 | tf_op jit(solution)/shard_map/ppermute | solution.py:646
  377.6 3.6 convolution_convert_fusion.17.dy_ref
  381.3 19.2 %mix_backward.1 = (bf16[1024,1024]{1,0:T(8,128)(2,1)}, f32[1024,2]{1,0:T(8,128)S(1)}, f32[8,768]{1,0:T(8,128)S(1)}, f32[8,128]{1,0:T(8,128)S(1)}) custom-call(f32[1024,640]{1,0:T(8,128)} %copy-done, f32[1024,512]{1,0:T(8,128)} %copy-done.1, f32[1024,640]{1,0:T(8,128)} %copy-done, f32[1024,512]{1,0:T(8,128)} %copy-done.1, ...), custom_call_target="tpu_custom_call" | custom-call | flops 3019898880 | bytes 10485760 | tf_op jit(solution)/shard_map/mix_backward/pallas_call | solution.py:324
  400.5 3.1 convolution_convert_fusion.16
  409.5 3.6 all-to-all-start.3
  416.1 3.5 convolution_convert_fusion.7
  420.6 3.6 collective-permute-start.25
  426.2 9.5 %convolution_convert_fusion = bf16[1024,2048]{1,0:T(8,128)(2,1)} fusion(bf16[2048,1152]{1,0:T(8,128)(2,1)} %pad_maximum_fusion, bf16[1024,128]{1,0:T(8,128)(2,1)S(1)} %copy-done.73, bf16[1024,1024]{1,0:T(8,128)(2,1)S(1)} %copy-done.32), kind=kOutput, calls=%fused_computation.6 | convolution fusion | flops 4838653952 | bytes 11272192 | tf_op jit(solution)/shard_map/dot_general | solution.py:637
  448.9 4.3 fusion.4
  453.2 5.3 collective-permute-done.28
  459.3 4.2 convolution_convert_fusion.8
  478.0 9.3 %collective-permute-done.29 = bf16[256,1024]{1,0:T(8,128)(2,1)S(1)} collective-permute-done((bf16[256,1024]{1,0:T(8,128)(2,1)S(1)}, bf16[256,1024]{1,0:T(8,128)(2,1)S(1)}, u32[]{:S(2)}, u32[]{:S(2)}) %collective-permute-start.29) | collective-permute-done | bytes 524320 | tf_op jit(solution)/shard_map/ppermute | solution.py:646
  490.4 4.9 all-to-all-start.4
  495.3 5.6 %collective-permute-done.34 = bf16[176,2048]{1,0:T(8,128)(2,1)S(1)} collective-permute-done((bf16[176,2048]{1,0:T(8,128)(2,1)}, bf16[176,2048]{1,0:T(8,128)(2,1)S(1)}, u32[]{:S(2)}, u32[]{:S(2)}) %collective-permute-start.34) | collective-permute-done | bytes 720928 | tf_op jit(solution)/shard_map/ppermute | solution.py:646
  500.9 3.3 convert_add_fusion.5
  509.2 7.0 %reduce-scatter.11.cloned.1.call-done = bf16[128,2048]{1,0:T(8,128)(2,1)} async-done(((bf16[1024,2048]{1,0:T(8,128)(2,1)}), bf16[128,2048]{1,0:T(8,128)(2,1)}) %reduce-scatter.11.cloned.1.call-update) | async-done | bytes 524304 | tf_op jit(solution)/shard_map/reduce_scatter | solution.py:940
  517.7 4.3 fusion.18
  522.0 10.9 %all-to-all-done.4.in_ref = bf16[8,64,1152]{2,1,0:T(8,128)(2,1)S(1)} async-done(((bf16[8,64,1152]{2,1,0:T(8,128)(2,1)}), bf16[8,64,1152]{2,1,0:T(8,128)(2,1)S(1)}, u32[]{:S(2)}, u32[]{:S(2)}) %all-to-all-start.4) | async-done | bytes 1179680 | tf_op jit(solution)/shard_map/all_to_all | solution.py:766
  (349 shorter events, 153.7 us)
Async XLA Ops:
  7.2 100.5 %all-gather.12.cloned.1.call-start = ((), (), s32[]{:S(2)}) async-start(), calls=%async_computation.16 | async-start | bytes 4718592 | tf_op jit(solution)/shard_map/all_gather | solution.py:812
  15.3 45.4 %all-to-all-start = ((bf16[8,64,640]{2,1,0:T(8,128)(2,1)}), bf16[8,64,640]{2,1,0:T(8,128)(2,1)S(1)}, u32[]{:S(2)}, u32[]{:S(2)}) async-start(bf16[8,64,640]{2,1,0:T(8,128)(2,1)} %get-tuple-element.111), calls=%async_computation | async-start | bytes 1310720 | tf_op jit(solution)/shard_map/all_to_all | solution.py:766
  21.6 19.1 %collective-permute-start = (bf16[176,2048]{1,0:T(8,128)(2,1)}, bf16[176,2048]{1,0:T(8,128)(2,1)S(1)}, u32[]{:S(2)}, u32[]{:S(2)}) collective-permute-start(bf16[176,2048]{1,0:T(8,128)(2,1)} %param.27), channel_id=1, source_target_pairs={{0,8},{8,0},{16,24},{24,16},{1,9},{9,1},{17,25},{25,17},{2,10},{10... | collective-permute-start | bytes 2162696 | tf_op jit(solution)/shard_map/ppermute | solution.py:646
  23.1 33.9 %collective-permute-start.1 = (bf16[176,2048]{1,0:T(8,128)(2,1)}, bf16[176,2048]{1,0:T(8,128)(2,1)S(1)}, u32[]{:S(2)}, u32[]{:S(2)}) collective-permute-start(bf16[176,2048]{1,0:T(8,128)(2,1)} %param.27), channel_id=1, source_target_pairs={{0,16},{8,24},{16,0},{24,8},{1,17},{9,25},{17,1},{25,9},{2,18},{10... | collective-permute-start | bytes 2162696 | tf_op jit(solution)/shard_map/ppermute | solution.py:646
  24.6 36.0 %collective-permute-start.2 = (bf16[176,2048]{1,0:T(8,128)(2,1)}, bf16[176,2048]{1,0:T(8,128)(2,1)S(1)}, u32[]{:S(2)}, u32[]{:S(2)}) collective-permute-start(bf16[176,2048]{1,0:T(8,128)(2,1)} %param.27), channel_id=1, source_target_pairs={{0,24},{8,16},{16,8},{24,0},{1,25},{9,17},{17,9},{25,1},{2,26},{10... | collective-permute-start | bytes 2162696 | tf_op jit(solution)/shard_map/ppermute | solution.py:646
  57.1 13.7 %collective-permute-start.5 = (bf16[64,2048]{1,0:T(8,128)(2,1)}, bf16[64,2048]{1,0:T(8,128)(2,1)}, u32[]{:S(2)}, u32[]{:S(2)}) collective-permute-start(bf16[64,2048]{1,0:T(8,128)(2,1)} %param.24), channel_id=1, source_target_pairs={{0,0},{1,8},{2,2},{3,10},{4,4},{5,12},{6,6},{7,14},{8,16},{9,24},{... | collective-permute-start | bytes 786440 | tf_op jit(solution)/shard_map/ppermute | solution.py:752
  60.7 36.0 %collective-permute-start.3 = (bf16[512,640]{1,0:T(8,128)(2,1)S(1)}, bf16[512,640]{1,0:T(8,128)(2,1)}, u32[]{:S(2)}, u32[]{:S(2)}) collective-permute-start(bf16[512,640]{1,0:T(8,128)(2,1)S(1)} %bitcast.203), channel_id=1, source_target_pairs={{0,8},{8,0},{16,24},{24,16},{1,9},{9,1},{17,25},{25,17},{2,10},{10... | collective-permute-start | bytes 1966088 | tf_op jit(solution)/shard_map/ppermute | solution.py:646
  62.1 34.6 %collective-permute-start.4 = (bf16[512,640]{1,0:T(8,128)(2,1)S(1)}, bf16[512,640]{1,0:T(8,128)(2,1)}, u32[]{:S(2)}, u32[]{:S(2)}) collective-permute-start(bf16[512,640]{1,0:T(8,128)(2,1)S(1)} %bitcast.204), channel_id=1, source_target_pairs={{0,16},{8,24},{16,0},{24,8},{1,17},{9,25},{17,1},{25,9},{2,18},{10... | collective-permute-start | bytes 1966088 | tf_op jit(solution)/shard_map/ppermute | solution.py:646
  62.1 34.6 %all-to-all-start.1 = ((bf16[8,64,512]{2,1,0:T(8,128)(2,1)}), bf16[8,64,512]{2,1,0:T(8,128)(2,1)}, u32[]{:S(2)}, u32[]{:S(2)}) async-start(bf16[8,64,512]{2,1,0:T(8,128)(2,1)} %get-tuple-element.113), calls=%async_computation.1 | async-start | bytes 1048576 | tf_op jit(solution)/shard_map/all_to_all | solution.py:766
  66.8 90.1 %all-gather.6.cloned.1.call-start = ((), (), s32[]{:S(2)}) async-start(), calls=%async_computation.9 | async-start | bytes 4718592 | tf_op jit(solution)/shard_map/all_gather | solution.py:821
  68.4 13.5 %collective-permute-start.6 = (bf16[64,2048]{1,0:T(8,128)(2,1)}, bf16[64,2048]{1,0:T(8,128)(2,1)S(1)}, u32[]{:S(2)}, u32[]{:S(2)}) collective-permute-start(bf16[64,2048]{1,0:T(8,128)(2,1)} %param.24), channel_id=1, source_target_pairs={{0,8},{1,0},{2,10},{3,2},{4,12},{5,4},{6,14},{7,6},{8,24},{9,16},{... | collective-permute-start | bytes 786440 | tf_op jit(solution)/shard_map/ppermute | solution.py:752
  69.2 27.5 %collective-permute-start.7 = (bf16[64,2048]{1,0:T(8,128)(2,1)}, bf16[64,2048]{1,0:T(8,128)(2,1)}, u32[]{:S(2)}, u32[]{:S(2)}) collective-permute-start(bf16[64,2048]{1,0:T(8,128)(2,1)} %param.24), channel_id=1, source_target_pairs={{0,16},{1,24},{2,18},{3,26},{4,20},{5,28},{6,22},{7,30},{8,0},{9,8... | collective-permute-start | bytes 786440 | tf_op jit(solution)/shard_map/ppermute | solution.py:752
  70.7 25.9 %collective-permute-start.8 = (bf16[64,2048]{1,0:T(8,128)(2,1)}, bf16[64,2048]{1,0:T(8,128)(2,1)}, u32[]{:S(2)}, u32[]{:S(2)}) collective-permute-start(bf16[64,2048]{1,0:T(8,128)(2,1)} %param.24), channel_id=1, source_target_pairs={{0,24},{1,16},{2,26},{3,18},{4,28},{5,20},{6,30},{7,22},{8,8},{9,0... | collective-permute-start | bytes 786440 | tf_op jit(solution)/shard_map/ppermute | solution.py:752
  81.9 30.4 %collective-permute-start.9 = (bf16[512,640]{1,0:T(8,128)(2,1)S(1)}, bf16[512,640]{1,0:T(8,128)(2,1)S(1)}, u32[]{:S(2)}, u32[]{:S(2)}) collective-permute-start(bf16[512,640]{1,0:T(8,128)(2,1)S(1)} %bitcast.205), channel_id=1, source_target_pairs={{0,24},{8,16},{16,8},{24,0},{1,25},{9,17},{17,9},{25,1},{2,26},{10... | collective-permute-start | bytes 1966088 | tf_op jit(solution)/shard_map/ppermute | solution.py:646
  96.7 23.8 %collective-permute-start.10 = (bf16[512,512]{1,0:T(8,128)(2,1)}, bf16[512,512]{1,0:T(8,128)(2,1)}, u32[]{:S(2)}, u32[]{:S(2)}) collective-permute-start(bf16[512,512]{1,0:T(8,128)(2,1)} %bitcast.7), channel_id=1, source_target_pairs={{0,8},{8,0},{16,24},{24,16},{1,9},{9,1},{17,25},{25,17},{2,10},{10... | collective-permute-start | bytes 1572872 | tf_op jit(solution)/shard_map/ppermute | solution.py:646
  96.8 23.7 %collective-permute-start.11 = (bf16[512,512]{1,0:T(8,128)(2,1)}, bf16[512,512]{1,0:T(8,128)(2,1)}, u32[]{:S(2)}, u32[]{:S(2)}) collective-permute-start(bf16[512,512]{1,0:T(8,128)(2,1)} %bitcast.7), channel_id=1, source_target_pairs={{0,16},{8,24},{16,0},{24,8},{1,17},{9,25},{17,1},{25,9},{2,18},{10... | collective-permute-start | bytes 1572872 | tf_op jit(solution)/shard_map/ppermute | solution.py:646
  97.3 26.8 %collective-permute-start.12 = (bf16[512,512]{1,0:T(8,128)(2,1)}, bf16[512,512]{1,0:T(8,128)(2,1)}, u32[]{:S(2)}, u32[]{:S(2)}) collective-permute-start(bf16[512,512]{1,0:T(8,128)(2,1)} %bitcast.7), channel_id=1, source_target_pairs={{0,24},{8,16},{16,8},{24,0},{1,25},{9,17},{17,9},{25,1},{2,26},{10... | collective-permute-start | bytes 1572872 | tf_op jit(solution)/shard_map/ppermute | solution.py:646
  103.3 53.5 %all-to-all-start.2 = ((bf16[8,64,1408]{2,1,0:T(8,128)(2,1)}), bf16[8,64,1408]{2,1,0:T(8,128)(2,1)}, u32[]{:S(2)}, u32[]{:S(2)}) async-start(bf16[8,64,1408]{2,1,0:T(8,128)(2,1)} %pack_ff.1), calls=%async_computation.2 | async-start | bytes 2883584 | tf_op jit(solution)/shard_map/all_to_all | solution.py:766
  107.6 102.8 %reduce-scatter.5.cloned.1.call-start = ((), (), s32[]{:S(2)}) async-start(), calls=%async_computation.10 | async-start | bytes 4718592 | tf_op jit(solution)/shard_map/reduce_scatter | solution.py:858
  161.6 97.6 %all-gather.8.cloned.1.call-start = ((), (), s32[]{:S(2)}) async-start(), calls=%async_computation.11 | async-start | bytes 4718592 | tf_op jit(solution)/shard_map/all_gather | solution.py:868
  166.0 18.0 %collective-permute-start.13 = (bf16[256,1408]{1,0:T(8,128)(2,1)S(1)}, bf16[256,1408]{1,0:T(8,128)(2,1)S(1)}, u32[]{:S(2)}, u32[]{:S(2)}) collective-permute-start(bf16[256,1408]{1,0:T(8,128)(2,1)S(1)} %get-tuple-element.275), channel_id=1, source_target_pairs={{0,8},{8,0},{16,24},{24,16},{1,9},{9,1},{17,25},{25,17},{2,10},{10... | collective-permute-start | bytes 2162696 | tf_op jit(solution)/shard_map/ppermute | solution.py:646
  167.4 18.0 %collective-permute-start.14 = (bf16[256,1408]{1,0:T(8,128)(2,1)S(1)}, bf16[256,1408]{1,0:T(8,128)(2,1)}, u32[]{:S(2)}, u32[]{:S(2)}) collective-permute-start(bf16[256,1408]{1,0:T(8,128)(2,1)S(1)} %get-tuple-element.274), channel_id=1, source_target_pairs={{0,16},{8,24},{16,0},{24,8},{1,17},{9,25},{17,1},{25,9},{2,18},{10... | collective-permute-start | bytes 2162696 | tf_op jit(solution)/shard_map/ppermute | solution.py:646
  213.8 113.3 %reduce-scatter.7.cloned.1.call-start = ((), (), s32[]{:S(2)}) async-start(), calls=%async_computation.12 | async-start | bytes 4718592 | tf_op jit(solution)/shard_map/reduce_scatter | solution.py:874
  221.2 31.2 %collective-permute-start.15 = (bf16[2,256,1408]{2,1,0:T(8,128)(2,1)S(1)}, bf16[2,256,1408]{2,1,0:T(8,128)(2,1)S(1)}, u32[]{:S(2)}, u32[]{:S(2)}) collective-permute-start(bf16[2,256,1408]{2,1,0:T(8,128)(2,1)S(1)} %pad_maximum_fusion.1), channel_id=1, source_target_pairs={{0,16},{8,24},{16,0},{24,8},{1,17},{9,25},{17,1},{25,9},{2,18},{10... | collective-permute-start | bytes 4325384 | tf_op jit(solution)/shard_map/ppermute | solution.py:646
  224.1 31.1 %collective-permute-start.16 = (bf16[2,256,1408]{2,1,0:T(8,128)(2,1)S(1)}, bf16[2,256,1408]{2,1,0:T(8,128)(2,1)S(1)}, u32[]{:S(2)}, u32[]{:S(2)}) collective-permute-start(bf16[2,256,1408]{2,1,0:T(8,128)(2,1)S(1)} %pad_maximum_fusion.2), channel_id=1, source_target_pairs={{0,8},{8,0},{16,24},{24,16},{1,9},{9,1},{17,25},{25,17},{2,10},{10... | collective-permute-start | bytes 4325384 | tf_op jit(solution)/shard_map/ppermute | solution.py:646
  278.2 98.8 %all-gather.10.cloned.1.call-start = ((), (), s32[]{:S(2)}) async-start(), calls=%async_computation.13 | async-start | bytes 4718592 | tf_op jit(solution)/shard_map/all_gather | solution.py:892
  287.7 33.8 %collective-permute-start.17 = (bf16[2,256,1408]{2,1,0:T(8,128)(2,1)S(1)}, bf16[2,256,1408]{2,1,0:T(8,128)(2,1)S(1)}, u32[]{:S(2)}, u32[]{:S(2)}) collective-permute-start(bf16[2,256,1408]{2,1,0:T(8,128)(2,1)S(1)} %pad_maximum_fusion.3), channel_id=1, source_target_pairs={{0,8},{8,0},{16,24},{24,16},{1,9},{9,1},{17,25},{25,17},{2,10},{10... | collective-permute-start | bytes 4325384 | tf_op jit(solution)/shard_map/ppermute | solution.py:646
  292.2 33.9 %collective-permute-start.18 = (bf16[2,256,1408]{2,1,0:T(8,128)(2,1)S(1)}, bf16[2,256,1408]{2,1,0:T(8,128)(2,1)}, u32[]{:S(2)}, u32[]{:S(2)}) collective-permute-start(bf16[2,256,1408]{2,1,0:T(8,128)(2,1)S(1)} %pad_maximum_fusion.4), channel_id=1, source_target_pairs={{0,16},{8,24},{16,0},{24,8},{1,17},{9,25},{17,1},{25,9},{2,18},{10... | collective-permute-start | bytes 4325384 | tf_op jit(solution)/shard_map/ppermute | solution.py:646
  331.6 127.7 %reduce-scatter.9.cloned.1.call-start = ((), (), s32[]{:S(2)}) async-start(), calls=%async_computation.14 | async-start | bytes 4718592 | tf_op jit(solution)/shard_map/reduce_scatter | solution.py:898
  336.1 39.1 %collective-permute-start.21 = (bf16[176,2048]{1,0:T(8,128)(2,1)}, bf16[176,2048]{1,0:T(8,128)(2,1)}, u32[]{:S(2)}, u32[]{:S(2)}) collective-permute-start(bf16[176,2048]{1,0:T(8,128)(2,1)} %convolution_convert_fusion.11), channel_id=1, source_target_pairs={{0,8},{8,0},{16,24},{24,16},{1,9},{9,1},{17,25},{25,17},{2,10},{10... | collective-permute-start | bytes 2162696 | tf_op jit(solution)/shard_map/ppermute | solution.py:646
  339.4 35.7 %collective-permute-start.22 = (bf16[176,2048]{1,0:T(8,128)(2,1)}, bf16[176,2048]{1,0:T(8,128)(2,1)}, u32[]{:S(2)}, u32[]{:S(2)}) collective-permute-start(bf16[176,2048]{1,0:T(8,128)(2,1)} %convolution_convert_fusion.10), channel_id=1, source_target_pairs={{0,16},{8,24},{16,0},{24,8},{1,17},{9,25},{17,1},{25,9},{2,18},{10... | collective-permute-start | bytes 2162696 | tf_op jit(solution)/shard_map/ppermute | solution.py:646
  346.3 25.2 %collective-permute-start.19 = (bf16[256,1408]{1,0:T(8,128)(2,1)}, bf16[256,1408]{1,0:T(8,128)(2,1)}, u32[]{:S(2)}, u32[]{:S(2)}) collective-permute-start(bf16[256,1408]{1,0:T(8,128)(2,1)} %fusion.11), channel_id=1, source_target_pairs={{0,16},{8,24},{16,0},{24,8},{1,17},{9,25},{17,1},{25,9},{2,18},{10... | collective-permute-start | bytes 2162696 | tf_op jit(solution)/shard_map/ppermute | solution.py:646
  349.2 22.2 %collective-permute-start.20 = (bf16[256,1408]{1,0:T(8,128)(2,1)}, bf16[256,1408]{1,0:T(8,128)(2,1)}, u32[]{:S(2)}, u32[]{:S(2)}) collective-permute-start(bf16[256,1408]{1,0:T(8,128)(2,1)} %fusion.8), channel_id=1, source_target_pairs={{0,8},{8,0},{16,24},{24,16},{1,9},{9,1},{17,25},{25,17},{2,10},{10... | collective-permute-start | bytes 2162696 | tf_op jit(solution)/shard_map/ppermute | solution.py:646
  409.5 49.8 %all-to-all-start.3 = ((bf16[8,64,1408]{2,1,0:T(8,128)(2,1)}), bf16[8,64,1408]{2,1,0:T(8,128)(2,1)S(1)}, u32[]{:S(2)}, u32[]{:S(2)}) async-start(bf16[8,64,1408]{2,1,0:T(8,128)(2,1)} %bitcast.191), calls=%async_computation.6 | async-start | bytes 2883584 | tf_op jit(solution)/shard_map/all_to_all | solution.py:766
  413.1 103.1 %reduce-scatter.11.cloned.1.call-start = ((), (), s32[]{:S(2)}) async-start(), calls=%async_computation.15 | async-start | bytes 4718592 | tf_op jit(solution)/shard_map/reduce_scatter | solution.py:940
  413.1 45.4 %collective-permute-start.23 = (bf16[2,256,1024]{2,1,0:T(8,128)(2,1)}, bf16[2,256,1024]{2,1,0:T(8,128)(2,1)}, u32[]{:S(2)}, u32[]{:S(2)}) collective-permute-start(bf16[2,256,1024]{2,1,0:T(8,128)(2,1)} %get-tuple-element.177), channel_id=1, source_target_pairs={{0,8},{8,0},{16,24},{24,16},{1,9},{9,1},{17,25},{25,17},{2,10},{10... | collective-permute-start | bytes 3145736 | tf_op jit(solution)/shard_map/ppermute | solution.py:646
  414.6 44.6 %collective-permute-start.24 = (bf16[2,256,1024]{2,1,0:T(8,128)(2,1)}, bf16[2,256,1024]{2,1,0:T(8,128)(2,1)}, u32[]{:S(2)}, u32[]{:S(2)}) collective-permute-start(bf16[2,256,1024]{2,1,0:T(8,128)(2,1)} %get-tuple-element.178), channel_id=1, source_target_pairs={{0,16},{8,24},{16,0},{24,8},{1,17},{9,25},{17,1},{25,9},{2,18},{10... | collective-permute-start | bytes 3145736 | tf_op jit(solution)/shard_map/ppermute | solution.py:646
  420.6 26.0 %collective-permute-start.25 = (bf16[64,2048]{1,0:T(8,128)(2,1)}, bf16[64,2048]{1,0:T(8,128)(2,1)}, u32[]{:S(2)}, u32[]{:S(2)}) collective-permute-start(bf16[64,2048]{1,0:T(8,128)(2,1)} %get-tuple-element.283), channel_id=1, source_target_pairs={{0,0},{8,1},{2,2},{10,3},{4,4},{12,5},{6,6},{14,7},{16,8},{24,9},{... | collective-permute-start | bytes 786440 | tf_op jit(solution)/shard_map/ppermute | solution.py:761
  424.2 29.0 %collective-permute-start.26 = (bf16[64,2048]{1,0:T(8,128)(2,1)}, bf16[64,2048]{1,0:T(8,128)(2,1)}, u32[]{:S(2)}, u32[]{:S(2)}) collective-permute-start(bf16[64,2048]{1,0:T(8,128)(2,1)} %get-tuple-element.282), channel_id=1, source_target_pairs={{8,0},{0,1},{10,2},{2,3},{12,4},{4,5},{14,6},{6,7},{24,8},{16,9},{... | collective-permute-start | bytes 786440 | tf_op jit(solution)/shard_map/ppermute | solution.py:761
  424.2 29.0 %collective-permute-start.27 = (bf16[64,2048]{1,0:T(8,128)(2,1)}, bf16[64,2048]{1,0:T(8,128)(2,1)}, u32[]{:S(2)}, u32[]{:S(2)}) collective-permute-start(bf16[64,2048]{1,0:T(8,128)(2,1)} %get-tuple-element.281), channel_id=1, source_target_pairs={{16,0},{24,1},{18,2},{26,3},{20,4},{28,5},{22,6},{30,7},{0,8},{8,9... | collective-permute-start | bytes 786440 | tf_op jit(solution)/shard_map/ppermute | solution.py:761
  446.7 11.8 %collective-permute-start.28 = (bf16[64,2048]{1,0:T(8,128)(2,1)S(1)}, bf16[64,2048]{1,0:T(8,128)(2,1)S(1)}, u32[]{:S(2)}, u32[]{:S(2)}) collective-permute-start(bf16[64,2048]{1,0:T(8,128)(2,1)S(1)} %copy-done.72), channel_id=1, source_target_pairs={{24,0},{16,1},{26,2},{18,3},{28,4},{20,5},{30,6},{22,7},{8,8},{0,9... | collective-permute-start | bytes 786440 | tf_op jit(solution)/shard_map/ppermute | solution.py:761
  465.7 10.0 %collective-permute-start.33 = (bf16[512,128]{1,0:T(8,128)(2,1)S(1)}, bf16[512,128]{1,0:T(8,128)(2,1)S(1)}, u32[]{:S(2)}, u32[]{:S(2)}) collective-permute-start(bf16[512,128]{1,0:T(8,128)(2,1)S(1)} %get-tuple-element.287), channel_id=1, source_target_pairs={{0,24},{8,16},{16,8},{24,0},{1,25},{9,17},{17,9},{25,1},{2,26},{10... | collective-permute-start | bytes 393224 | tf_op jit(solution)/shard_map/ppermute | solution.py:646
  466.5 11.5 %collective-permute-start.32 = (bf16[512,128]{1,0:T(8,128)(2,1)S(1)}, bf16[512,128]{1,0:T(8,128)(2,1)S(1)}, u32[]{:S(2)}, u32[]{:S(2)}) collective-permute-start(bf16[512,128]{1,0:T(8,128)(2,1)S(1)} %get-tuple-element.288), channel_id=1, source_target_pairs={{0,16},{8,24},{16,0},{24,8},{1,17},{9,25},{17,1},{25,9},{2,18},{10... | collective-permute-start | bytes 393224 | tf_op jit(solution)/shard_map/ppermute | solution.py:646
  467.1 10.9 %collective-permute-start.31 = (bf16[512,128]{1,0:T(8,128)(2,1)S(1)}, bf16[512,128]{1,0:T(8,128)(2,1)S(1)}, u32[]{:S(2)}, u32[]{:S(2)}) collective-permute-start(bf16[512,128]{1,0:T(8,128)(2,1)S(1)} %get-tuple-element.286), channel_id=1, source_target_pairs={{0,8},{8,0},{16,24},{24,16},{1,9},{9,1},{17,25},{25,17},{2,10},{10... | collective-permute-start | bytes 393224 | tf_op jit(solution)/shard_map/ppermute | solution.py:646
  470.5 16.8 %collective-permute-start.29 = (bf16[256,1024]{1,0:T(8,128)(2,1)S(1)}, bf16[256,1024]{1,0:T(8,128)(2,1)S(1)}, u32[]{:S(2)}, u32[]{:S(2)}) collective-permute-start(bf16[256,1024]{1,0:T(8,128)(2,1)S(1)} %fusion.22), channel_id=1, source_target_pairs={{0,16},{8,24},{16,0},{24,8},{1,17},{9,25},{17,1},{25,9},{2,18},{10... | collective-permute-start | bytes 1572872 | tf_op jit(solution)/shard_map/ppermute | solution.py:646
  472.5 14.9 %collective-permute-start.30 = (bf16[256,1024]{1,0:T(8,128)(2,1)S(1)}, bf16[256,1024]{1,0:T(8,128)(2,1)S(1)}, u32[]{:S(2)}, u32[]{:S(2)}) collective-permute-start(bf16[256,1024]{1,0:T(8,128)(2,1)S(1)} %fusion.19), channel_id=1, source_target_pairs={{0,8},{8,0},{16,24},{24,16},{1,9},{9,1},{17,25},{25,17},{2,10},{10... | collective-permute-start | bytes 1572872 | tf_op jit(solution)/shard_map/ppermute | solution.py:646
  475.7 25.2 %collective-permute-start.34 = (bf16[176,2048]{1,0:T(8,128)(2,1)}, bf16[176,2048]{1,0:T(8,128)(2,1)S(1)}, u32[]{:S(2)}, u32[]{:S(2)}) collective-permute-start(bf16[176,2048]{1,0:T(8,128)(2,1)} %convolution_convert_fusion.8), channel_id=1, source_target_pairs={{0,24},{8,16},{16,8},{24,0},{1,25},{9,17},{17,9},{25,1},{2,26},{10... | collective-permute-start | bytes 2162696 | tf_op jit(solution)/shard_map/ppermute | solution.py:646
  490.4 42.5 %all-to-all-start.4 = ((bf16[8,64,1152]{2,1,0:T(8,128)(2,1)}), bf16[8,64,1152]{2,1,0:T(8,128)(2,1)S(1)}, u32[]{:S(2)}, u32[]{:S(2)}) async-start(bf16[8,64,1152]{2,1,0:T(8,128)(2,1)} %bitcast.192), calls=%async_computation.7 | async-start | bytes 2359296 | tf_op jit(solution)/shard_map/all_to_all | solution.py:766
  (83 other events, 983.4 us)
Sparse Core Ops, SparseCore 0:
  9.6 65.4 all-gather.11
  77.3 64.0 all-gather.5
  161.7 48.6 reduce-scatter.4
  213.9 45.2 all-gather.7
  278.3 48.7 reduce-scatter.6
  331.7 45.2 all-gather.9
  379.3 57.3 reduce-scatter.8
  459.4 56.7 reduce-scatter.10

commit v3 on v2

--- a/solution.py
+++ b/solution.py
@@ -933,8 +933,8 @@
 
     g_out = dot(y_local, d_attn_later, TN).astype(BF)
     g_out_parts = row_owner_parts(g_out.reshape(dps, row_part, width))
-    d_h1_part, out_sum, g_gate_up, g_mix_moved, small_grad, *g_out_parts = lax.optimization_barrier(
-        (d_h1_part, out_sum, g_gate_up, g_mix_moved, small_grad, *g_out_parts)
+    d_h1_part, out_sum, g_gate_up, g_mix_moved, *g_out_parts = lax.optimization_barrier(
+        (d_h1_part, out_sum, g_gate_up, g_mix_moved, *g_out_parts)
     )
     block_out = (resid + out_sum.astype(F32)).astype(BF)[None]
     d_h1 = lax.psum_scatter(d_h1_part, "ctx", scatter_dimension=0, tiled=True).astype(F32)

time: 556 us -> 554 us (level)
    ppermute x4, waiting for transfers between devices: 5.35 us -> 17 us  [row_owner_parts(): parts.append(lax.ppermute(block, ('dp', 'ctx'), routes))]
    ppermute x27, waiting for transfers between devices: 131 us -> 124 us  [swapped(): return lax.ppermute(value, axis, [(i, i ^ distance) for i in range(count)])]
    reduce_scatter x1, waiting for transfers between devices: 6.99 us -> 0.01 us  [per_device(): lax.psum_scatter(d_h1_part, 'ctx', scatter_dimension=0, tiled=True)]
    unnamed x168 -> x130, local copies, waits for them, and re-layouts: 15.6 us -> 16.4 us
  transfers between devices with their start and end apart: 48 -> 48, of which waited for: 23 -> 22; matrix products, arithmetic and copies ran while one was open for 28% -> 27% of each run, Pallas kernels for 7% -> 7%
where the time goes in v3:
time: 554 us; the launch traced here: 545 us
  waiting for transfers between devices  197 us (36%)
  starting transfers between devices  92 us (17%)
  matrix products  75.7 us (14%)
  Pallas kernels  58.9 us (11%)
  local copies, waits for them, and re-layouts  57.1 us (10%)
  other arithmetic  47.2 us (9%)
  between operations  16.4 us (3%)
    ppermute x27, waiting for transfers between devices, swapped(): return lax.ppermute(value, axis, [(i, i ^ distance) for i in range(count)])  124 us
    dot_general x21, matrix products, dot(): lax.dot_general(left, right, (dims, ((), ())), preferred_element_type=F32)  75.7 us
    ppermute x27, starting transfers between devices, swapped(): return lax.ppermute(value, axis, [(i, i ^ distance) for i in range(count)])  50.8 us
    dynamic_update_slice x24, local copies, waits for them, and re-layouts, placed(): whole = lax.dynamic_update_index_in_dim(whole, part, place, 0)  26.8 us
    all_to_all x5, starting transfers between devices, spread(): return lax.all_to_all(value, axis, 0, 0, tiled=True)  23 us
    reduce_scatter x1, waiting for transfers between devices, per_device(): lax.psum_scatter(attn_part, 'ctx', scatter_dimension=0, tiled=True)  22.2 us
    all_to_all x5, waiting for transfers between devices, spread(): return lax.all_to_all(value, axis, 0, 0, tiled=True)  20.7 us
    pallas_call x1, Pallas kernels, mix_backward(): pl.pallas_call(functools.partial(mix_backward_kernel, heads=heads, blocks...  19.1 us
  transfers between devices with their start and end apart: 48, of which 22 were waited for; matrix products, arithmetic and copies ran while one was open for 27% of the time, Pallas kernels for 7%

profile of v3, /device:TPU:0, one launch (start us, length us, event | category | flops | bytes accessed | tf_op | source)
XLA Modules:
  0.0 544.6 jit_solution(16515629907107710895)
XLA Ops:
  15.3 6.3 %all-to-all-start = ((bf16[8,64,640]{2,1,0:T(8,128)(2,1)}), bf16[8,64,640]{2,1,0:T(8,128)(2,1)S(1)}, u32[]{:S(2)}, u32[]{:S(2)}) async-start(bf16[8,64,640]{2,1,0:T(8,128)(2,1)} %get-tuple-element.110), calls=%async_computation | async-start | bytes 1310720 | tf_op jit(solution)/shard_map/all_to_all | solution.py:766
  27.0 13.7 %collective-permute-done = bf16[176,2048]{1,0:T(8,128)(2,1)S(1)} collective-permute-done((bf16[176,2048]{1,0:T(8,128)(2,1)}, bf16[176,2048]{1,0:T(8,128)(2,1)S(1)}, u32[]{:S(2)}, u32[]{:S(2)}) %collective-permute-start) | collective-permute-done | bytes 720928 | tf_op jit(solution)/shard_map/ppermute | solution.py:646
  40.8 16.3 %collective-permute-done.1 = bf16[176,2048]{1,0:T(8,128)(2,1)S(1)} collective-permute-done((bf16[176,2048]{1,0:T(8,128)(2,1)}, bf16[176,2048]{1,0:T(8,128)(2,1)S(1)}, u32[]{:S(2)}, u32[]{:S(2)}) %collective-permute-start.1) | collective-permute-done | bytes 720928 | tf_op jit(solution)/shard_map/ppermute | solution.py:646
  58.7 3.4 collective-permute-start.3
  62.0 4.7 all-to-all-start.1
  70.6 2.9 collective-permute-start.8
  75.2 6.8 %collective-permute-done.6 = bf16[64,2048]{1,0:T(8,128)(2,1)S(1)} collective-permute-done((bf16[64,2048]{1,0:T(8,128)(2,1)}, bf16[64,2048]{1,0:T(8,128)(2,1)S(1)}, u32[]{:S(2)}, u32[]{:S(2)}) %collective-permute-start.6) | collective-permute-done | bytes 262176 | tf_op jit(solution)/shard_map/ppermute | solution.py:752
  81.9 14.7 %collective-permute-start.9 = (bf16[512,640]{1,0:T(8,128)(2,1)S(1)}, bf16[512,640]{1,0:T(8,128)(2,1)}, u32[]{:S(2)}, u32[]{:S(2)}) collective-permute-start(bf16[512,640]{1,0:T(8,128)(2,1)S(1)} %bitcast.206), channel_id=1, source_target_pairs={{0,24},{8,16},{16,8},{24,0},{1,25},{9,17},{17,9},{25,1},{2,26},{10... | collective-permute-start | bytes 1966088 | tf_op jit(solution)/shard_map/ppermute | solution.py:646
  97.3 2.9 collective-permute-start.12
  105.2 3.6 all-to-all-start.2
  108.8 3.1 fusion
  120.2 3.4 fusion.61.first_ref.first_before_ref
  131.3 12.9 %mix_forward.1 = (bf16[1024,256]{1,0:T(8,128)(2,1)S(1)}, f32[1024,256]{1,0:T(8,128)}, f32[8,2,128,128]{3,2,1,0:T(8,128)}, f32[8,2,128,128]{3,2,1,0:T(8,128)}) custom-call(f32[1024,640]{1,0:T(8,128)S(1)} %fusion.61.first_ref.first_before_ref, f32[1024,512]{1,0:T(8,128)S(1)} %fusion.62.second_ref.second_before_ref, f32[8,768]{1,0:T(8,128)S(1)} %get-tuple-element.133.taps_ref, ...), custom_call_target="tpu_custom_call" | custom-call | flops 3019898880 | bytes 10485760 | tf_op jit(solution)/shard_map/mix_forward/pallas_call | solution.py:275
  146.3 11.4 %all-to-all-done.2 = bf16[8,64,1408]{2,1,0:T(8,128)(2,1)S(1)} async-done(((bf16[8,64,1408]{2,1,0:T(8,128)(2,1)}), bf16[8,64,1408]{2,1,0:T(8,128)(2,1)S(1)}, u32[]{:S(2)}, u32[]{:S(2)}) %all-to-all-start.2) | async-done | bytes 1441824 | tf_op jit(solution)/shard_map/all_to_all | solution.py:766
  157.7 5.2 convolution_convert_fusion.2
  177.7 10.5 %collective-permute-done.13 = bf16[256,1408]{1,0:T(8,128)(2,1)S(1)} collective-permute-done((bf16[256,1408]{1,0:T(8,128)(2,1)S(1)}, bf16[256,1408]{1,0:T(8,128)(2,1)S(1)}, u32[]{:S(2)}, u32[]{:S(2)}) %collective-permute-start.13) | collective-permute-done | bytes 720928 | tf_op jit(solution)/shard_map/ppermute | solution.py:646
  189.6 22.2 %reduce-scatter.5.cloned.1.call-done = bf16[128,2048]{1,0:T(8,128)(2,1)} async-done(((bf16[1024,2048]{1,0:T(8,128)(2,1)}), bf16[128,2048]{1,0:T(8,128)(2,1)}) %reduce-scatter.5.cloned.1.call-update) | async-done | bytes 524304 | tf_op jit(solution)/shard_map/reduce_scatter | solution.py:858
  215.3 2.9 broadcast_in_dim.144
  227.8 6.8 %convolution_convert_fusion.12.dhidden_ref = bf16[1024,704]{1,0:T(8,128)(2,1)} fusion(bf16[1024,2048]{1,0:T(8,128)(2,1)S(1)} %copy-done.19, bf16[704,2048]{1,0:T(8,128)(2,1)} %bitcast.32), kind=kOutput, calls=%fused_computation.28 | convolution fusion | flops 2953510912 | bytes 8519680 | tf_op jit(solution)/shard_map/dot_general | solution.py:637
  234.6 16.8 %collective-permute-done.15 = bf16[2,256,1408]{2,1,0:T(8,128)(2,1)S(1)} collective-permute-done((bf16[2,256,1408]{2,1,0:T(8,128)(2,1)S(1)}, bf16[2,256,1408]{2,1,0:T(8,128)(2,1)S(1)}, u32[]{:S(2)}, u32[]{:S(2)}) %collective-permute-start.15) | collective-permute-done | bytes 1441824 | tf_op jit(solution)/shard_map/ppermute | solution.py:646
  256.9 3.7 all-gather.8.cloned.1.call-done.h2_ref
  260.6 18.9 %gate_up_both_ways.1 = (bf16[1024,704]{1,0:T(8,128)(2,1)S(1)}, bf16[1024,1408]{1,0:T(8,128)(2,1)}, bf16[1024,2048]{1,0:T(8,128)(2,1)}) custom-call(bf16[1024,2048]{1,0:T(8,128)(2,1)} %all-gather.8.cloned.1.call-done.h2_ref, bf16[1024,704]{1,0:T(8,128)(2,1)} %convolution_convert_fusion.12.dhidden_ref, bf16[2048,1408]{1,0:T(8,128)(2,1)} %bitcast.38.weight_ref), custom_call_target="tpu_custom_call" | custom-call | flops 11811160064 | bytes 12582912 | tf_op jit(solution)/shard_map/gate_up_both_ways/pallas_call | solution.py:612
  279.7 4.1 convolution_convert_fusion.5
  283.8 3.8 convolution_convert_fusion.6
  295.3 27.7 %collective-permute-done.17 = bf16[2,256,1408]{2,1,0:T(8,128)(2,1)S(1)} collective-permute-done((bf16[2,256,1408]{2,1,0:T(8,128)(2,1)S(1)}, bf16[2,256,1408]{2,1,0:T(8,128)(2,1)S(1)}, u32[]{:S(2)}, u32[]{:S(2)}) %collective-permute-start.17) | collective-permute-done | bytes 1441824 | tf_op jit(solution)/shard_map/ppermute | solution.py:646
  324.1 3.5 collective-permute-done.18
  329.8 2.9 fusion.59
  333.0 4.2 convolution_convert_fusion.11
  342.1 4.2 convolution_convert_fusion.3
  351.1 6.8 %convolution_convert_fusion.1 = bf16[1024,2048]{1,0:T(8,128)(2,1)} fusion(bf16[1024,704]{1,0:T(8,128)(2,1)S(1)} %get-tuple-element.161, bf16[704,2048]{1,0:T(8,128)(2,1)} %bitcast.32), kind=kOutput, calls=%fused_computation.7 | convolution fusion | flops 2954887168 | bytes 8519680 | tf_op jit(solution)/shard_map/dot_general | solution.py:637
  357.8 15.0 %collective-permute-done.19 = bf16[256,1408]{1,0:T(8,128)(2,1)} collective-permute-done((bf16[256,1408]{1,0:T(8,128)(2,1)}, bf16[256,1408]{1,0:T(8,128)(2,1)}, u32[]{:S(2)}, u32[]{:S(2)}) %collective-permute-start.19) | collective-permute-done | bytes 720928 | tf_op jit(solution)/shard_map/ppermute | solution.py:646
  378.3 3.6 all-to-all-start.3
  381.9 3.9 convolution_convert_fusion.17.dy_ref
  385.9 19.1 %mix_backward.1 = (bf16[1024,1024]{1,0:T(8,128)(2,1)}, f32[1024,2]{1,0:T(8,128)S(1)}, f32[8,768]{1,0:T(8,128)S(1)}, f32[8,128]{1,0:T(8,128)S(1)}) custom-call(f32[1024,640]{1,0:T(8,128)} %copy-done, f32[1024,512]{1,0:T(8,128)} %copy-done.1, f32[1024,640]{1,0:T(8,128)} %copy-done, f32[1024,512]{1,0:T(8,128)} %copy-done.1, ...), custom_call_target="tpu_custom_call" | custom-call | flops 3019898880 | bytes 10485760 | tf_op jit(solution)/shard_map/mix_backward/pallas_call | solution.py:324
  405.0 3.0 convolution_convert_fusion.16
  417.1 3.3 collective-permute-start.23
  424.7 8.3 %collective-permute-start.28 = (bf16[64,2048]{1,0:T(8,128)(2,1)}, bf16[64,2048]{1,0:T(8,128)(2,1)}, u32[]{:S(2)}, u32[]{:S(2)}) collective-permute-start(bf16[64,2048]{1,0:T(8,128)(2,1)} %get-tuple-element.278), channel_id=1, source_target_pairs={{24,0},{16,1},{26,2},{18,3},{28,4},{20,5},{30,6},{22,7},{8,8},{0,9... | collective-permute-start | bytes 786440 | tf_op jit(solution)/shard_map/ppermute | solution.py:761
  433.0 7.5 %convolution_convert_fusion = bf16[1024,2048]{1,0:T(8,128)(2,1)} fusion(bf16[2048,1152]{1,0:T(8,128)(2,1)S(1)} %bitcast.196, bf16[1024,128]{1,0:T(8,128)(2,1)S(1)} %pad.12, bf16[1024,1024]{1,0:T(8,128)(2,1)S(1)} %copy-done.24), kind=kOutput, calls=%fused_computation.6 | convolution fusion | flops 4838653952 | bytes 11272192 | tf_op jit(solution)/shard_map/dot_general | solution.py:637
  440.5 14.8 %collective-permute-done.26 = bf16[64,2048]{1,0:T(8,128)(2,1)} collective-permute-done((bf16[64,2048]{1,0:T(8,128)(2,1)}, bf16[64,2048]{1,0:T(8,128)(2,1)}, u32[]{:S(2)}, u32[]{:S(2)}) %collective-permute-start.26) | collective-permute-done | bytes 262176 | tf_op jit(solution)/shard_map/ppermute | solution.py:761
  457.7 4.3 convolution_convert_fusion.8
  469.1 3.7 fusion.4
  481.3 2.5 convolution_convert_fusion.13
  485.3 10.1 %collective-permute-done.29 = bf16[256,1024]{1,0:T(8,128)(2,1)S(1)} collective-permute-done((bf16[256,1024]{1,0:T(8,128)(2,1)S(1)}, bf16[256,1024]{1,0:T(8,128)(2,1)S(1)}, u32[]{:S(2)}, u32[]{:S(2)}) %collective-permute-start.29) | collective-permute-done | bytes 524320 | tf_op jit(solution)/shard_map/ppermute | solution.py:646
  498.3 4.8 all-to-all-start.4
  503.2 5.7 %collective-permute-done.34 = bf16[176,2048]{1,0:T(8,128)(2,1)} collective-permute-done((bf16[176,2048]{1,0:T(8,128)(2,1)}, bf16[176,2048]{1,0:T(8,128)(2,1)}, u32[]{:S(2)}, u32[]{:S(2)}) %collective-permute-start.34) | collective-permute-done | bytes 720928 | tf_op jit(solution)/shard_map/ppermute | solution.py:646
  508.9 3.5 convert_add_fusion.5
  519.0 4.3 fusion.18
  523.3 9.3 %all-to-all-done.4.in_ref = bf16[8,64,1152]{2,1,0:T(8,128)(2,1)S(1)} async-done(((bf16[8,64,1152]{2,1,0:T(8,128)(2,1)}), bf16[8,64,1152]{2,1,0:T(8,128)(2,1)S(1)}, u32[]{:S(2)}, u32[]{:S(2)}) %all-to-all-start.4) | async-done | bytes 1179680 | tf_op jit(solution)/shard_map/all_to_all | solution.py:766
  (312 shorter events, 151.1 us)
Async XLA Ops:
  7.2 101.6 %all-gather.12.cloned.1.call-start = ((), (), s32[]{:S(2)}) async-start(), calls=%async_computation.16 | async-start | bytes 4718592 | tf_op jit(solution)/shard_map/all_gather | solution.py:812
  15.3 43.4 %all-to-all-start = ((bf16[8,64,640]{2,1,0:T(8,128)(2,1)}), bf16[8,64,640]{2,1,0:T(8,128)(2,1)S(1)}, u32[]{:S(2)}, u32[]{:S(2)}) async-start(bf16[8,64,640]{2,1,0:T(8,128)(2,1)} %get-tuple-element.110), calls=%async_computation | async-start | bytes 1310720 | tf_op jit(solution)/shard_map/all_to_all | solution.py:766
  21.6 19.1 %collective-permute-start = (bf16[176,2048]{1,0:T(8,128)(2,1)}, bf16[176,2048]{1,0:T(8,128)(2,1)S(1)}, u32[]{:S(2)}, u32[]{:S(2)}) collective-permute-start(bf16[176,2048]{1,0:T(8,128)(2,1)} %param.27), channel_id=1, source_target_pairs={{0,8},{8,0},{16,24},{24,16},{1,9},{9,1},{17,25},{25,17},{2,10},{10... | collective-permute-start | bytes 2162696 | tf_op jit(solution)/shard_map/ppermute | solution.py:646
  23.1 33.9 %collective-permute-start.1 = (bf16[176,2048]{1,0:T(8,128)(2,1)}, bf16[176,2048]{1,0:T(8,128)(2,1)S(1)}, u32[]{:S(2)}, u32[]{:S(2)}) collective-permute-start(bf16[176,2048]{1,0:T(8,128)(2,1)} %param.27), channel_id=1, source_target_pairs={{0,16},{8,24},{16,0},{24,8},{1,17},{9,25},{17,1},{25,9},{2,18},{10... | collective-permute-start | bytes 2162696 | tf_op jit(solution)/shard_map/ppermute | solution.py:646
  24.6 34.0 %collective-permute-start.2 = (bf16[176,2048]{1,0:T(8,128)(2,1)}, bf16[176,2048]{1,0:T(8,128)(2,1)}, u32[]{:S(2)}, u32[]{:S(2)}) collective-permute-start(bf16[176,2048]{1,0:T(8,128)(2,1)} %param.27), channel_id=1, source_target_pairs={{0,24},{8,16},{16,8},{24,0},{1,25},{9,17},{17,9},{25,1},{2,26},{10... | collective-permute-start | bytes 2162696 | tf_op jit(solution)/shard_map/ppermute | solution.py:646
  57.1 13.5 %collective-permute-start.5 = (bf16[64,2048]{1,0:T(8,128)(2,1)}, bf16[64,2048]{1,0:T(8,128)(2,1)S(1)}, u32[]{:S(2)}, u32[]{:S(2)}) collective-permute-start(bf16[64,2048]{1,0:T(8,128)(2,1)} %param.24), channel_id=1, source_target_pairs={{0,0},{1,8},{2,2},{3,10},{4,4},{5,12},{6,6},{7,14},{8,16},{9,24},{... | collective-permute-start | bytes 786440 | tf_op jit(solution)/shard_map/ppermute | solution.py:752
  58.7 38.0 %collective-permute-start.3 = (bf16[512,640]{1,0:T(8,128)(2,1)S(1)}, bf16[512,640]{1,0:T(8,128)(2,1)}, u32[]{:S(2)}, u32[]{:S(2)}) collective-permute-start(bf16[512,640]{1,0:T(8,128)(2,1)S(1)} %bitcast.204), channel_id=1, source_target_pairs={{0,8},{8,0},{16,24},{24,16},{1,9},{9,1},{17,25},{25,17},{2,10},{10... | collective-permute-start | bytes 1966088 | tf_op jit(solution)/shard_map/ppermute | solution.py:646
  62.0 34.6 %collective-permute-start.4 = (bf16[512,640]{1,0:T(8,128)(2,1)S(1)}, bf16[512,640]{1,0:T(8,128)(2,1)}, u32[]{:S(2)}, u32[]{:S(2)}) collective-permute-start(bf16[512,640]{1,0:T(8,128)(2,1)S(1)} %bitcast.205), channel_id=1, source_target_pairs={{0,16},{8,24},{16,0},{24,8},{1,17},{9,25},{17,1},{25,9},{2,18},{10... | collective-permute-start | bytes 1966088 | tf_op jit(solution)/shard_map/ppermute | solution.py:646
  62.0 34.6 %all-to-all-start.1 = ((bf16[8,64,512]{2,1,0:T(8,128)(2,1)}), bf16[8,64,512]{2,1,0:T(8,128)(2,1)}, u32[]{:S(2)}, u32[]{:S(2)}) async-start(bf16[8,64,512]{2,1,0:T(8,128)(2,1)} %get-tuple-element.112), calls=%async_computation.1 | async-start | bytes 1048576 | tf_op jit(solution)/shard_map/all_to_all | solution.py:766
  66.8 91.0 %all-gather.6.cloned.1.call-start = ((), (), s32[]{:S(2)}) async-start(), calls=%async_computation.9 | async-start | bytes 4718592 | tf_op jit(solution)/shard_map/all_gather | solution.py:821
  68.4 13.5 %collective-permute-start.6 = (bf16[64,2048]{1,0:T(8,128)(2,1)}, bf16[64,2048]{1,0:T(8,128)(2,1)S(1)}, u32[]{:S(2)}, u32[]{:S(2)}) collective-permute-start(bf16[64,2048]{1,0:T(8,128)(2,1)} %param.24), channel_id=1, source_target_pairs={{0,8},{1,0},{2,10},{3,2},{4,12},{5,4},{6,14},{7,6},{8,24},{9,16},{... | collective-permute-start | bytes 786440 | tf_op jit(solution)/shard_map/ppermute | solution.py:752
  69.0 27.6 %collective-permute-start.7 = (bf16[64,2048]{1,0:T(8,128)(2,1)}, bf16[64,2048]{1,0:T(8,128)(2,1)S(1)}, u32[]{:S(2)}, u32[]{:S(2)}) collective-permute-start(bf16[64,2048]{1,0:T(8,128)(2,1)} %param.24), channel_id=1, source_target_pairs={{0,16},{1,24},{2,18},{3,26},{4,20},{5,28},{6,22},{7,30},{8,0},{9,8... | collective-permute-start | bytes 786440 | tf_op jit(solution)/shard_map/ppermute | solution.py:752
  70.6 26.1 %collective-permute-start.8 = (bf16[64,2048]{1,0:T(8,128)(2,1)}, bf16[64,2048]{1,0:T(8,128)(2,1)}, u32[]{:S(2)}, u32[]{:S(2)}) collective-permute-start(bf16[64,2048]{1,0:T(8,128)(2,1)} %param.24), channel_id=1, source_target_pairs={{0,24},{1,16},{2,26},{3,18},{4,28},{5,20},{6,30},{7,22},{8,8},{9,0... | collective-permute-start | bytes 786440 | tf_op jit(solution)/shard_map/ppermute | solution.py:752
  81.9 30.6 %collective-permute-start.9 = (bf16[512,640]{1,0:T(8,128)(2,1)S(1)}, bf16[512,640]{1,0:T(8,128)(2,1)}, u32[]{:S(2)}, u32[]{:S(2)}) collective-permute-start(bf16[512,640]{1,0:T(8,128)(2,1)S(1)} %bitcast.206), channel_id=1, source_target_pairs={{0,24},{8,16},{16,8},{24,0},{1,25},{9,17},{17,9},{25,1},{2,26},{10... | collective-permute-start | bytes 1966088 | tf_op jit(solution)/shard_map/ppermute | solution.py:646
  96.7 27.0 %collective-permute-start.10 = (bf16[512,512]{1,0:T(8,128)(2,1)}, bf16[512,512]{1,0:T(8,128)(2,1)}, u32[]{:S(2)}, u32[]{:S(2)}) collective-permute-start(bf16[512,512]{1,0:T(8,128)(2,1)} %bitcast.7), channel_id=1, source_target_pairs={{0,8},{8,0},{16,24},{24,16},{1,9},{9,1},{17,25},{25,17},{2,10},{10... | collective-permute-start | bytes 1572872 | tf_op jit(solution)/shard_map/ppermute | solution.py:646
  96.8 26.9 %collective-permute-start.11 = (bf16[512,512]{1,0:T(8,128)(2,1)}, bf16[512,512]{1,0:T(8,128)(2,1)}, u32[]{:S(2)}, u32[]{:S(2)}) collective-permute-start(bf16[512,512]{1,0:T(8,128)(2,1)} %bitcast.7), channel_id=1, source_target_pairs={{0,16},{8,24},{16,0},{24,8},{1,17},{9,25},{17,1},{25,9},{2,18},{10... | collective-permute-start | bytes 1572872 | tf_op jit(solution)/shard_map/ppermute | solution.py:646
  97.3 26.8 %collective-permute-start.12 = (bf16[512,512]{1,0:T(8,128)(2,1)}, bf16[512,512]{1,0:T(8,128)(2,1)}, u32[]{:S(2)}, u32[]{:S(2)}) collective-permute-start(bf16[512,512]{1,0:T(8,128)(2,1)} %bitcast.7), channel_id=1, source_target_pairs={{0,24},{8,16},{16,8},{24,0},{1,25},{9,17},{17,9},{25,1},{2,26},{10... | collective-permute-start | bytes 1572872 | tf_op jit(solution)/shard_map/ppermute | solution.py:646
  105.2 52.6 %all-to-all-start.2 = ((bf16[8,64,1408]{2,1,0:T(8,128)(2,1)}), bf16[8,64,1408]{2,1,0:T(8,128)(2,1)S(1)}, u32[]{:S(2)}, u32[]{:S(2)}) async-start(bf16[8,64,1408]{2,1,0:T(8,128)(2,1)} %pack_ff.1), calls=%async_computation.2 | async-start | bytes 2883584 | tf_op jit(solution)/shard_map/all_to_all | solution.py:766
  108.7 103.0 %reduce-scatter.5.cloned.1.call-start = ((), (), s32[]{:S(2)}) async-start(), calls=%async_computation.10 | async-start | bytes 4718592 | tf_op jit(solution)/shard_map/reduce_scatter | solution.py:858
  163.0 97.7 %all-gather.8.cloned.1.call-start = ((), (), s32[]{:S(2)}) async-start(), calls=%async_computation.11 | async-start | bytes 4718592 | tf_op jit(solution)/shard_map/all_gather | solution.py:868
  170.2 18.0 %collective-permute-start.13 = (bf16[256,1408]{1,0:T(8,128)(2,1)S(1)}, bf16[256,1408]{1,0:T(8,128)(2,1)S(1)}, u32[]{:S(2)}, u32[]{:S(2)}) collective-permute-start(bf16[256,1408]{1,0:T(8,128)(2,1)S(1)} %get-tuple-element.273), channel_id=1, source_target_pairs={{0,8},{8,0},{16,24},{24,16},{1,9},{9,1},{17,25},{25,17},{2,10},{10... | collective-permute-start | bytes 2162696 | tf_op jit(solution)/shard_map/ppermute | solution.py:646
  171.7 17.9 %collective-permute-start.14 = (bf16[256,1408]{1,0:T(8,128)(2,1)S(1)}, bf16[256,1408]{1,0:T(8,128)(2,1)}, u32[]{:S(2)}, u32[]{:S(2)}) collective-permute-start(bf16[256,1408]{1,0:T(8,128)(2,1)S(1)} %get-tuple-element.272), channel_id=1, source_target_pairs={{0,16},{8,24},{16,0},{24,8},{1,17},{9,25},{17,1},{25,9},{2,18},{10... | collective-permute-start | bytes 2162696 | tf_op jit(solution)/shard_map/ppermute | solution.py:646
  215.2 113.3 %reduce-scatter.7.cloned.1.call-start = ((), (), s32[]{:S(2)}) async-start(), calls=%async_computation.12 | async-start | bytes 4718592 | tf_op jit(solution)/shard_map/reduce_scatter | solution.py:874
  220.2 31.2 %collective-permute-start.15 = (bf16[2,256,1408]{2,1,0:T(8,128)(2,1)S(1)}, bf16[2,256,1408]{2,1,0:T(8,128)(2,1)S(1)}, u32[]{:S(2)}, u32[]{:S(2)}) collective-permute-start(bf16[2,256,1408]{2,1,0:T(8,128)(2,1)S(1)} %pad_maximum_fusion.1), channel_id=1, source_target_pairs={{0,16},{8,24},{16,0},{24,8},{1,17},{9,25},{17,1},{25,9},{2,18},{10... | collective-permute-start | bytes 4325384 | tf_op jit(solution)/shard_map/ppermute | solution.py:646
  223.2 31.0 %collective-permute-start.16 = (bf16[2,256,1408]{2,1,0:T(8,128)(2,1)S(1)}, bf16[2,256,1408]{2,1,0:T(8,128)(2,1)S(1)}, u32[]{:S(2)}, u32[]{:S(2)}) collective-permute-start(bf16[2,256,1408]{2,1,0:T(8,128)(2,1)S(1)} %pad_maximum_fusion.2), channel_id=1, source_target_pairs={{0,8},{8,0},{16,24},{24,16},{1,9},{9,1},{17,25},{25,17},{2,10},{10... | collective-permute-start | bytes 4325384 | tf_op jit(solution)/shard_map/ppermute | solution.py:646
  279.6 98.7 %all-gather.10.cloned.1.call-start = ((), (), s32[]{:S(2)}) async-start(), calls=%async_computation.13 | async-start | bytes 4718592 | tf_op jit(solution)/shard_map/all_gather | solution.py:892
  289.1 33.8 %collective-permute-start.17 = (bf16[2,256,1408]{2,1,0:T(8,128)(2,1)S(1)}, bf16[2,256,1408]{2,1,0:T(8,128)(2,1)S(1)}, u32[]{:S(2)}, u32[]{:S(2)}) collective-permute-start(bf16[2,256,1408]{2,1,0:T(8,128)(2,1)S(1)} %pad_maximum_fusion.3), channel_id=1, source_target_pairs={{0,8},{8,0},{16,24},{24,16},{1,9},{9,1},{17,25},{25,17},{2,10},{10... | collective-permute-start | bytes 4325384 | tf_op jit(solution)/shard_map/ppermute | solution.py:646
  293.8 33.7 %collective-permute-start.18 = (bf16[2,256,1408]{2,1,0:T(8,128)(2,1)S(1)}, bf16[2,256,1408]{2,1,0:T(8,128)(2,1)}, u32[]{:S(2)}, u32[]{:S(2)}) collective-permute-start(bf16[2,256,1408]{2,1,0:T(8,128)(2,1)S(1)} %pad_maximum_fusion.4), channel_id=1, source_target_pairs={{0,16},{8,24},{16,0},{24,8},{1,17},{9,25},{17,1},{25,9},{2,18},{10... | collective-permute-start | bytes 4325384 | tf_op jit(solution)/shard_map/ppermute | solution.py:646
  332.8 124.8 %reduce-scatter.9.cloned.1.call-start = ((), (), s32[]{:S(2)}) async-start(), calls=%async_computation.14 | async-start | bytes 4718592 | tf_op jit(solution)/shard_map/reduce_scatter | solution.py:898
  337.3 39.3 %collective-permute-start.21 = (bf16[176,2048]{1,0:T(8,128)(2,1)}, bf16[176,2048]{1,0:T(8,128)(2,1)}, u32[]{:S(2)}, u32[]{:S(2)}) collective-permute-start(bf16[176,2048]{1,0:T(8,128)(2,1)} %convolution_convert_fusion.11), channel_id=1, source_target_pairs={{0,8},{8,0},{16,24},{24,16},{1,9},{9,1},{17,25},{25,17},{2,10},{10... | collective-permute-start | bytes 2162696 | tf_op jit(solution)/shard_map/ppermute | solution.py:646
  340.7 35.9 %collective-permute-start.22 = (bf16[176,2048]{1,0:T(8,128)(2,1)}, bf16[176,2048]{1,0:T(8,128)(2,1)}, u32[]{:S(2)}, u32[]{:S(2)}) collective-permute-start(bf16[176,2048]{1,0:T(8,128)(2,1)} %convolution_convert_fusion.10), channel_id=1, source_target_pairs={{0,16},{8,24},{16,0},{24,8},{1,17},{9,25},{17,1},{25,9},{2,18},{10... | collective-permute-start | bytes 2162696 | tf_op jit(solution)/shard_map/ppermute | solution.py:646
  347.4 25.4 %collective-permute-start.19 = (bf16[256,1408]{1,0:T(8,128)(2,1)}, bf16[256,1408]{1,0:T(8,128)(2,1)}, u32[]{:S(2)}, u32[]{:S(2)}) collective-permute-start(bf16[256,1408]{1,0:T(8,128)(2,1)} %fusion.11), channel_id=1, source_target_pairs={{0,16},{8,24},{16,0},{24,8},{1,17},{9,25},{17,1},{25,9},{2,18},{10... | collective-permute-start | bytes 2162696 | tf_op jit(solution)/shard_map/ppermute | solution.py:646
  350.5 22.4 %collective-permute-start.20 = (bf16[256,1408]{1,0:T(8,128)(2,1)}, bf16[256,1408]{1,0:T(8,128)(2,1)}, u32[]{:S(2)}, u32[]{:S(2)}) collective-permute-start(bf16[256,1408]{1,0:T(8,128)(2,1)} %fusion.8), channel_id=1, source_target_pairs={{0,8},{8,0},{16,24},{24,16},{1,9},{9,1},{17,25},{25,17},{2,10},{10... | collective-permute-start | bytes 2162696 | tf_op jit(solution)/shard_map/ppermute | solution.py:646
  378.3 79.3 %all-to-all-start.3 = ((bf16[8,64,1408]{2,1,0:T(8,128)(2,1)}), bf16[8,64,1408]{2,1,0:T(8,128)(2,1)S(1)}, u32[]{:S(2)}, u32[]{:S(2)}) async-start(bf16[8,64,1408]{2,1,0:T(8,128)(2,1)} %bitcast.194), calls=%async_computation.6 | async-start | bytes 2883584 | tf_op jit(solution)/shard_map/all_to_all | solution.py:766
  381.9 135.5 %reduce-scatter.11.cloned.1.call-start = ((), (), s32[]{:S(2)}) async-start(), calls=%async_computation.15 | async-start | bytes 4718592 | tf_op jit(solution)/shard_map/reduce_scatter | solution.py:940
  416.4 7.6 %collective-permute-start.25 = (bf16[64,2048]{1,0:T(8,128)(2,1)S(1)}, bf16[64,2048]{1,0:T(8,128)(2,1)S(1)}, u32[]{:S(2)}, u32[]{:S(2)}) collective-permute-start(bf16[64,2048]{1,0:T(8,128)(2,1)S(1)} %get-tuple-element.281), channel_id=1, source_target_pairs={{0,0},{8,1},{2,2},{10,3},{4,4},{12,5},{6,6},{14,7},{16,8},{24,9},{... | collective-permute-start | bytes 786440 | tf_op jit(solution)/shard_map/ppermute | solution.py:761
  417.1 40.5 %collective-permute-start.23 = (bf16[2,256,1024]{2,1,0:T(8,128)(2,1)}, bf16[2,256,1024]{2,1,0:T(8,128)(2,1)}, u32[]{:S(2)}, u32[]{:S(2)}) collective-permute-start(bf16[2,256,1024]{2,1,0:T(8,128)(2,1)} %get-tuple-element.176), channel_id=1, source_target_pairs={{0,8},{8,0},{16,24},{24,16},{1,9},{9,1},{17,25},{25,17},{2,10},{10... | collective-permute-start | bytes 3145736 | tf_op jit(solution)/shard_map/ppermute | solution.py:646
  420.3 37.2 %collective-permute-start.24 = (bf16[2,256,1024]{2,1,0:T(8,128)(2,1)}, bf16[2,256,1024]{2,1,0:T(8,128)(2,1)}, u32[]{:S(2)}, u32[]{:S(2)}) collective-permute-start(bf16[2,256,1024]{2,1,0:T(8,128)(2,1)} %get-tuple-element.177), channel_id=1, source_target_pairs={{0,16},{8,24},{16,0},{24,8},{1,17},{9,25},{17,1},{25,9},{2,18},{10... | collective-permute-start | bytes 3145736 | tf_op jit(solution)/shard_map/ppermute | solution.py:646
  421.9 33.5 %collective-permute-start.26 = (bf16[64,2048]{1,0:T(8,128)(2,1)}, bf16[64,2048]{1,0:T(8,128)(2,1)}, u32[]{:S(2)}, u32[]{:S(2)}) collective-permute-start(bf16[64,2048]{1,0:T(8,128)(2,1)} %get-tuple-element.280), channel_id=1, source_target_pairs={{8,0},{0,1},{10,2},{2,3},{12,4},{4,5},{14,6},{6,7},{24,8},{16,9},{... | collective-permute-start | bytes 786440 | tf_op jit(solution)/shard_map/ppermute | solution.py:761
  422.0 33.4 %collective-permute-start.27 = (bf16[64,2048]{1,0:T(8,128)(2,1)}, bf16[64,2048]{1,0:T(8,128)(2,1)}, u32[]{:S(2)}, u32[]{:S(2)}) collective-permute-start(bf16[64,2048]{1,0:T(8,128)(2,1)} %get-tuple-element.279), channel_id=1, source_target_pairs={{16,0},{24,1},{18,2},{26,3},{20,4},{28,5},{22,6},{30,7},{0,8},{8,9... | collective-permute-start | bytes 786440 | tf_op jit(solution)/shard_map/ppermute | solution.py:761
  424.7 32.9 %collective-permute-start.28 = (bf16[64,2048]{1,0:T(8,128)(2,1)}, bf16[64,2048]{1,0:T(8,128)(2,1)}, u32[]{:S(2)}, u32[]{:S(2)}) collective-permute-start(bf16[64,2048]{1,0:T(8,128)(2,1)} %get-tuple-element.278), channel_id=1, source_target_pairs={{24,0},{16,1},{26,2},{18,3},{28,4},{20,5},{30,6},{22,7},{8,8},{0,9... | collective-permute-start | bytes 786440 | tf_op jit(solution)/shard_map/ppermute | solution.py:761
  472.9 10.9 %collective-permute-start.33 = (bf16[512,128]{1,0:T(8,128)(2,1)S(1)}, bf16[512,128]{1,0:T(8,128)(2,1)S(1)}, u32[]{:S(2)}, u32[]{:S(2)}) collective-permute-start(bf16[512,128]{1,0:T(8,128)(2,1)S(1)} %get-tuple-element.285), channel_id=1, source_target_pairs={{0,24},{8,16},{16,8},{24,0},{1,25},{9,17},{17,9},{25,1},{2,26},{10... | collective-permute-start | bytes 393224 | tf_op jit(solution)/shard_map/ppermute | solution.py:646
  474.6 10.6 %collective-permute-start.32 = (bf16[512,128]{1,0:T(8,128)(2,1)S(1)}, bf16[512,128]{1,0:T(8,128)(2,1)S(1)}, u32[]{:S(2)}, u32[]{:S(2)}) collective-permute-start(bf16[512,128]{1,0:T(8,128)(2,1)S(1)} %get-tuple-element.286), channel_id=1, source_target_pairs={{0,16},{8,24},{16,0},{24,8},{1,17},{9,25},{17,1},{25,9},{2,18},{10... | collective-permute-start | bytes 393224 | tf_op jit(solution)/shard_map/ppermute | solution.py:646
  474.6 10.6 %collective-permute-start.31 = (bf16[512,128]{1,0:T(8,128)(2,1)S(1)}, bf16[512,128]{1,0:T(8,128)(2,1)S(1)}, u32[]{:S(2)}, u32[]{:S(2)}) collective-permute-start(bf16[512,128]{1,0:T(8,128)(2,1)S(1)} %get-tuple-element.284), channel_id=1, source_target_pairs={{0,8},{8,0},{16,24},{24,16},{1,9},{9,1},{17,25},{25,17},{2,10},{10... | collective-permute-start | bytes 393224 | tf_op jit(solution)/shard_map/ppermute | solution.py:646
  477.7 17.7 %collective-permute-start.29 = (bf16[256,1024]{1,0:T(8,128)(2,1)S(1)}, bf16[256,1024]{1,0:T(8,128)(2,1)S(1)}, u32[]{:S(2)}, u32[]{:S(2)}) collective-permute-start(bf16[256,1024]{1,0:T(8,128)(2,1)S(1)} %fusion.22), channel_id=1, source_target_pairs={{0,16},{8,24},{16,0},{24,8},{1,17},{9,25},{17,1},{25,9},{2,18},{10... | collective-permute-start | bytes 1572872 | tf_op jit(solution)/shard_map/ppermute | solution.py:646
  479.1 16.2 %collective-permute-start.30 = (bf16[256,1024]{1,0:T(8,128)(2,1)S(1)}, bf16[256,1024]{1,0:T(8,128)(2,1)S(1)}, u32[]{:S(2)}, u32[]{:S(2)}) collective-permute-start(bf16[256,1024]{1,0:T(8,128)(2,1)S(1)} %fusion.19), channel_id=1, source_target_pairs={{0,8},{8,0},{16,24},{24,16},{1,9},{9,1},{17,25},{25,17},{2,10},{10... | collective-permute-start | bytes 1572872 | tf_op jit(solution)/shard_map/ppermute | solution.py:646
  483.8 25.1 %collective-permute-start.34 = (bf16[176,2048]{1,0:T(8,128)(2,1)}, bf16[176,2048]{1,0:T(8,128)(2,1)}, u32[]{:S(2)}, u32[]{:S(2)}) collective-permute-start(bf16[176,2048]{1,0:T(8,128)(2,1)} %convolution_convert_fusion.8), channel_id=1, source_target_pairs={{0,24},{8,16},{16,8},{24,0},{1,25},{9,17},{17,9},{25,1},{2,26},{10... | collective-permute-start | bytes 2162696 | tf_op jit(solution)/shard_map/ppermute | solution.py:646
  498.3 34.2 %all-to-all-start.4 = ((bf16[8,64,1152]{2,1,0:T(8,128)(2,1)}), bf16[8,64,1152]{2,1,0:T(8,128)(2,1)S(1)}, u32[]{:S(2)}, u32[]{:S(2)}) async-start(bf16[8,64,1152]{2,1,0:T(8,128)(2,1)} %bitcast.197), calls=%async_computation.7 | async-start | bytes 2359296 | tf_op jit(solution)/shard_map/all_to_all | solution.py:766
  (64 other events, 540.4 us)
Sparse Core Ops, SparseCore 0:
  9.6 65.4 all-gather.11
  77.3 64.8 all-gather.5
  163.1 48.6 reduce-scatter.4
  215.3 45.2 all-gather.7
  279.7 48.7 reduce-scatter.6
  332.9 45.2 all-gather.9
  380.5 72.6 reduce-scatter.8
  457.7 50.5 reduce-scatter.10
